TPU v7x, 32 devices: a whole 2x2x4 slice. The times are simulated.
32 devices in a mesh: leaf: 4 (over z), row: 4 (over y, x), col: 2 (over core).
Axes of the slice: x: 2, y: 2, z: 4, core: 2. Of those that a mesh axis runs over, the one named last changes fastest.
Arguments:
- left_panels: float32 [4, 1024, 1024], P('leaf', 'row', 'col'), may hold values from -6 to 6
- upper_panels: float32 [4, 1024, 6144], P('leaf', 'row', 'col'), may hold values from -0.1875 to 0.1875
- row_blocks: int32 [4, 4], P('leaf', 'row'), may hold values from 0 to 1
- col_blocks: int32 [4, 24], P('leaf', 'col'), may hold values from 0 to 1
- ancestor: float32 [1024, 6144], P('row', 'col'), may hold values from -60 to 60
Outputs:
- equilibrated: float32 [1024, 6144], P('row', ('col', 'leaf'))
All inputs are finite; a program needn't handle non-finite values. Where the computation divides by a largest or mean magnitude, that divisor is 1e-20 or more.
Results may differ from a plain program's by a relative error of at most 0.00011.
Values sent between devices are 32-bit elements; how exact they have to be, the bound alone decides.
No kernel may reach another device: no remote copies, remote signals or barrier semaphores. Data moves between devices by JAX's collectives and lax.ppermute only.
A program may use at most 64 MiB of HBM per device.

v0:
```python
import jax
import jax.numpy as jnp
from jax import lax
from jax.sharding import PartitionSpec as P

BLK = 256


def shards(left_panels, upper_panels, row_blocks, col_blocks, ancestor):
    row_mask = jnp.repeat((row_blocks[0] > 0).astype(jnp.float32), BLK, axis=0)
    col_mask = jnp.repeat((col_blocks[0] > 0).astype(jnp.float32), BLK, axis=0)
    lower = left_panels[0] * row_mask[:, None]
    upper = upper_panels[0] * col_mask[None, :]
    upper_full = lax.all_gather(upper, "row", axis=0, tiled=True)
    local_cols = upper_full.shape[1]
    partial_value = jnp.dot(
        lax.all_gather(lower, "col", axis=1, tiled=True),
        upper_full,
        precision=lax.Precision.HIGHEST,
        preferred_element_type=jnp.float32,
    )
    leaf_index = lax.axis_index("leaf")
    leaf_count = lax.axis_size("leaf")
    share_cols = local_cols // leaf_count
    schur_share = lax.psum_scatter(partial_value, "leaf", scatter_dimension=1, tiled=True)
    ancestor_share = lax.dynamic_slice_in_dim(ancestor, leaf_index * share_cols, share_cols, 1)
    updated = ancestor_share - schur_share
    peak = lax.pmax(jnp.max(jnp.abs(updated), axis=1), ("leaf", "col"))
    return updated / (peak[:, None] + 1e-06)


def solution(mesh):
    return jax.shard_map(
        shards,
        mesh=mesh,
        in_specs=(
            P("leaf", "row", "col"),
            P("leaf", "row", "col"),
            P("leaf", "row"),
            P("leaf", "col"),
            P("row", "col"),
        ),
        out_specs=P("row", ("col", "leaf")),
        check_vma=False,
    )
```

profile of v0, /device:TPU:0, one launch (start us, length us, event | category | flops | bytes accessed | tf_op | source)
XLA Modules:
  0.0 247.0 jit_solution(10065018254280990387)
XLA Ops:
  6.5 0.0 all-gather.6.cloned.1.call-start
  7.2 1.9 broadcast_multiply_fusion
  9.1 0.0 all-gather.6.cloned.1.call-update
  9.1 0.0 all-gather.4.cloned.1.call-start
  9.1 0.7 fusion.2
  9.8 0.1 broadcast_in_dim.2
  9.9 4.0 %bitcast_multiply_fusion = f32[256,3072]{1,0:T(8,128)} fusion(f32[1,256,3072]{2,1,0:T(8,128)} %param.6, f32[3072]{0:T(1024)S(1)} %mul.28), kind=kLoop, calls=%fused_computation | loop fusion | flops 786432 | bytes 6303744 | tf_op jit(solution)/shard_map/mul | solution.py:13
  13.9 0.0 all-gather.4.cloned.1.call-update
  13.9 0.0 reduce-scatter.2.cloned.1.call-start
  14.0 7.0 %all-gather.6.cloned.1.call-done = f32[1,256,1024]{2,1,0:T(8,128)} async-done(((f32[1,256,512]{2,1,0:T(8,128)}), f32[1,256,1024]{2,1,0:T(8,128)}) %all-gather.6.cloned.1.call-update) | async-done | bytes 1048592 | tf_op jit(solution)/shard_map/all_gather | solution.py:17
  21.0 125.6 %all-gather.4.cloned.1.call-done = f32[1024,3072]{1,0:T(8,128)} async-done(((f32[256,3072]{1,0:T(8,128)}), f32[1024,3072]{1,0:T(8,128)}) %all-gather.4.cloned.1.call-update) | async-done | bytes 12582928 | tf_op jit(solution)/shard_map/all_gather | solution.py:14
  146.5 14.6 %fusion = f32[256,3072]{1,0:T(8,128)} fusion(f32[1024,3072]{1,0:T(8,128)} %all-gather.4.cloned.1.call-done, f32[1,256,1024]{2,1,0:T(8,128)} %all-gather.6.cloned.1.call-done), kind=kOutput, calls=%fused_computation.1 | convolution fusion | flops 9663676416 | bytes 16777216 | tf_op jit(solution)/shard_map/dot_general | solution.py:16
  161.1 0.0 copy-start
  161.1 0.0 reduce-scatter.2.cloned.1.call-update
  161.2 60.4 %reduce-scatter.2.cloned.1.call-done = f32[256,768]{1,0:T(8,128)} async-done(((f32[256,3072]{1,0:T(8,128)}), f32[256,768]{1,0:T(8,128)}) %reduce-scatter.2.cloned.1.call-update) | async-done | bytes 786448 | tf_op jit(solution)/shard_map/reduce_scatter | solution.py:25
  221.6 0.0 copy-done
  221.6 1.3 abs_reduce_fusion
  222.9 15.4 %pmax.7 = f32[256]{0:T(256)S(1)} all-reduce(f32[256]{0:T(256)S(1)} %abs_reduce_fusion), channel_id=1, replica_groups=mesh['leaf'=4,'row'=4,'col'=2] {'leaf','col'}, use_global_device_ids=true, to_apply=%region_2.0 | all-reduce | flops 256 | bytes 2048 | tf_op jit(solution)/shard_map/pmax | solution.py:28
  238.3 2.2 broadcast_divide_fusion
  (2 shorter events, 0.0 us)
Async XLA Ops:
  6.5 14.4 %all-gather.6.cloned.1.call-start = ((), (), s32[]{:S(2)}) async-start(), calls=%async_computation.3 | async-start | bytes 1572864 | tf_op jit(solution)/shard_map/all_gather | solution.py:17
  9.1 137.4 %all-gather.4.cloned.1.call-start = ((), (), s32[]{:S(2)}) async-start(), calls=%async_computation.1 | async-start | bytes 15728640 | tf_op jit(solution)/shard_map/all_gather | solution.py:14
  13.9 207.7 %reduce-scatter.2.cloned.1.call-start = ((), (), s32[]{:S(2)}) async-start(), calls=%async_computation.2 | async-start | bytes 3932160 | tf_op jit(solution)/shard_map/reduce_scatter | solution.py:25
  161.1 60.4 %copy-start = (f32[256,3072]{1,0:T(8,128)S(1)}, f32[256,3072]{1,0:T(8,128)}, u32[]{:S(2)}) copy-start(f32[256,3072]{1,0:T(8,128)} %param.9) | copy-start | bytes 9437188
Sparse Core Ops, SparseCore 0:
  9.2 11.7 all-gather.5
  22.8 123.6 all-gather.3
  161.3 60.2 reduce-scatter.1
where the time goes:
time: 247 us
  waiting for transfers between devices  193 us (78%)
  blocking collectives  15.4 us (6%)
  matrix products  14.6 us (6%)
  between operations  13.8 us (6%)
  other arithmetic  10 us (4%)
    all_gather x1, waiting for transfers between devices, shards(): upper_full = lax.all_gather(upper, 'row', axis=0, tiled=True)  126 us
    reduce_scatter x1, waiting for transfers between devices, shards(): lax.psum_scatter(partial_value, 'leaf', scatter_dimension=1, tiled=True)  60.4 us
    pmax x1, blocking collectives, shards(): peak = lax.pmax(jnp.max(jnp.abs(updated), axis=1), ('leaf', 'col'))  15.4 us
    dot_general x1, matrix products, shards(): jnp.dot(lax.all_gather(lower, 'col', axis=1, tiled=True), upper_full, pre...  14.6 us
    all_gather x1, waiting for transfers between devices, shards(): lax.all_gather(lower, 'col', axis=1, tiled=True)  7.02 us
  transfers between devices with their start and end apart: 3, of which 3 were waited for; matrix products, arithmetic and copies ran while one was open for 2% of the time, Pallas kernels for 0%

commit v1 on v0

v1 whole, which is shorter than its diff:
```python
import jax
import jax.numpy as jnp
from jax import lax
from jax.sharding import PartitionSpec as P

LANES = 128
HIGHEST = lax.Precision.HIGHEST


def swap(value, axis, size, bit):
    return lax.ppermute(value, axis, [(i, i ^ bit) for i in range(size)])


def butterfly_max(value, axis):
    size = lax.axis_size(axis)
    if size & (size - 1):
        return lax.pmax(value, axis)
    bit = 1
    while bit < size:
        value = jnp.maximum(value, swap(value, axis, size, bit))
        bit *= 2
    return value


def bit_order(count):
    order = [0]
    bit = 1
    while bit < count:
        order = order + [i + bit for i in order]
        bit *= 2
    width = count.bit_length() - 1
    return [int(format(i, "b").zfill(width)[::-1], 2) if width else 0 for i in range(count)]


def dot(a, b):
    return jnp.dot(a, b, precision=HIGHEST, preferred_element_type=jnp.float32)


def plain(left, upper, row_on, col_on, ancestor):
    lower = left * row_on
    upper_full = lax.all_gather(upper, "row", axis=0, tiled=True)
    lower_full = lax.all_gather(lower, "col", axis=1, tiled=True)
    partial_value = dot(lower_full, upper_full) * col_on[None, :]
    leaf_count = lax.axis_size("leaf")
    share_cols = upper.shape[1] // leaf_count
    schur = lax.psum_scatter(partial_value, "leaf", scatter_dimension=1, tiled=True)
    share = lax.dynamic_slice_in_dim(ancestor, lax.axis_index("leaf") * share_cols, share_cols, 1)
    updated = share - schur
    peak = lax.pmax(jnp.max(jnp.abs(updated), axis=1), ("leaf", "col"))
    return updated / (peak[:, None] + 1e-6)


def chunked(left, upper, row_on, col_on, ancestor):
    leaf_count, rows, cols = (lax.axis_size(a) for a in ("leaf", "row", "col"))
    leaf, row, col = (lax.axis_index(a) for a in ("leaf", "row", "col"))
    low_one, high_one = row % 2 == 1, row // 2 == 1
    depth = upper.shape[0]
    share_cols = upper.shape[1] // leaf_count
    order = bit_order(leaf_count)

    lower = left * row_on
    first, second = lower[:, :depth], lower[:, depth:]
    mine = jnp.where(low_one, second, first)
    theirs = swap(jnp.where(low_one, first, second), "row", rows, 1)
    here = jnp.concatenate([theirs, mine], 0)
    there = swap(here, "col", cols, 1)
    aligned = (col == 1) == high_one
    left_own = jnp.where(aligned, here, there)
    left_other = jnp.where(aligned, there, here)

    step = LANES
    pieces = []
    for at in range(0, share_cols, step):
        spans = [(s * share_cols + at, s * share_cols + min(at + step, share_cols)) for s in order]
        block = jnp.concatenate([upper[:, a:b] for a, b in spans], 1)
        on = jnp.concatenate([col_on[a:b] for a, b in spans], 0)[None, :]
        got = swap(block, "row", rows, 2)
        part = (dot(left_own, block) + dot(left_other, got)) * on
        half = part.shape[0] // 2
        total = part[half:] + swap(part[:half], "row", rows, 1)
        bit = 1
        while bit < leaf_count:
            half = total.shape[1] // 2
            upper_half = (leaf // bit) % 2 == 1
            send = jnp.where(upper_half, total[:, :half], total[:, half:])
            keep = jnp.where(upper_half, total[:, half:], total[:, :half])
            total = keep + swap(send, "leaf", leaf_count, bit)
            bit *= 2
        pieces.append(total)
    schur = jnp.concatenate(pieces, 1)
    share = lax.dynamic_slice_in_dim(ancestor, leaf * share_cols, share_cols, 1)
    updated = share - schur
    peak = butterfly_max(butterfly_max(jnp.max(jnp.abs(updated), axis=1), "col"), "leaf")
    return updated / (peak[:, None] + 1e-6)


def solution(mesh):
    leaf_count, rows, cols = (mesh.shape[a] for a in ("leaf", "row", "col"))
    fits = rows == 4 and cols == 2 and leaf_count & (leaf_count - 1) == 0

    def shards(left_panels, upper_panels, row_blocks, col_blocks, ancestor):
        row_each = left_panels.shape[1] // row_blocks.shape[1]
        col_each = upper_panels.shape[2] // col_blocks.shape[1]
        row_on = jnp.repeat((row_blocks[0] > 0).astype(jnp.float32), row_each)[:, None]
        col_on = jnp.repeat((col_blocks[0] > 0).astype(jnp.float32), col_each)
        body = chunked if fits else plain
        return body(left_panels[0], upper_panels[0], row_on, col_on, ancestor)

    return jax.shard_map(
        shards,
        mesh=mesh,
        in_specs=(
            P("leaf", "row", "col"),
            P("leaf", "row", "col"),
            P("leaf", "row"),
            P("leaf", "col"),
            P("row", "col"),
        ),
        out_specs=P("row", ("col", "leaf")),
        check_vma=False,
    )
```

time: 247 us -> 163 us (0.66)
  waiting for transfers between devices: 193 us -> 87.5 us
  starting transfers between devices: 0.09 us -> 27.7 us
  blocking collectives: 15.4 us -> 0 us
  local copies, waits for them, and re-layouts: 0.08 us -> 13.6 us
  between operations: 13.8 us -> 1.95 us
  other arithmetic: 10 us -> 15 us
  matrix products: 14.6 us -> 17.1 us
    all_gather x2 -> x0, waiting for transfers between devices: 133 us -> none  [the longest x1 126 us: shards(): upper_full = lax.all_gather(upper, 'row', axis=0, tiled=True)]
    ppermute x0 -> x29, waiting for transfers between devices: none -> 87.5 us  [swap(): return lax.ppermute(value, axis, [(i, i ^ bit) for i in range(size)])]
    reduce_scatter x1 -> x0, waiting for transfers between devices: 60.4 us -> none  [shards(): lax.psum_scatter(partial_value, 'leaf', scatter_dimension=1, tiled=True)]
    ppermute x0 -> x29, starting transfers between devices: none -> 27.7 us  [swap(): return lax.ppermute(value, axis, [(i, i ^ bit) for i in range(size)])]
    pmax x1 -> x0, blocking collectives: 15.4 us -> none  [shards(): peak = lax.pmax(jnp.max(jnp.abs(updated), axis=1), ('leaf', 'col'))]
    concatenate x0 -> x14, other arithmetic: none -> 9.46 us  [the longest x6 5.82 us: chunked(): block = jnp.concatenate([upper[:, a:b] for a, b in spans], 1)]
    slice x0 -> x10, local copies, waits for them, and re-layouts: none -> 7.19 us  [the longest x2 4.63 us: chunked(): block = jnp.concatenate([upper[:, a:b] for a, b in spans], 1)]
    mul x2 -> x1, other arithmetic: 5.88 us -> 1.23 us  [chunked(): lower = left * row_on]
  transfers between devices with their start and end apart: 3 -> 29, of which waited for: 3 -> 12; matrix products, arithmetic and copies ran while one was open for 2% -> 25% of each run, Pallas kernels for 0% -> 0%
where the time goes in v1:
time: 163 us
  waiting for transfers between devices  87.5 us (54%)
  starting transfers between devices  27.7 us (17%)
  matrix products  17.1 us (10%)
  other arithmetic  15 us (9%)
  local copies, waits for them, and re-layouts  13.6 us (8%)
  between operations  1.95 us (1%)
    ppermute x29, waiting for transfers between devices, swap(): return lax.ppermute(value, axis, [(i, i ^ bit) for i in range(size)])  87.5 us
    ppermute x29, starting transfers between devices, swap(): return lax.ppermute(value, axis, [(i, i ^ bit) for i in range(size)])  27.7 us
    dot_general x12, matrix products, dot(): return jnp.dot(a, b, precision=HIGHEST, preferred_element_type=jnp.float32)  17.1 us
    concatenate x6, other arithmetic, chunked(): block = jnp.concatenate([upper[:, a:b] for a, b in spans], 1)  5.82 us
    slice x2, local copies, waits for them, and re-layouts, chunked(): block = jnp.concatenate([upper[:, a:b] for a, b in spans], 1)  4.63 us
  transfers between devices with their start and end apart: 29, of which 12 were waited for; matrix products, arithmetic and copies ran while one was open for 25% of the time, Pallas kernels for 0%

profile of v1, /device:TPU:0, one launch (start us, length us, event | category | flops | bytes accessed | tf_op | source)
XLA Modules:
  0.0 162.8 jit_solution(3739328085478058107)
XLA Ops:
  0.8 1.2 multiply_bitcast_fusion
  2.8 2.9 %collective-permute-start = (f32[256,256]{1,0:T(8,128)}, f32[256,256]{1,0:T(8,128)}, u32[]{:S(2)}, u32[]{:S(2)}) collective-permute-start(f32[256,256]{1,0:T(8,128)} %get-tuple-element.33), channel_id=1, source_target_pairs={{0,2},{2,0},{4,6},{6,4},{1,3},{3,1},{5,7},{7,5},{8,10},{10,8},{12,... | collective-permute-start | bytes 786440 | tf_op jit(solution)/shard_map/ppermute | solution.py:11
  5.7 2.6 %fusion.7 = (f32[256,128]{1,0:T(8,128)S(1)}, f32[256,128]{1,0:T(8,128)S(1)}, f32[256,128]{1,0:T(8,128)S(1)}, f32[256,128]{1,0:T(8,128)S(1)}, f32[256,128]{1,0:T(...) fusion(f32[256,3072]{1,0:T(8,128)} %bitcast.24), kind=kLoop, calls=%fused_computation.66 | loop fusion | bytes 4980736 | tf_op jit(solution)/shard_map/slice | solution.py:75
  8.5 1.1 pad_maximum_fusion.6
  9.6 1.5 collective-permute-start.22
  13.3 1.5 collective-permute-start.14
  17.9 1.4 fusion.10
  20.4 2.0 %fusion.8 = (f32[256,128]{1,0:T(8,128)}, f32[256,128]{1,0:T(8,128)}, f32[256,128]{1,0:T(8,128)}, f32[256,128]{1,0:T(8,128)}, f32[256,128]{1,0:T(8,128)}) fusion(f32[256,3072]{1,0:T(8,128)} %bitcast.25), kind=kLoop, calls=%fused_computation.67 | loop fusion | bytes 1310720 | tf_op jit(solution)/shard_map/slice | solution.py:75
  22.4 1.8 %pad_maximum_fusion = f32[512,256]{1,0:T(8,128)} fusion(f32[256,256]{1,0:T(8,128)S(1)} %get-tuple-element.34, f32[256,256]{1,0:T(8,128)} %collective-permute-done), kind=kLoop, calls=%fused_computation.19 | loop fusion | flops 131072 | bytes 1048576 | tf_op jit(solution)/shard_map/concatenate | solution.py:65
  25.9 2.3 %copy.8 = f32[256,768]{0,1:T(8,128)} copy(f32[256,768]{1,0:T(8,128)} %constant_dynamic-slice_fusion) | data formatting | bytes 1572864
  28.3 1.1 pad_maximum_fusion.2
  29.4 1.1 pad_maximum_fusion.1
  30.5 1.6 collective-permute-start.6
  32.1 1.2 broadcast_select_fusion.1
  33.9 2.1 %fusion.16 = f32[512,512]{0,1:T(8,128)S(1)} fusion(f32[512,256]{1,0:T(8,128)S(1)} %get-tuple-element.32, f32[256,512]{1,0:T(8,128)} %collective-permute-done.22), kind=kOutput, calls=%fused_computation.75 | convolution fusion | flops 805306368 | bytes 2097152 | tf_op jit(solution)/shard_map/dot_general | solution.py:36
  36.1 1.1 fusion
  37.4 2.1 %fusion.15 = f32[512,512]{0,1:T(8,128)S(1)} fusion(f32[512,256]{1,0:T(8,128)S(1)} %get-tuple-element.32, f32[256,512]{1,0:T(8,128)} %collective-permute-done.18), kind=kOutput, calls=%fused_computation.74 | convolution fusion | flops 805306368 | bytes 2097152 | tf_op jit(solution)/shard_map/dot_general | solution.py:36
  39.5 1.1 fusion.1
  40.7 6.5 %collective-permute-done.14 = f32[256,512]{1,0:T(8,128)} collective-permute-done((f32[256,512]{1,0:T(8,128)}, f32[256,512]{1,0:T(8,128)}, u32[]{:S(2)}, u32[]{:S(2)}) %collective-permute-start.14) | collective-permute-done | bytes 524320 | tf_op jit(solution)/shard_map/ppermute | solution.py:11
  47.2 2.1 %fusion.14 = f32[512,512]{0,1:T(8,128)S(1)} fusion(f32[512,256]{1,0:T(8,128)S(1)} %get-tuple-element.32, f32[256,512]{1,0:T(8,128)} %collective-permute-done.14), kind=kOutput, calls=%fused_computation.73 | convolution fusion | flops 805306368 | bytes 2097152 | tf_op jit(solution)/shard_map/dot_general | solution.py:36
  49.4 1.1 fusion.2
  50.5 7.9 %collective-permute-done.10 = f32[256,512]{1,0:T(8,128)} collective-permute-done((f32[256,512]{1,0:T(8,128)}, f32[256,512]{1,0:T(8,128)}, u32[]{:S(2)}, u32[]{:S(2)}) %collective-permute-start.10) | collective-permute-done | bytes 524320 | tf_op jit(solution)/shard_map/ppermute | solution.py:11
  58.5 2.1 %fusion.13 = f32[512,512]{0,1:T(8,128)S(1)} fusion(f32[512,256]{1,0:T(8,128)S(1)} %get-tuple-element.32, f32[256,512]{1,0:T(8,128)} %collective-permute-done.10), kind=kOutput, calls=%fused_computation.72 | convolution fusion | flops 805306368 | bytes 2097152 | tf_op jit(solution)/shard_map/dot_general | solution.py:36
  60.6 1.1 fusion.3
  61.7 7.8 %collective-permute-done.6 = f32[256,512]{1,0:T(8,128)S(1)} collective-permute-done((f32[256,512]{1,0:T(8,128)S(1)}, f32[256,512]{1,0:T(8,128)S(1)}, u32[]{:S(2)}, u32[]{:S(2)}) %collective-permute-start.6) | collective-permute-done | bytes 524320 | tf_op jit(solution)/shard_map/ppermute | solution.py:11
  69.6 1.3 fusion.12
  70.9 1.1 fusion.4
  72.0 7.3 %collective-permute-done.2 = f32[256,512]{1,0:T(8,128)S(1)} collective-permute-done((f32[256,512]{1,0:T(8,128)S(1)}, f32[256,512]{1,0:T(8,128)S(1)}, u32[]{:S(2)}, u32[]{:S(2)}) %collective-permute-start.2) | collective-permute-done | bytes 524320 | tf_op jit(solution)/shard_map/ppermute | solution.py:11
  79.7 1.1 fusion.11
  80.8 1.1 fusion.5
  81.9 1.8 %collective-permute-start.3 = (f32[256,512]{0,1:T(8,128)S(1)}, f32[256,512]{0,1:T(8,128)S(1)}, u32[]{:S(2)}, u32[]{:S(2)}) collective-permute-start(f32[256,512]{0,1:T(8,128)S(1)} %slice.379), channel_id=1, source_target_pairs={{0,2},{2,0},{4,6},{6,4},{1,3},{3,1},{5,7},{7,5},{8,10},{10,8},{12,... | collective-permute-start | bytes 1572872 | tf_op jit(solution)/shard_map/ppermute | solution.py:11
  83.8 1.6 %collective-permute-start.24 = (f32[256,256]{0,1:T(8,128)S(1)}, f32[256,256]{0,1:T(8,128)S(1)}, u32[]{:S(2)}, u32[]{:S(2)}) collective-permute-start(f32[256,256]{0,1:T(8,128)S(1)} %slice_select_fusion), channel_id=1, source_target_pairs={{0,8},{8,0},{16,24},{24,16},{1,9},{9,1},{17,25},{25,17},{2,10},{10... | collective-permute-start | bytes 786440 | tf_op jit(solution)/shard_map/ppermute | solution.py:11
  86.3 1.6 %collective-permute-start.16 = (f32[256,256]{0,1:T(8,128)S(1)}, f32[256,256]{0,1:T(8,128)S(1)}, u32[]{:S(2)}, u32[]{:S(2)}) collective-permute-start(f32[256,256]{0,1:T(8,128)S(1)} %slice_select_fusion.2), channel_id=1, source_target_pairs={{0,8},{8,0},{16,24},{24,16},{1,9},{9,1},{17,25},{25,17},{2,10},{10... | collective-permute-start | bytes 786440 | tf_op jit(solution)/shard_map/ppermute | solution.py:11
  88.0 9.0 %collective-permute-done.7 = f32[256,512]{0,1:T(8,128)S(1)} collective-permute-done((f32[256,512]{0,1:T(8,128)S(1)}, f32[256,512]{0,1:T(8,128)S(1)}, u32[]{:S(2)}, u32[]{:S(2)}) %collective-permute-start.7) | collective-permute-done | bytes 524320 | tf_op jit(solution)/shard_map/ppermute | solution.py:11
  97.0 1.6 collective-permute-start.12
  98.8 8.5 %collective-permute-done.3 = f32[256,512]{0,1:T(8,128)S(1)} collective-permute-done((f32[256,512]{0,1:T(8,128)S(1)}, f32[256,512]{0,1:T(8,128)S(1)}, u32[]{:S(2)}, u32[]{:S(2)}) %collective-permute-start.3) | collective-permute-done | bytes 524320 | tf_op jit(solution)/shard_map/ppermute | solution.py:11
  107.2 1.6 collective-permute-start.8
  109.6 2.7 %collective-permute-start.25 = (f32[256,128]{0,1:T(8,128)S(1)}, f32[256,128]{0,1:T(8,128)S(1)}, u32[]{:S(2)}, u32[]{:S(2)}) collective-permute-start(f32[256,128]{0,1:T(8,128)S(1)} %slice_select_fusion.8), channel_id=1, source_target_pairs={{0,16},{8,24},{16,0},{24,8},{1,17},{9,25},{17,1},{25,9},{2,18},{10... | collective-permute-start | bytes 393224 | tf_op jit(solution)/shard_map/ppermute | solution.py:11
  112.8 2.7 %collective-permute-start.17 = (f32[256,128]{0,1:T(8,128)S(1)}, f32[256,128]{0,1:T(8,128)S(1)}, u32[]{:S(2)}, u32[]{:S(2)}) collective-permute-start(f32[256,128]{0,1:T(8,128)S(1)} %slice_select_fusion.10), channel_id=1, source_target_pairs={{0,16},{8,24},{16,0},{24,8},{1,17},{9,25},{17,1},{25,9},{2,18},{10... | collective-permute-start | bytes 393224 | tf_op jit(solution)/shard_map/ppermute | solution.py:11
  115.5 13.0 %collective-permute-done.4 = f32[256,256]{0,1:T(8,128)S(1)} collective-permute-done((f32[256,256]{0,1:T(8,128)S(1)}, f32[256,256]{0,1:T(8,128)S(1)}, u32[]{:S(2)}, u32[]{:S(2)}) %collective-permute-start.4) | collective-permute-done | bytes 262176 | tf_op jit(solution)/shard_map/ppermute | solution.py:11
  128.6 1.6 collective-permute-start.13
  130.2 1.4 collective-permute-start.5
  131.7 10.1 %collective-permute-done.5 = f32[256,128]{0,1:T(8,128)S(1)} collective-permute-done((f32[256,128]{0,1:T(8,128)S(1)}, f32[256,128]{0,1:T(8,128)S(1)}, u32[]{:S(2)}, u32[]{:S(2)}) %collective-permute-start.5) | collective-permute-done | bytes 131104 | tf_op jit(solution)/shard_map/ppermute | solution.py:11
  141.9 8.1 %collective-permute-done.9 = f32[256,128]{0,1:T(8,128)S(1)} collective-permute-done((f32[256,128]{0,1:T(8,128)S(1)}, f32[256,128]{0,1:T(8,128)S(1)}, u32[]{:S(2)}, u32[]{:S(2)}) %collective-permute-start.9) | collective-permute-done | bytes 131104 | tf_op jit(solution)/shard_map/ppermute | solution.py:11
  150.3 1.1 collective-permute-done.26
  151.5 3.6 %collective-permute-done.27 = f32[256]{0:T(256)S(1)} collective-permute-done((f32[256]{0:T(256)S(1)}, f32[256]{0:T(256)S(1)}, u32[]{:S(2)}, u32[]{:S(2)}) %collective-permute-start.27) | collective-permute-done | bytes 1056 | tf_op jit(solution)/shard_map/ppermute | solution.py:11
  155.1 4.5 %collective-permute-done.28 = f32[256]{0:T(256)S(1)} collective-permute-done((f32[256]{0:T(256)S(1)}, f32[256]{0:T(256)S(1)}, u32[]{:S(2)}, u32[]{:S(2)}) %collective-permute-start.28) | collective-permute-done | bytes 1056 | tf_op jit(solution)/shard_map/ppermute | solution.py:11
  160.5 2.3 %copy.7 = f32[256,768]{1,0:T(8,128)} copy(f32[256,768]{0,1:T(8,128)} %broadcast_divide_fusion) | data formatting | bytes 1572864 | tf_op jit(solution)/shard_map/div | solution.py:94
  (177 shorter events, 14.0 us)
Async XLA Ops:
  0.0 24.2 %copy-start = (f32[256,3072]{1,0:T(8,128)S(1)}, f32[256,3072]{1,0:T(8,128)}, u32[]{:S(2)}) copy-start(f32[256,3072]{1,0:T(8,128)} %param.9) | copy-start | bytes 9437188
  2.8 19.6 %collective-permute-start = (f32[256,256]{1,0:T(8,128)}, f32[256,256]{1,0:T(8,128)}, u32[]{:S(2)}, u32[]{:S(2)}) collective-permute-start(f32[256,256]{1,0:T(8,128)} %get-tuple-element.33), channel_id=1, source_target_pairs={{0,2},{2,0},{4,6},{6,4},{1,3},{3,1},{5,7},{7,5},{8,10},{10,8},{12,... | collective-permute-start | bytes 786440 | tf_op jit(solution)/shard_map/ppermute | solution.py:11
  8.3 7.8 %copy-start.10 = (f32[256,128]{1,0:T(8,128)}, f32[256,128]{1,0:T(8,128)S(1)}, u32[]{:S(2)}) copy-start(f32[256,128]{1,0:T(8,128)S(1)} %get-tuple-element.22) | copy-start | bytes 393220
  9.6 23.7 %collective-permute-start.22 = (f32[256,512]{1,0:T(8,128)}, f32[256,512]{1,0:T(8,128)}, u32[]{:S(2)}, u32[]{:S(2)}) collective-permute-start(f32[256,512]{1,0:T(8,128)} %pad_maximum_fusion.6), channel_id=1, source_target_pairs={{0,4},{2,6},{4,0},{6,2},{1,5},{3,7},{5,1},{7,3},{8,12},{10,14},{12... | collective-permute-start | bytes 1572872 | tf_op jit(solution)/shard_map/ppermute | solution.py:11
  11.9 25.3 %collective-permute-start.18 = (f32[256,512]{1,0:T(8,128)}, f32[256,512]{1,0:T(8,128)}, u32[]{:S(2)}, u32[]{:S(2)}) collective-permute-start(f32[256,512]{1,0:T(8,128)} %pad_maximum_fusion.5), channel_id=1, source_target_pairs={{0,4},{2,6},{4,0},{6,2},{1,5},{3,7},{5,1},{7,3},{8,12},{10,14},{12... | collective-permute-start | bytes 1572872 | tf_op jit(solution)/shard_map/ppermute | solution.py:11
  13.3 34.0 %collective-permute-start.14 = (f32[256,512]{1,0:T(8,128)}, f32[256,512]{1,0:T(8,128)}, u32[]{:S(2)}, u32[]{:S(2)}) collective-permute-start(f32[256,512]{1,0:T(8,128)} %pad_maximum_fusion.4), channel_id=1, source_target_pairs={{0,4},{2,6},{4,0},{6,2},{1,5},{3,7},{5,1},{7,3},{8,12},{10,14},{12... | collective-permute-start | bytes 1572872 | tf_op jit(solution)/shard_map/ppermute | solution.py:11
  15.6 42.8 %collective-permute-start.10 = (f32[256,512]{1,0:T(8,128)}, f32[256,512]{1,0:T(8,128)}, u32[]{:S(2)}, u32[]{:S(2)}) collective-permute-start(f32[256,512]{1,0:T(8,128)} %pad_maximum_fusion.3), channel_id=1, source_target_pairs={{0,4},{2,6},{4,0},{6,2},{1,5},{3,7},{5,1},{7,3},{8,12},{10,14},{12... | collective-permute-start | bytes 1572872 | tf_op jit(solution)/shard_map/ppermute | solution.py:11
  24.2 6.3 %collective-permute-start.1 = (f32[512,256]{1,0:T(8,128)}, f32[512,256]{1,0:T(8,128)}, u32[]{:S(2)}, u32[]{:S(2)}) collective-permute-start(f32[512,256]{1,0:T(8,128)} %pad_maximum_fusion), channel_id=1, source_target_pairs={{0,1},{1,0},{2,3},{3,2},{4,5},{5,4},{6,7},{7,6},{8,9},{9,8},{10,11... | collective-permute-start | bytes 1572872 | tf_op jit(solution)/shard_map/ppermute | solution.py:11
  28.3 7.8 %copy-start.42 = (f32[512]{0:T(512)S(1)}, f32[512]{0:T(512)}, u32[]{:S(2)}) copy-start(f32[512]{0:T(512)} %pad_maximum_fusion.12) | copy-start | bytes 6148
  30.5 39.0 %collective-permute-start.6 = (f32[256,512]{1,0:T(8,128)S(1)}, f32[256,512]{1,0:T(8,128)S(1)}, u32[]{:S(2)}, u32[]{:S(2)}) collective-permute-start(f32[256,512]{1,0:T(8,128)S(1)} %pad_maximum_fusion.2), channel_id=1, source_target_pairs={{0,4},{2,6},{4,0},{6,2},{1,5},{3,7},{5,1},{7,3},{8,12},{10,14},{12... | collective-permute-start | bytes 1572872 | tf_op jit(solution)/shard_map/ppermute | solution.py:11
  33.3 46.0 %collective-permute-start.2 = (f32[256,512]{1,0:T(8,128)S(1)}, f32[256,512]{1,0:T(8,128)S(1)}, u32[]{:S(2)}, u32[]{:S(2)}) collective-permute-start(f32[256,512]{1,0:T(8,128)S(1)} %pad_maximum_fusion.1), channel_id=1, source_target_pairs={{0,4},{2,6},{4,0},{6,2},{1,5},{3,7},{5,1},{7,3},{8,12},{10,14},{12... | collective-permute-start | bytes 1572872 | tf_op jit(solution)/shard_map/ppermute | solution.py:11
  37.2 44.7 %collective-permute-start.23 = (f32[256,512]{0,1:T(8,128)S(1)}, f32[256,512]{0,1:T(8,128)S(1)}, u32[]{:S(2)}, u32[]{:S(2)}) collective-permute-start(f32[256,512]{0,1:T(8,128)S(1)} %slice.449), channel_id=1, source_target_pairs={{0,2},{2,0},{4,6},{6,4},{1,3},{3,1},{5,7},{7,5},{8,10},{10,8},{12,... | collective-permute-start | bytes 1572872 | tf_op jit(solution)/shard_map/ppermute | solution.py:11
  39.5 9.8 %copy-start.13 = (f32[256,128]{1,0:T(8,128)S(1)}, f32[256,128]{1,0:T(8,128)}, u32[]{:S(2)}) copy-start(f32[256,128]{1,0:T(8,128)} %copy-done.12) | copy-start | bytes 393220
  39.5 9.8 %copy-start.15 = (f32[256,128]{1,0:T(8,128)S(1)}, f32[256,128]{1,0:T(8,128)}, u32[]{:S(2)}) copy-start(f32[256,128]{1,0:T(8,128)} %copy-done.14) | copy-start | bytes 393220
  39.5 9.8 %copy-start.17 = (f32[256,128]{1,0:T(8,128)S(1)}, f32[256,128]{1,0:T(8,128)}, u32[]{:S(2)}) copy-start(f32[256,128]{1,0:T(8,128)} %copy-done.16) | copy-start | bytes 393220
  39.5 9.8 %copy-start.19 = (f32[256,128]{1,0:T(8,128)S(1)}, f32[256,128]{1,0:T(8,128)}, u32[]{:S(2)}) copy-start(f32[256,128]{1,0:T(8,128)} %copy-done.18) | copy-start | bytes 393220
  47.2 36.6 %collective-permute-start.19 = (f32[256,512]{0,1:T(8,128)S(1)}, f32[256,512]{0,1:T(8,128)S(1)}, u32[]{:S(2)}, u32[]{:S(2)}) collective-permute-start(f32[256,512]{0,1:T(8,128)S(1)} %slice.435), channel_id=1, source_target_pairs={{0,2},{2,0},{4,6},{6,4},{1,3},{3,1},{5,7},{7,5},{8,10},{10,8},{12,... | collective-permute-start | bytes 1572872 | tf_op jit(solution)/shard_map/ppermute | solution.py:11
  49.4 11.2 %copy-start.5 = (f32[256,128]{1,0:T(8,128)S(1)}, f32[256,128]{1,0:T(8,128)}, u32[]{:S(2)}) copy-start(f32[256,128]{1,0:T(8,128)} %copy-done.4) | copy-start | bytes 393220
  49.4 11.2 %copy-start.7 = (f32[256,128]{1,0:T(8,128)S(1)}, f32[256,128]{1,0:T(8,128)}, u32[]{:S(2)}) copy-start(f32[256,128]{1,0:T(8,128)} %copy-done.6) | copy-start | bytes 393220
  49.4 11.2 %copy-start.9 = (f32[256,128]{1,0:T(8,128)S(1)}, f32[256,128]{1,0:T(8,128)}, u32[]{:S(2)}) copy-start(f32[256,128]{1,0:T(8,128)} %copy-done.8) | copy-start | bytes 393220
  49.4 11.2 %copy-start.11 = (f32[256,128]{1,0:T(8,128)S(1)}, f32[256,128]{1,0:T(8,128)}, u32[]{:S(2)}) copy-start(f32[256,128]{1,0:T(8,128)} %copy-done.10) | copy-start | bytes 393220
  58.4 27.2 %collective-permute-start.15 = (f32[256,512]{0,1:T(8,128)S(1)}, f32[256,512]{0,1:T(8,128)S(1)}, u32[]{:S(2)}, u32[]{:S(2)}) collective-permute-start(f32[256,512]{0,1:T(8,128)S(1)} %slice.421), channel_id=1, source_target_pairs={{0,2},{2,0},{4,6},{6,4},{1,3},{3,1},{5,7},{7,5},{8,10},{10,8},{12,... | collective-permute-start | bytes 1572872 | tf_op jit(solution)/shard_map/ppermute | solution.py:11
  60.6 10.3 %copy-start.2 = (f32[256,128]{1,0:T(8,128)S(1)}, f32[256,128]{1,0:T(8,128)}, u32[]{:S(2)}) copy-start(f32[256,128]{1,0:T(8,128)} %get-tuple-element.24) | copy-start | bytes 393220
  60.6 10.3 %copy-start.3 = (f32[256,128]{1,0:T(8,128)S(1)}, f32[256,128]{1,0:T(8,128)}, u32[]{:S(2)}) copy-start(f32[256,128]{1,0:T(8,128)} %get-tuple-element.25) | copy-start | bytes 393220
  60.6 10.3 %copy-start.40 = (f32[256,128]{1,0:T(8,128)S(1)}, f32[256,128]{1,0:T(8,128)}, u32[]{:S(2)}) copy-start(f32[256,128]{1,0:T(8,128)} %get-tuple-element.26) | copy-start | bytes 393220
  69.6 16.7 %collective-permute-start.11 = (f32[256,512]{0,1:T(8,128)S(1)}, f32[256,512]{0,1:T(8,128)S(1)}, u32[]{:S(2)}, u32[]{:S(2)}) collective-permute-start(f32[256,512]{0,1:T(8,128)S(1)} %slice.407), channel_id=1, source_target_pairs={{0,2},{2,0},{4,6},{6,4},{1,3},{3,1},{5,7},{7,5},{8,10},{10,8},{12,... | collective-permute-start | bytes 1572872 | tf_op jit(solution)/shard_map/ppermute | solution.py:11
  70.9 9.8 %copy-start.36 = (f32[256,128]{1,0:T(8,128)S(1)}, f32[256,128]{1,0:T(8,128)}, u32[]{:S(2)}) copy-start(f32[256,128]{1,0:T(8,128)} %get-tuple-element.27) | copy-start | bytes 393220
  70.9 9.8 %copy-start.37 = (f32[256,128]{1,0:T(8,128)S(1)}, f32[256,128]{1,0:T(8,128)}, u32[]{:S(2)}) copy-start(f32[256,128]{1,0:T(8,128)} %get-tuple-element.28) | copy-start | bytes 393220
  70.9 9.8 %copy-start.38 = (f32[256,128]{1,0:T(8,128)S(1)}, f32[256,128]{1,0:T(8,128)}, u32[]{:S(2)}) copy-start(f32[256,128]{1,0:T(8,128)} %get-tuple-element.29) | copy-start | bytes 393220
  70.9 9.8 %copy-start.39 = (f32[256,128]{1,0:T(8,128)S(1)}, f32[256,128]{1,0:T(8,128)}, u32[]{:S(2)}) copy-start(f32[256,128]{1,0:T(8,128)} %get-tuple-element.30) | copy-start | bytes 393220
  79.3 17.7 %collective-permute-start.7 = (f32[256,512]{0,1:T(8,128)S(1)}, f32[256,512]{0,1:T(8,128)S(1)}, u32[]{:S(2)}, u32[]{:S(2)}) collective-permute-start(f32[256,512]{0,1:T(8,128)S(1)} %slice.393), channel_id=1, source_target_pairs={{0,2},{2,0},{4,6},{6,4},{1,3},{3,1},{5,7},{7,5},{8,10},{10,8},{12,... | collective-permute-start | bytes 1572872 | tf_op jit(solution)/shard_map/ppermute | solution.py:11
  81.9 25.3 %collective-permute-start.3 = (f32[256,512]{0,1:T(8,128)S(1)}, f32[256,512]{0,1:T(8,128)S(1)}, u32[]{:S(2)}, u32[]{:S(2)}) collective-permute-start(f32[256,512]{0,1:T(8,128)S(1)} %slice.379), channel_id=1, source_target_pairs={{0,2},{2,0},{4,6},{6,4},{1,3},{3,1},{5,7},{7,5},{8,10},{10,8},{12,... | collective-permute-start | bytes 1572872 | tf_op jit(solution)/shard_map/ppermute | solution.py:11
  83.8 25.1 %collective-permute-start.24 = (f32[256,256]{0,1:T(8,128)S(1)}, f32[256,256]{0,1:T(8,128)S(1)}, u32[]{:S(2)}, u32[]{:S(2)}) collective-permute-start(f32[256,256]{0,1:T(8,128)S(1)} %slice_select_fusion), channel_id=1, source_target_pairs={{0,8},{8,0},{16,24},{24,16},{1,9},{9,1},{17,25},{25,17},{2,10},{10... | collective-permute-start | bytes 786440 | tf_op jit(solution)/shard_map/ppermute | solution.py:11
  85.6 23.9 %collective-permute-start.20 = (f32[256,256]{0,1:T(8,128)S(1)}, f32[256,256]{0,1:T(8,128)S(1)}, u32[]{:S(2)}, u32[]{:S(2)}) collective-permute-start(f32[256,256]{0,1:T(8,128)S(1)} %slice_select_fusion.1), channel_id=1, source_target_pairs={{0,8},{8,0},{16,24},{24,16},{1,9},{9,1},{17,25},{25,17},{2,10},{10... | collective-permute-start | bytes 786440 | tf_op jit(solution)/shard_map/ppermute | solution.py:11
  86.3 26.0 %collective-permute-start.16 = (f32[256,256]{0,1:T(8,128)S(1)}, f32[256,256]{0,1:T(8,128)S(1)}, u32[]{:S(2)}, u32[]{:S(2)}) collective-permute-start(f32[256,256]{0,1:T(8,128)S(1)} %slice_select_fusion.2), channel_id=1, source_target_pairs={{0,8},{8,0},{16,24},{24,16},{1,9},{9,1},{17,25},{25,17},{2,10},{10... | collective-permute-start | bytes 786440 | tf_op jit(solution)/shard_map/ppermute | solution.py:11
  97.0 15.8 %collective-permute-start.12 = (f32[256,256]{0,1:T(8,128)S(1)}, f32[256,256]{0,1:T(8,128)S(1)}, u32[]{:S(2)}, u32[]{:S(2)}) collective-permute-start(f32[256,256]{0,1:T(8,128)S(1)} %slice_select_fusion.3), channel_id=1, source_target_pairs={{0,8},{8,0},{16,24},{24,16},{1,9},{9,1},{17,25},{25,17},{2,10},{10... | collective-permute-start | bytes 786440 | tf_op jit(solution)/shard_map/ppermute | solution.py:11
  107.2 23.0 %collective-permute-start.8 = (f32[256,256]{0,1:T(8,128)S(1)}, f32[256,256]{0,1:T(8,128)S(1)}, u32[]{:S(2)}, u32[]{:S(2)}) collective-permute-start(f32[256,256]{0,1:T(8,128)S(1)} %slice_select_fusion.4), channel_id=1, source_target_pairs={{0,8},{8,0},{16,24},{24,16},{1,9},{9,1},{17,25},{25,17},{2,10},{10... | collective-permute-start | bytes 786440 | tf_op jit(solution)/shard_map/ppermute | solution.py:11
  109.0 19.6 %collective-permute-start.4 = (f32[256,256]{0,1:T(8,128)S(1)}, f32[256,256]{0,1:T(8,128)S(1)}, u32[]{:S(2)}, u32[]{:S(2)}) collective-permute-start(f32[256,256]{0,1:T(8,128)S(1)} %slice_select_fusion.5), channel_id=1, source_target_pairs={{0,8},{8,0},{16,24},{24,16},{1,9},{9,1},{17,25},{25,17},{2,10},{10... | collective-permute-start | bytes 786440 | tf_op jit(solution)/shard_map/ppermute | solution.py:11
  109.6 40.5 %collective-permute-start.25 = (f32[256,128]{0,1:T(8,128)S(1)}, f32[256,128]{0,1:T(8,128)S(1)}, u32[]{:S(2)}, u32[]{:S(2)}) collective-permute-start(f32[256,128]{0,1:T(8,128)S(1)} %slice_select_fusion.8), channel_id=1, source_target_pairs={{0,16},{8,24},{16,0},{24,8},{1,17},{9,25},{17,1},{25,9},{2,18},{10... | collective-permute-start | bytes 393224 | tf_op jit(solution)/shard_map/ppermute | solution.py:11
  112.3 37.8 %collective-permute-start.21 = (f32[256,128]{0,1:T(8,128)S(1)}, f32[256,128]{0,1:T(8,128)S(1)}, u32[]{:S(2)}, u32[]{:S(2)}) collective-permute-start(f32[256,128]{0,1:T(8,128)S(1)} %slice_select_fusion.9), channel_id=1, source_target_pairs={{0,16},{8,24},{16,0},{24,8},{1,17},{9,25},{17,1},{25,9},{2,18},{10... | collective-permute-start | bytes 393224 | tf_op jit(solution)/shard_map/ppermute | solution.py:11
  112.8 37.2 %collective-permute-start.17 = (f32[256,128]{0,1:T(8,128)S(1)}, f32[256,128]{0,1:T(8,128)S(1)}, u32[]{:S(2)}, u32[]{:S(2)}) collective-permute-start(f32[256,128]{0,1:T(8,128)S(1)} %slice_select_fusion.10), channel_id=1, source_target_pairs={{0,16},{8,24},{16,0},{24,8},{1,17},{9,25},{17,1},{25,9},{2,18},{10... | collective-permute-start | bytes 393224 | tf_op jit(solution)/shard_map/ppermute | solution.py:11
  115.5 34.6 %copy-start.1 = (f32[256,768]{0,1:T(8,128)S(1)}, f32[256,768]{0,1:T(8,128)}, u32[]{:S(2)}) copy-start(f32[256,768]{0,1:T(8,128)} %copy.8) | copy-start | bytes 2359300
  128.6 21.4 %collective-permute-start.13 = (f32[256,128]{0,1:T(8,128)S(1)}, f32[256,128]{0,1:T(8,128)S(1)}, u32[]{:S(2)}, u32[]{:S(2)}) collective-permute-start(f32[256,128]{0,1:T(8,128)S(1)} %slice_select_fusion.11), channel_id=1, source_target_pairs={{0,16},{8,24},{16,0},{24,8},{1,17},{9,25},{17,1},{25,9},{2,18},{10... | collective-permute-start | bytes 393224 | tf_op jit(solution)/shard_map/ppermute | solution.py:11
  130.2 11.6 %collective-permute-start.5 = (f32[256,128]{0,1:T(8,128)S(1)}, f32[256,128]{0,1:T(8,128)S(1)}, u32[]{:S(2)}, u32[]{:S(2)}) collective-permute-start(f32[256,128]{0,1:T(8,128)S(1)} %slice_select_fusion.13), channel_id=1, source_target_pairs={{0,16},{8,24},{16,0},{24,8},{1,17},{9,25},{17,1},{25,9},{2,18},{10... | collective-permute-start | bytes 393224 | tf_op jit(solution)/shard_map/ppermute | solution.py:11
  141.8 8.1 %collective-permute-start.9 = (f32[256,128]{0,1:T(8,128)S(1)}, f32[256,128]{0,1:T(8,128)S(1)}, u32[]{:S(2)}, u32[]{:S(2)}) collective-permute-start(f32[256,128]{0,1:T(8,128)S(1)} %slice_select_fusion.12), channel_id=1, source_target_pairs={{0,16},{8,24},{16,0},{24,8},{1,17},{9,25},{17,1},{25,9},{2,18},{10... | collective-permute-start | bytes 393224 | tf_op jit(solution)/shard_map/ppermute | solution.py:11
  150.3 1.2 collective-permute-start.26
  151.5 3.6 %collective-permute-start.27 = (f32[256]{0:T(256)S(1)}, f32[256]{0:T(256)S(1)}, u32[]{:S(2)}, u32[]{:S(2)}) collective-permute-start(f32[256]{0:T(256)S(1)} %max.9), channel_id=1, source_target_pairs={{0,8},{8,0},{16,24},{24,16},{1,9},{9,1},{17,25},{25,17},{2,10},{10... | collective-permute-start | bytes 3080 | tf_op jit(solution)/shard_map/ppermute | solution.py:11
  155.0 4.5 %collective-permute-start.28 = (f32[256]{0:T(256)S(1)}, f32[256]{0:T(256)S(1)}, u32[]{:S(2)}, u32[]{:S(2)}) collective-permute-start(f32[256]{0:T(256)S(1)} %max.10), channel_id=1, source_target_pairs={{0,16},{8,24},{16,0},{24,8},{1,17},{9,25},{17,1},{25,9},{2,18},{10... | collective-permute-start | bytes 3080 | tf_op jit(solution)/shard_map/ppermute | solution.py:11
  (25 other events, 170.7 us)

commit v2 on v0

v2 whole, which is shorter than its diff:
```python
import functools

import jax
import jax.numpy as jnp
from jax import lax
from jax.experimental import pallas as pl
from jax.experimental.pallas import tpu as pltpu
from jax.sharding import PartitionSpec as P

LANES = 128
F32, BF16 = jnp.float32, jnp.bfloat16
VMEM = "whole"
SMEM = pl.BlockSpec(memory_space=pltpu.SMEM)
ANY = pl.BlockSpec(memory_space=pl.ANY)

PANEL_ROUNDS = (
    ("n00n", ((1, 0), (2, 0), (2, 1), (1, 1))),
    ("011x", (None, (2, 0), (2, 1), (0, 1))),
    ("0nn0", ((0, 1), (1, 1), (1, 0), None)),
    ("1x00", ((0, 1), (0, 1), None, None)),
)
SHARES = (0, 2, 1, 3)
PORTIONS = (2, 2, 2, 2, 2, 2)


def dot(a, b):
    return jnp.dot(a, b, precision=lax.Precision.HIGHEST, preferred_element_type=F32)


def plain(left, upper, row_blocks, col_blocks, ancestor):
    row_on = jnp.repeat((row_blocks[0] > 0).astype(F32), left.shape[0] // row_blocks.shape[1])[:, None]
    col_on = jnp.repeat((col_blocks[0] > 0).astype(F32), upper.shape[1] // col_blocks.shape[1])[None, :]
    upper_full = lax.all_gather(upper, "row", axis=0, tiled=True)
    lower_full = lax.all_gather(left * row_on, "col", axis=1, tiled=True)
    leaf_count = lax.axis_size("leaf")
    share_cols = upper.shape[1] // leaf_count
    schur = lax.psum_scatter(dot(lower_full, upper_full) * col_on, "leaf", scatter_dimension=1, tiled=True)
    share = lax.dynamic_slice_in_dim(ancestor, lax.axis_index("leaf") * share_cols, share_cols, 1)
    updated = share - schur
    peak = lax.pmax(jnp.max(jnp.abs(updated), axis=1), ("leaf", "col"))
    return updated / (peak[:, None] + 1e-6)


def run(body, ins, outs, flops=0, limit=24):
    size = sum(4 * a.size for s, a in ins if s is VMEM) + sum(4 * o.size for o in outs)

    def whole(a):
        return pl.BlockSpec(a.shape, lambda step: (0,) * len(a.shape))

    return pl.pallas_call(
        body,
        grid=(1,),
        in_specs=[whole(a) if s is VMEM else s for s, a in ins],
        out_specs=[whole(o) for o in outs],
        out_shape=outs,
        compiler_params=pltpu.CompilerParams(vmem_limit_bytes=limit * 2**20),
        cost_estimate=pl.CostEstimate(flops=flops, bytes_accessed=size, transcendentals=0),
    )(*[a for _, a in ins])


def shape(*dims, dtype=F32):
    return jax.ShapeDtypeStruct(dims, dtype)


def split(x):
    high = x.astype(BF16)
    return high, (x - high.astype(F32)).astype(BF16)


def product(ah, al, b):
    bh, bl = split(b)
    d = functools.partial(jnp.dot, preferred_element_type=F32)
    return d(ah, bh) + (d(ah, bl) + d(al, bh))


def coordinates():
    row = lax.axis_index("row")
    return row % 2 == 1, row // 2 == 1, lax.axis_index("col") == 1


def pick(y, c, a, b, cc, d):
    return jnp.where(c, jnp.where(y, d, b), jnp.where(y, cc, a))


def copy_chunk(tiles, out, chunk):
    at, wide = chunk
    each = len(tiles) // len(SHARES)
    for k in range(len(SHARES)):
        done = 0
        for m in range(each):
            skip = (at + done) % LANES
            take = min(LANES - skip, wide - done)
            out[:, pl.ds(k * wide + done, take)] = tiles[k * each + m][:, pl.ds(skip, take)]
            done += take


def copy_message(tiles, out, chunks):
    at = 0
    for chunk in chunks:
        count = len(SHARES) * spanned(chunk)
        copy_chunk(tiles[:count], out.at[:, pl.ds(at, len(SHARES) * chunk[1])], chunk)
        tiles, at = tiles[count:], at + len(SHARES) * chunk[1]


def message_body(chunks, token, *refs):
    copy_message(refs[:-1], refs[-1], chunks)


def first_body(chunks, row_blocks, left, *refs):
    x, y, c = coordinates()
    depth = left.shape[1] // 2
    mask = jnp.where(row_blocks[0, 0] > 0, 1.0, 0.0).astype(F32)
    l0, l1 = left[:, :depth] * mask, left[:, depth:] * mask
    named = {"0": l0, "1": l1, "x": jnp.where(x, l1, l0), "n": jnp.where(x, l0, l1)}
    count = sum(len(SHARES) * spanned(c0) for c0 in chunks)
    tiles, outs = refs[:count], refs[count:]
    for out, (index, _) in zip(outs, PANEL_ROUNDS):
        out[...] = pick(y, c, *(named[k] for k in index))
    outs[4][:, :depth] = l0
    outs[4][:, depth:] = l1
    copy_message(tiles, outs[5], chunks)


def spanned(chunk):
    at, wide = chunk
    return (at + wide - 1) // LANES - at // LANES + 1


def panel_body(left, *refs):
    x, y, c = coordinates()
    height, depth = left.shape[0], left.shape[1] // 2
    r1, r2, r3, r4 = (r[...] for r in refs[:4])
    l0, l1 = left[:, :depth], left[:, depth:]
    lx = jnp.where(x, l1, l0)
    partner = pick(y, c, r1, r1, r3, r1), pick(y, c, r3, r2, r1, r2)
    own = pick(y, c, lx, r3, lx, l0), pick(y, c, r4, r4, r2, l1)
    second = jnp.logical_or(jnp.logical_and(c, x), jnp.logical_and(jnp.logical_not(c), y))
    for at in (0, 1):
        high, low = refs[4 + 2 * at:6 + 2 * at]
        for rows, pair in ((pl.ds(0, height), partner), (pl.ds(height, height), own)):
            a, b = pair[::-1] if at else pair
            high[rows], low[rows] = split(jnp.where(second, b, a))


def multiply_body(half, plan, col_blocks, ah, al, bh, bl, block, got, token, *refs):
    ranges, begin, wide, later = plan
    tiles, (send, keep), rest = refs[:-2 - bool(later)], refs[len(refs) - 2 - bool(later):][:2], refs[-1]
    own, other = block[:, pl.ds(begin, wide)], got[:, pl.ds(begin, wide)]
    for out, rows in ((send, pl.ds(0, half)), (keep, pl.ds(half, half))):
        value = product(ah[rows], al[rows], own) + product(bh[rows], bl[rows], other)
        for at, width, b in ranges:
            on = jnp.where(col_blocks[0, b] > 0, 1.0, 0.0).astype(F32)
            out[:, pl.ds(at, width)] = value[:, at:at + width] * on
    if later:
        copy_message(tiles, rest, later)


def reduce_body(jobs, *refs):
    n_in = sum(count for _, count, _ in jobs)
    ins, outs = list(refs[:n_in]), list(refs[n_in + 1:])
    leaf = lax.axis_index("leaf")
    for step, count, wide in jobs:
        mine, ins = ins[:count], ins[count:]
        send, keep, outs = outs[0], outs[1], outs[2:]
        if step == "f":
            got, kept, share, peak = mine
            value = share[...] - (kept[...] + got[...])
            send[...] = value
            top = jnp.max(jnp.abs(value), axis=1, keepdims=True)
            keep[...] = jnp.maximum(peak[...], jnp.broadcast_to(top, keep.shape))
            continue
        bit = (leaf % 2 if step == "o" else leaf // 2) == 1
        half = 2 * wide if step == "o" else wide
        total = mine[0][...] + mine[1][...]
        a, b = total[:, :half], total[:, half:]
        send[...] = jnp.where(bit, a, b)
        keep[...] = jnp.where(bit, b, a)


def swap(value, axis, size, bit):
    return lax.ppermute(value, axis, [(i, i ^ bit) for i in range(size)])


def after(value, *others):
    return lax.optimization_barrier((value,) + others)[0]


STEPS = (
    "A0", "A1", "o0", "A2", "o1t0", "A3", "o2t1", "A4", "f0o3t2", "A5", "f1o4", "t3", "f2o5", "t4", "f3t5", "f4", "f5",
)
GATHERS = ((0,), (1,), (2,), (3,), (4,), (5,))
TIES = (None, None, 0, 1, 2, 3)
FIRST = 56


def chunked(left, upper, row_blocks, col_blocks, ancestor):
    rows, cols = lax.axis_size("row"), lax.axis_size("col")
    leaf_count = lax.axis_size("leaf")
    leaf, row, col = (lax.axis_index(a).astype(jnp.int32) for a in ("leaf", "row", "col"))
    depth, height = upper.shape[0], left.shape[0]
    share_cols = upper.shape[1] // leaf_count
    block_cols = upper.shape[1] // col_blocks.shape[1]
    unit = share_cols // sum(PORTIONS)
    chunks, at = [], 0
    for p in PORTIONS:
        chunks.append((at, p * unit))
        at += p * unit
    n = len(chunks)
    def move(value, flip):
        pairs = []
        for r in range(rows):
            for c in range(cols):
                hop = flip(r, c)
                if hop is not None:
                    pairs.append((cols * r + c, cols * (r ^ hop[0]) + (c ^ hop[1])))
        return lax.ppermute(value, ("row", "col"), pairs)

    def gather(value):
        return move(value, lambda r, c: (1 if c else 2, 0))

    def exchange(value):
        return move(value, lambda r, c: (2 if c else 1, 0))

    def tiles(chunk):
        at, _ = chunk
        return [
            (pl.BlockSpec((depth, LANES), functools.partial(lambda k, step: (0, k), (s * share_cols + at) // LANES + m)), upper)
            for s in SHARES for m in range(spanned(chunk))
        ]

    def tiles_of(members):
        return [spec for i in members for spec in tiles(chunks[i])]

    def widths(members):
        return 4 * sum(chunks[i][1] for i in members)

    first = run(
        functools.partial(first_body, [chunks[i] for i in GATHERS[0]]),
        [(SMEM, row_blocks), (VMEM, left)] + tiles_of(GATHERS[0]),
        [shape(height, depth)] * 4 + [shape(height, 2 * depth), shape(depth, widths(GATHERS[0]))],
        limit=FIRST,
    )
    blocks, gots = {0: first[5]}, {0: gather(first[5])}
    landed = [move(v, lambda r, c, hops=hops: hops[(r // 2) * 2 + c]) for v, (_, hops) in zip(first[:4], PANEL_ROUNDS)]
    lower = first[4]
    for g, tie in enumerate(TIES):
        if g and tie is None:
            blocks[g], = run(
                functools.partial(message_body, [chunks[i] for i in GATHERS[g]]),
                [(ANY, lower)] + tiles_of(GATHERS[g]), [shape(depth, widths(GATHERS[g]))], limit=FIRST,
            )
            gots[g] = gather(blocks[g])
    halves = run(panel_body, [(VMEM, lower)] + [(VMEM, v) for v in landed], [shape(2 * height, depth, dtype=BF16)] * 4)

    share = lax.dynamic_slice_in_dim(after(ancestor, halves[0]), leaf * share_cols, share_cols, 1)
    x_got, kept, z1, z1_kept, z2, z2_kept, upds = ({} for _ in range(7))
    peak = jnp.zeros((height, LANES), F32)
    token = lower
    for word in STEPS:
        if word[0] == "A":
            t = int(word[1:])
            at, wide = chunks[t]
            ranges = []
            for k, s in enumerate(SHARES):
                start = s * share_cols + at
                end, base = start + wide, start
                while start < end:
                    stop = min(end, (start // block_cols + 1) * block_cols)
                    ranges.append((k * wide + start - base, stop - start, start // block_cols))
                    start = stop
            g = [t in members for members in GATHERS].index(True)
            begin = widths([i for i in GATHERS[g] if i < t])
            later = [k for k, tie in enumerate(TIES) if tie == t]
            members = [chunks[i] for k in later for i in GATHERS[k]]
            res = run(
                functools.partial(multiply_body, height, (ranges, begin, 4 * wide, members)),
                [(SMEM, col_blocks)] + [(VMEM, h) for h in halves] + [(VMEM, blocks[g]), (VMEM, gots[g]), (ANY, token)]
                + [spec for k in later for spec in tiles_of(GATHERS[k])],
                [shape(height, 4 * wide)] * 2 + [shape(depth, widths(GATHERS[k])) for k in later],
                flops=48 * height * depth * wide,
            )
            kept[t] = token = res[1]
            for k in later:
                blocks[k] = res[2]
                gots[k] = gather(res[2])
            x_got[t] = exchange(res[0])
            continue
        todo = [(word[i], int(word[i + 1])) for i in range(0, len(word), 2)]
        jobs, ins, outs = [], [], []
        for step, t in todo:
            at, wide = chunks[t]
            if step == "o":
                mine, new = [x_got[t], kept[t]], [shape(height, 2 * wide)] * 2
            elif step == "t":
                mine, new = [z1[t], z1_kept[t]], [shape(height, wide)] * 2
            else:
                mine, new = [z2[t], z2_kept[t], share[:, at:at + wide], peak], [shape(height, wide), shape(height, LANES)]
            jobs.append((step, len(mine), wide))
            ins += [(VMEM, v) for v in mine]
            outs += new
        res = run(functools.partial(reduce_body, jobs), ins + [(ANY, token)], outs)
        token = res[1]
        tops = []
        for k, (step, t) in enumerate(todo):
            a, b = res[2 * k], res[2 * k + 1]
            if step == "o":
                z1[t], z1_kept[t] = swap(a, "leaf", leaf_count, 1), b
            elif step == "t":
                z2[t], z2_kept[t] = swap(a, "leaf", leaf_count, 2), b
            else:
                upds[t] = a
                tops.append(b)
        if tops:
            peak = functools.reduce(jnp.maximum, tops)

    updated = jnp.concatenate([upds[g] for g in range(n)], 1)
    top = jnp.max(peak, axis=1)
    top = jnp.maximum(top, swap(top, "col", cols, 1))
    for bit in (1, 2):
        top = jnp.maximum(top, swap(top, "leaf", leaf_count, bit))
    return updated / (top[:, None] + 1e-6)


def solution(mesh):
    leaf_count, rows, cols = (mesh.shape[a] for a in ("leaf", "row", "col"))

    def shards(left_panels, upper_panels, row_blocks, col_blocks, ancestor):
        share_cols = upper_panels.shape[2] // leaf_count
        fits = (
            rows == 4 and cols == 2 and leaf_count == 4
            and share_cols % (sum(PORTIONS) * 64) == 0
            and left_panels.shape[2] == 2 * upper_panels.shape[1]
            and row_blocks.shape[1] == 1
        )
        body = chunked if fits else plain
        return body(left_panels[0], upper_panels[0], row_blocks, col_blocks, ancestor)

    return jax.shard_map(
        shards,
        mesh=mesh,
        in_specs=(
            P("leaf", "row", "col"),
            P("leaf", "row", "col"),
            P("leaf", "row"),
            P("leaf", "col"),
            P("row", "col"),
        ),
        out_specs=P("row", ("col", "leaf")),
        check_vma=False,
    )
```

time: 247 us -> 125 us (0.51)
  waiting for transfers between devices: 193 us -> 35.5 us
  starting transfers between devices: 0.09 us -> 65.8 us
  Pallas kernels: 0 us -> 18.5 us
  blocking collectives: 15.4 us -> 0 us
  matrix products: 14.6 us -> 0 us
  between operations: 13.8 us -> 0.94 us
  other arithmetic: 10 us -> 1.13 us
  local copies, waits for them, and re-layouts: 0.08 us -> 2.68 us
    all_gather x2 -> x0, waiting for transfers between devices: 133 us -> none  [the longest x1 126 us: shards(): upper_full = lax.all_gather(upper, 'row', axis=0, tiled=True)]
    ppermute x0 -> x31, starting transfers between devices: none -> 65.8 us  [the longest x16 43.5 us: move(): return lax.ppermute(value, ('row', 'col'), pairs)]
    reduce_scatter x1 -> x0, waiting for transfers between devices: 60.4 us -> none  [shards(): lax.psum_scatter(partial_value, 'leaf', scatter_dimension=1, tiled=True)]
    ppermute x0 -> x31, waiting for transfers between devices: none -> 35.5 us  [the longest x15 31.1 us: swap(): return lax.ppermute(value, axis, [(i, i ^ bit) for i in range(size)])]
    pallas_call x0 -> x20, Pallas kernels: none -> 18.5 us  [run(): pl.pallas_call(body, grid=(1,), in_specs=[whole(a) if s is VMEM else s fo...]
    pmax x1 -> x0, blocking collectives: 15.4 us -> none  [shards(): peak = lax.pmax(jnp.max(jnp.abs(updated), axis=1), ('leaf', 'col'))]
    dot_general x1 -> x0, matrix products: 14.6 us -> none  [shards(): jnp.dot(lax.all_gather(lower, 'col', axis=1, tiled=True), upper_full, pre...]
    mul x2 -> x0, other arithmetic: 5.88 us -> none  [the longest x1 4 us: shards(): upper = upper_panels[0] * col_mask[None, :]]
  transfers between devices with their start and end apart: 3 -> 31, of which waited for: 3 -> 14; matrix products, arithmetic and copies ran while one was open for 2% -> 1% of each run, Pallas kernels for 0% -> 13%
where the time goes in v2:
time: 125 us; the launch traced here: 124 us
  starting transfers between devices  65.8 us (53%)
  waiting for transfers between devices  35.5 us (28%)
  Pallas kernels  18.5 us (15%)
  local copies, waits for them, and re-layouts  2.68 us (2%)
    ppermute x16, starting transfers between devices, move(): return lax.ppermute(value, ('row', 'col'), pairs)  43.5 us
    ppermute x15, waiting for transfers between devices, swap(): return lax.ppermute(value, axis, [(i, i ^ bit) for i in range(size)])  31.1 us
    ppermute x15, starting transfers between devices, swap(): return lax.ppermute(value, axis, [(i, i ^ bit) for i in range(size)])  22.3 us
    pallas_call x20, Pallas kernels, run(): pl.pallas_call(body, grid=(1,), in_specs=[whole(a) if s is VMEM else s fo...  18.5 us
    ppermute x16, waiting for transfers between devices, move(): return lax.ppermute(value, ('row', 'col'), pairs)  4.36 us
  transfers between devices with their start and end apart: 31, of which 14 were waited for; matrix products, arithmetic and copies ran while one was open for 1% of the time, Pallas kernels for 13%

profile of v2, /device:TPU:0, one launch (start us, length us, event | category | flops | bytes accessed | tf_op | source)
XLA Modules:
  0.0 124.5 jit_solution(15127600155180166506)
XLA Ops:
  0.7 2.7 %shard_map.55 = (f32[256,256]{1,0:T(8,128)}, f32[256,256]{1,0:T(8,128)}, f32[256,256]{1,0:T(8,128)}, f32[256,256]{1,0:T(8,128)}, f32[256,512]{1,0:T(8,128)}, /*index=5*/f32[256,512]{1,0:T(8,128)}) custom-call(s32[1,1]{1,0:T(1,128)S(6)} %copy.11.row_blocks, f32[256,512]{1,0:T(8,128)} %bitcast.26, f32[256,3072]{1,0:T(8,128)} %bitcast.2, f32[256,3072]{1,0:T(8,128)} %bitcast.3, ...), custom_call_target="tpu_custom_call" | custom-call | bytes 2621440 | tf_op jit(solution)/shard_map/pallas_call | solution.py:50
  3.3 3.0 %collective-permute-start.5 = (f32[256,512]{1,0:T(8,128)}, f32[256,512]{1,0:T(8,128)S(1)}, u32[]{:S(2)}, u32[]{:S(2)}) collective-permute-start(f32[256,512]{1,0:T(8,128)} %get-tuple-element.77.block), channel_id=1, source_target_pairs={{0,4},{1,3},{2,6},{3,1},{4,0},{5,7},{6,2},{7,5},{8,12},{9,11},{10,... | collective-permute-start | bytes 1572872 | tf_op jit(solution)/shard_map/ppermute | solution.py:216
  6.3 1.5 %collective-permute-start = (f32[256,256]{1,0:T(8,128)}, f32[256,256]{1,0:T(8,128)S(1)}, u32[]{:S(2)}, u32[]{:S(2)}) collective-permute-start(f32[256,256]{1,0:T(8,128)} %get-tuple-element.69), channel_id=1, source_target_pairs={{0,2},{1,5},{2,0},{3,7},{4,1},{5,6},{6,3},{7,4},{8,10},{9,13},{10,... | collective-permute-start | bytes 786440 | tf_op jit(solution)/shard_map/ppermute | solution.py:216
  8.4 3.5 %collective-permute-start.2 = (f32[256,256]{1,0:T(8,128)}, f32[256,256]{1,0:T(8,128)S(1)}, u32[]{:S(2)}, u32[]{:S(2)}) collective-permute-start(f32[256,256]{1,0:T(8,128)} %get-tuple-element.71), channel_id=1, source_target_pairs={{0,1},{1,2},{2,3},{3,0},{4,6},{6,4},{8,9},{9,10},{10,11},{11,8},{1... | collective-permute-start | bytes 786440 | tf_op jit(solution)/shard_map/ppermute | solution.py:216
  11.9 1.9 %collective-permute-start.3 = (f32[256,256]{1,0:T(8,128)}, f32[256,256]{1,0:T(8,128)S(1)}, u32[]{:S(2)}, u32[]{:S(2)}) collective-permute-start(f32[256,256]{1,0:T(8,128)} %get-tuple-element.72), channel_id=1, source_target_pairs={{0,1},{1,0},{2,3},{3,2},{8,9},{9,8},{10,11},{11,10},{16,17},{17,16... | collective-permute-start | bytes 786440 | tf_op jit(solution)/shard_map/ppermute | solution.py:216
  13.9 2.1 %shard_map.57.block = f32[256,512]{1,0:T(8,128)} custom-call(f32[256,512]{1,0:T(8,128)} %get-tuple-element.68.left.token, f32[256,3072]{1,0:T(8,128)} %bitcast.6, f32[256,3072]{1,0:T(8,128)} %bitcast.7, f32[256,3072]{1,0:T(8,128)} %bitcast.8, f32[256,3072]{1,0:T(8,128)} %bitcast.9), custom_call_target="tpu_custom_call" | custom-call | bytes 524288 | tf_op jit(solution)/shard_map/pallas_call | solution.py:50
  16.0 2.3 %collective-permute-start.4 = (f32[256,512]{1,0:T(8,128)}, f32[256,512]{1,0:T(8,128)S(1)}, u32[]{:S(2)}, u32[]{:S(2)}) collective-permute-start(f32[256,512]{1,0:T(8,128)} %shard_map.57.block), channel_id=1, source_target_pairs={{0,4},{1,3},{2,6},{3,1},{4,0},{5,7},{6,2},{7,5},{8,12},{9,11},{10,... | collective-permute-start | bytes 1572872 | tf_op jit(solution)/shard_map/ppermute | solution.py:216
  18.8 1.6 %shard_map.58 = (f32[256,512]{1,0:T(8,128)S(1)}, f32[256,512]{1,0:T(8,128)S(1)}, f32[256,512]{1,0:T(8,128)S(1)}) custom-call(s32[1,12]{1,0:T(1,128)S(1)} %copy-done.6, bf16[512,256]{1,0:T(8,128)(2,1)S(1)} %get-tuple-element.73.ah, bf16[512,256]{1,0:T(8,128)(2,1)S(1)} %get-tuple-element.74.al, bf16[512,256]{1,0:T(8,128)(2,1)S(1)} %get-tuple-element.75.bh, ...), custom_call_target="tpu_custom_call" | custom-call | flops 402653184 | bytes 4718592 | tf_op jit(solution)/shard_map/pallas_call | solution.py:50
  20.5 2.4 %collective-permute-start.7 = (f32[256,512]{1,0:T(8,128)S(1)}, f32[256,512]{1,0:T(8,128)S(1)}, u32[]{:S(2)}, u32[]{:S(2)}) collective-permute-start(f32[256,512]{1,0:T(8,128)S(1)} %get-tuple-element.81), channel_id=1, source_target_pairs={{0,2},{1,5},{2,0},{3,7},{4,6},{5,1},{6,4},{7,3},{8,10},{9,13},{10,... | collective-permute-start | bytes 1572872 | tf_op jit(solution)/shard_map/ppermute | solution.py:216
  23.7 3.5 %collective-permute-done.4.got = f32[256,512]{1,0:T(8,128)S(1)} collective-permute-done((f32[256,512]{1,0:T(8,128)}, f32[256,512]{1,0:T(8,128)S(1)}, u32[]{:S(2)}, u32[]{:S(2)}) %collective-permute-start.4) | collective-permute-done | bytes 524320 | tf_op jit(solution)/shard_map/ppermute | solution.py:216
  27.2 1.6 %shard_map.59 = (f32[256,512]{1,0:T(8,128)S(1)}, f32[256,512]{1,0:T(8,128)S(1)}, f32[256,512]{1,0:T(8,128)S(1)}) custom-call(s32[1,12]{1,0:T(1,128)S(1)} %copy-done.6, bf16[512,256]{1,0:T(8,128)(2,1)S(1)} %get-tuple-element.73.ah, bf16[512,256]{1,0:T(8,128)(2,1)S(1)} %get-tuple-element.74.al, bf16[512,256]{1,0:T(8,128)(2,1)S(1)} %get-tuple-element.75.bh, ...), custom_call_target="tpu_custom_call" | custom-call | flops 402653184 | bytes 4718592 | tf_op jit(solution)/shard_map/pallas_call | solution.py:50
  28.8 4.9 %collective-permute-start.6 = (f32[256,512]{1,0:T(8,128)S(1)}, f32[256,512]{1,0:T(8,128)S(1)}, u32[]{:S(2)}, u32[]{:S(2)}) collective-permute-start(f32[256,512]{1,0:T(8,128)S(1)} %get-tuple-element.79), channel_id=1, source_target_pairs={{0,2},{1,5},{2,0},{3,7},{4,6},{5,1},{6,4},{7,3},{8,10},{9,13},{10,... | collective-permute-start | bytes 1572872 | tf_op jit(solution)/shard_map/ppermute | solution.py:216
  33.6 2.4 %collective-permute-start.11 = (f32[256,512]{1,0:T(8,128)S(1)}, f32[256,512]{1,0:T(8,128)S(1)}, u32[]{:S(2)}, u32[]{:S(2)}) collective-permute-start(f32[256,512]{1,0:T(8,128)S(1)} %get-tuple-element.89.block), channel_id=1, source_target_pairs={{0,4},{1,3},{2,6},{3,1},{4,0},{5,7},{6,2},{7,5},{8,12},{9,11},{10,... | collective-permute-start | bytes 1572872 | tf_op jit(solution)/shard_map/ppermute | solution.py:216
  36.1 1.6 %collective-permute-start.8 = (f32[256,256]{1,0:T(8,128)S(1)}, f32[256,256]{1,0:T(8,128)S(1)}, u32[]{:S(2)}, u32[]{:S(2)}) collective-permute-start(f32[256,256]{1,0:T(8,128)S(1)} %get-tuple-element.82), channel_id=1, source_target_pairs={{0,8},{8,0},{16,24},{24,16},{1,9},{9,1},{17,25},{25,17},{2,10},{10... | collective-permute-start | bytes 786440 | tf_op jit(solution)/shard_map/ppermute | solution.py:181
  38.4 1.6 %shard_map.61 = (f32[256,512]{1,0:T(8,128)S(1)}, f32[256,512]{1,0:T(8,128)S(1)}, f32[256,512]{1,0:T(8,128)S(1)}) custom-call(s32[1,12]{1,0:T(1,128)S(1)} %copy-done.6, bf16[512,256]{1,0:T(8,128)(2,1)S(1)} %get-tuple-element.73.ah, bf16[512,256]{1,0:T(8,128)(2,1)S(1)} %get-tuple-element.74.al, bf16[512,256]{1,0:T(8,128)(2,1)S(1)} %get-tuple-element.75.bh, ...), custom_call_target="tpu_custom_call" | custom-call | flops 402653184 | bytes 4718592 | tf_op jit(solution)/shard_map/pallas_call | solution.py:50
  40.0 4.8 %collective-permute-start.13 = (f32[256,512]{1,0:T(8,128)S(1)}, f32[256,512]{1,0:T(8,128)S(1)}, u32[]{:S(2)}, u32[]{:S(2)}) collective-permute-start(f32[256,512]{1,0:T(8,128)S(1)} %get-tuple-element.93), channel_id=1, source_target_pairs={{0,2},{1,5},{2,0},{3,7},{4,6},{5,1},{6,4},{7,3},{8,10},{9,13},{10,... | collective-permute-start | bytes 1572872 | tf_op jit(solution)/shard_map/ppermute | solution.py:216
  44.8 2.5 %collective-permute-start.16 = (f32[256,512]{1,0:T(8,128)S(1)}, f32[256,512]{1,0:T(8,128)}, u32[]{:S(2)}, u32[]{:S(2)}) collective-permute-start(f32[256,512]{1,0:T(8,128)S(1)} %get-tuple-element.97.block), channel_id=1, source_target_pairs={{0,4},{1,3},{2,6},{3,1},{4,0},{5,7},{6,2},{7,5},{8,12},{9,11},{10,... | collective-permute-start | bytes 1572872 | tf_op jit(solution)/shard_map/ppermute | solution.py:216
  48.0 1.6 %collective-permute-start.14 = (f32[256,256]{1,0:T(8,128)S(1)}, f32[256,256]{1,0:T(8,128)S(1)}, u32[]{:S(2)}, u32[]{:S(2)}) collective-permute-start(f32[256,256]{1,0:T(8,128)S(1)} %get-tuple-element.94), channel_id=1, source_target_pairs={{0,8},{8,0},{16,24},{24,16},{1,9},{9,1},{17,25},{25,17},{2,10},{10... | collective-permute-start | bytes 786440 | tf_op jit(solution)/shard_map/ppermute | solution.py:181
  49.6 2.0 %shard_map.63 = (f32[256,512]{1,0:T(8,128)}, f32[256,512]{1,0:T(8,128)S(1)}, f32[256,512]{1,0:T(8,128)S(1)}) custom-call(s32[1,12]{1,0:T(1,128)S(1)} %copy-done.6, bf16[512,256]{1,0:T(8,128)(2,1)S(1)} %get-tuple-element.73.ah, bf16[512,256]{1,0:T(8,128)(2,1)S(1)} %get-tuple-element.74.al, bf16[512,256]{1,0:T(8,128)(2,1)S(1)} %get-tuple-element.75.bh, ...), custom_call_target="tpu_custom_call" | custom-call | flops 402653184 | bytes 4718592 | tf_op jit(solution)/shard_map/pallas_call | solution.py:50
  51.6 4.7 %collective-permute-start.12 = (f32[256,512]{1,0:T(8,128)}, f32[256,512]{1,0:T(8,128)}, u32[]{:S(2)}, u32[]{:S(2)}) collective-permute-start(f32[256,512]{1,0:T(8,128)} %get-tuple-element.91), channel_id=1, source_target_pairs={{0,2},{1,5},{2,0},{3,7},{4,6},{5,1},{6,4},{7,3},{8,10},{9,13},{10,... | collective-permute-start | bytes 1572872 | tf_op jit(solution)/shard_map/ppermute | solution.py:216
  56.3 2.5 %collective-permute-start.19 = (f32[256,512]{1,0:T(8,128)S(1)}, f32[256,512]{1,0:T(8,128)S(1)}, u32[]{:S(2)}, u32[]{:S(2)}) collective-permute-start(f32[256,512]{1,0:T(8,128)S(1)} %get-tuple-element.104.block), channel_id=1, source_target_pairs={{0,4},{1,3},{2,6},{3,1},{4,0},{5,7},{6,2},{7,5},{8,12},{9,11},{10,... | collective-permute-start | bytes 1572872 | tf_op jit(solution)/shard_map/ppermute | solution.py:216
  60.3 1.6 %collective-permute-start.15 = (f32[256,256]{1,0:T(8,128)}, f32[256,256]{1,0:T(8,128)}, u32[]{:S(2)}, u32[]{:S(2)}) collective-permute-start(f32[256,256]{1,0:T(8,128)} %get-tuple-element.95), channel_id=1, source_target_pairs={{0,8},{8,0},{16,24},{24,16},{1,9},{9,1},{17,25},{25,17},{2,10},{10... | collective-permute-start | bytes 786440 | tf_op jit(solution)/shard_map/ppermute | solution.py:181
  61.8 2.6 %collective-permute-start.10 = (f32[256,128]{1,0:T(8,128)}, f32[256,128]{1,0:T(8,128)S(1)}, u32[]{:S(2)}, u32[]{:S(2)}) collective-permute-start(f32[256,128]{1,0:T(8,128)} %copy-done.9), channel_id=1, source_target_pairs={{0,16},{8,24},{16,0},{24,8},{1,17},{9,25},{17,1},{25,9},{2,18},{10... | collective-permute-start | bytes 393224 | tf_op jit(solution)/shard_map/ppermute | solution.py:181
  64.4 1.3 %constant_dynamic-slice_fusion.5 = (f32[256,128]{1,0:T(8,128)S(1)}, f32[256,128]{1,0:T(8,128)S(1)}, f32[256,128]{1,0:T(8,128)S(1)}, f32[256,128]{1,0:T(8,128)S(1...) fusion(f32[256,3072]{1,0:T(8,128)} %param.9, s32[]{:T(128)S(6)} %add.17, s32[]{:T(128)S(6)} %add.16, s32[]{:T(128)S(6)} %add.15, ...), kind=kLoop, calls=%fused_computation.12 | loop fusion | bytes 1572888 | tf_op jit(solution)/shard_map/slice | solution.py:297
  65.7 2.1 %shard_map.65 = (f32[256,512]{1,0:T(8,128)S(1)}, f32[256,512]{1,0:T(8,128)S(1)}) custom-call(s32[1,12]{1,0:T(1,128)S(1)} %copy-done.6, bf16[512,256]{1,0:T(8,128)(2,1)S(1)} %get-tuple-element.73.ah, bf16[512,256]{1,0:T(8,128)(2,1)S(1)} %get-tuple-element.74.al, bf16[512,256]{1,0:T(8,128)(2,1)S(1)} %get-tuple-element.75.bh, ...), custom_call_target="tpu_custom_call" | custom-call | flops 402653184 | bytes 4194304 | tf_op jit(solution)/shard_map/pallas_call | solution.py:50
  67.8 1.5 %collective-permute-start.18 = (f32[256,512]{1,0:T(8,128)S(1)}, f32[256,512]{1,0:T(8,128)S(1)}, u32[]{:S(2)}, u32[]{:S(2)}) collective-permute-start(f32[256,512]{1,0:T(8,128)S(1)} %get-tuple-element.103), channel_id=1, source_target_pairs={{0,2},{1,5},{2,0},{3,7},{4,6},{5,1},{6,4},{7,3},{8,10},{9,13},{10,... | collective-permute-start | bytes 1572872 | tf_op jit(solution)/shard_map/ppermute | solution.py:216
  69.3 0.8 collective-permute-done.10.refs_0_
  70.1 0.9 collective-permute-done.15.refs_6_
  71.0 1.4 %shard_map.66 = (f32[256,128]{1,0:T(8,128)S(1)}, f32[256,128]{1,0:T(8,128)S(1)}, f32[256,256]{1,0:T(8,128)S(1)}, f32[256,256]{1,0:T(8,128)S(1)}, f32[256,128]{1,0:T(8,128)S(1)}, /*index=5*/f32[256,128]{1,0:T(8,128)S(1)}) custom-call(f32[256,128]{1,0:T(8,128)S(1)} %collective-permute-done.10.refs_0_, f32[256,128]{1,0:T(8,128)S(1)} %copy-done.5, ...), custom_call_target="tpu_custom_call" | custom-call | bytes 3145728 | tf_op jit(solution)/shard_map/pallas_call | solution.py:50
  72.4 1.5 %shard_map.67 = (f32[256,512]{1,0:T(8,128)S(1)}, f32[256,512]{1,0:T(8,128)S(1)}) custom-call(s32[1,12]{1,0:T(1,128)S(1)} %copy-done.6, bf16[512,256]{1,0:T(8,128)(2,1)S(1)} %get-tuple-element.73.ah, bf16[512,256]{1,0:T(8,128)(2,1)S(1)} %get-tuple-element.74.al, bf16[512,256]{1,0:T(8,128)(2,1)S(1)} %get-tuple-element.75.bh, ...), custom_call_target="tpu_custom_call" | custom-call | flops 402653184 | bytes 4194304 | tf_op jit(solution)/shard_map/pallas_call | solution.py:50
  74.0 4.3 %collective-permute-start.21 = (f32[256,512]{1,0:T(8,128)S(1)}, f32[256,512]{1,0:T(8,128)S(1)}, u32[]{:S(2)}, u32[]{:S(2)}) collective-permute-start(f32[256,512]{1,0:T(8,128)S(1)} %get-tuple-element.110), channel_id=1, source_target_pairs={{0,2},{1,5},{2,0},{3,7},{4,6},{5,1},{6,4},{7,3},{8,10},{9,13},{10,... | collective-permute-start | bytes 1572872 | tf_op jit(solution)/shard_map/ppermute | solution.py:216
  78.3 1.7 %collective-permute-start.22 = (f32[256,256]{1,0:T(8,128)S(1)}, f32[256,256]{1,0:T(8,128)S(1)}, u32[]{:S(2)}, u32[]{:S(2)}) collective-permute-start(f32[256,256]{1,0:T(8,128)S(1)} %get-tuple-element.111), channel_id=1, source_target_pairs={{0,8},{8,0},{16,24},{24,16},{1,9},{9,1},{17,25},{25,17},{2,10},{10... | collective-permute-start | bytes 786440 | tf_op jit(solution)/shard_map/ppermute | solution.py:181
  80.0 2.6 %collective-permute-start.17 = (f32[256,128]{1,0:T(8,128)S(1)}, f32[256,128]{1,0:T(8,128)S(1)}, u32[]{:S(2)}, u32[]{:S(2)}) collective-permute-start(f32[256,128]{1,0:T(8,128)S(1)} %copy-done.8), channel_id=1, source_target_pairs={{0,16},{8,24},{16,0},{24,8},{1,17},{9,25},{17,1},{25,9},{2,18},{10... | collective-permute-start | bytes 393224 | tf_op jit(solution)/shard_map/ppermute | solution.py:181
  82.9 6.6 %collective-permute-done.17.refs_0_ = f32[256,128]{1,0:T(8,128)S(1)} collective-permute-done((f32[256,128]{1,0:T(8,128)S(1)}, f32[256,128]{1,0:T(8,128)S(1)}, u32[]{:S(2)}, u32[]{:S(2)}) %collective-permute-start.17) | collective-permute-done | bytes 131104 | tf_op jit(solution)/shard_map/ppermute | solution.py:181
  89.7 1.8 %collective-permute-start.25 = (f32[256,256]{1,0:T(8,128)S(1)}, f32[256,256]{1,0:T(8,128)S(1)}, u32[]{:S(2)}, u32[]{:S(2)}) collective-permute-start(f32[256,256]{1,0:T(8,128)S(1)} %get-tuple-element.119), channel_id=1, source_target_pairs={{0,8},{8,0},{16,24},{24,16},{1,9},{9,1},{17,25},{25,17},{2,10},{10... | collective-permute-start | bytes 786440 | tf_op jit(solution)/shard_map/ppermute | solution.py:181
  91.5 0.9 collective-permute-done.20.refs_0_
  92.5 1.8 %collective-permute-start.24 = (f32[256,256]{1,0:T(8,128)S(1)}, f32[256,256]{1,0:T(8,128)S(1)}, u32[]{:S(2)}, u32[]{:S(2)}) collective-permute-start(f32[256,256]{1,0:T(8,128)S(1)} %get-tuple-element.117), channel_id=1, source_target_pairs={{0,8},{8,0},{16,24},{24,16},{1,9},{9,1},{17,25},{25,17},{2,10},{10... | collective-permute-start | bytes 786440 | tf_op jit(solution)/shard_map/ppermute | solution.py:181
  94.3 1.8 %collective-permute-start.23 = (f32[256,128]{1,0:T(8,128)S(1)}, f32[256,128]{1,0:T(8,128)S(1)}, u32[]{:S(2)}, u32[]{:S(2)}) collective-permute-start(f32[256,128]{1,0:T(8,128)S(1)} %get-tuple-element.115), channel_id=1, source_target_pairs={{0,16},{8,24},{16,0},{24,8},{1,17},{9,25},{17,1},{25,9},{2,18},{10... | collective-permute-start | bytes 393224 | tf_op jit(solution)/shard_map/ppermute | solution.py:181
  96.1 5.4 %collective-permute-done.25.refs_0_ = f32[256,256]{1,0:T(8,128)S(1)} collective-permute-done((f32[256,256]{1,0:T(8,128)S(1)}, f32[256,256]{1,0:T(8,128)S(1)}, u32[]{:S(2)}, u32[]{:S(2)}) %collective-permute-start.25) | collective-permute-done | bytes 262176 | tf_op jit(solution)/shard_map/ppermute | solution.py:181
  102.0 3.1 %collective-permute-done.23.refs_0_ = f32[256,128]{1,0:T(8,128)S(1)} collective-permute-done((f32[256,128]{1,0:T(8,128)S(1)}, f32[256,128]{1,0:T(8,128)S(1)}, u32[]{:S(2)}, u32[]{:S(2)}) %collective-permute-start.23) | collective-permute-done | bytes 131104 | tf_op jit(solution)/shard_map/ppermute | solution.py:181
  105.2 3.5 %collective-permute-start.27 = (f32[256,128]{1,0:T(8,128)S(1)}, f32[256,128]{1,0:T(8,128)S(1)}, u32[]{:S(2)}, u32[]{:S(2)}) collective-permute-start(f32[256,128]{1,0:T(8,128)S(1)} %get-tuple-element.126), channel_id=1, source_target_pairs={{0,16},{8,24},{16,0},{24,8},{1,17},{9,25},{17,1},{25,9},{2,18},{10... | collective-permute-start | bytes 393224 | tf_op jit(solution)/shard_map/ppermute | solution.py:181
  108.7 2.5 %collective-permute-done.26.refs_0_ = f32[256,128]{1,0:T(8,128)S(1)} collective-permute-done((f32[256,128]{1,0:T(8,128)S(1)}, f32[256,128]{1,0:T(8,128)S(1)}, u32[]{:S(2)}, u32[]{:S(2)}) %collective-permute-start.26) | collective-permute-done | bytes 131104 | tf_op jit(solution)/shard_map/ppermute | solution.py:181
  111.3 2.7 %collective-permute-done.27.refs_0_ = f32[256,128]{1,0:T(8,128)S(1)} collective-permute-done((f32[256,128]{1,0:T(8,128)S(1)}, f32[256,128]{1,0:T(8,128)S(1)}, u32[]{:S(2)}, u32[]{:S(2)}) %collective-permute-start.27) | collective-permute-done | bytes 131104 | tf_op jit(solution)/shard_map/ppermute | solution.py:181
  114.3 1.1 collective-permute-done.28
  115.5 3.6 %collective-permute-done.29 = f32[256]{0:T(256)S(1)} collective-permute-done((f32[256]{0:T(256)S(1)}, f32[256]{0:T(256)S(1)}, u32[]{:S(2)}, u32[]{:S(2)}) %collective-permute-start.29) | collective-permute-done | bytes 1056 | tf_op jit(solution)/shard_map/ppermute | solution.py:181
  119.0 0.9 collective-permute-start.30
  119.9 3.6 %collective-permute-done.30 = f32[256]{0:T(256)S(1)} collective-permute-done((f32[256]{0:T(256)S(1)}, f32[256]{0:T(256)S(1)}, u32[]{:S(2)}, u32[]{:S(2)}) %collective-permute-start.30) | collective-permute-done | bytes 1056 | tf_op jit(solution)/shard_map/ppermute | solution.py:181
  123.5 1.0 broadcast_divide_fusion
  (67 shorter events, 6.7 us)
Async XLA Ops:
  3.3 15.5 %collective-permute-start.5 = (f32[256,512]{1,0:T(8,128)}, f32[256,512]{1,0:T(8,128)S(1)}, u32[]{:S(2)}, u32[]{:S(2)}) collective-permute-start(f32[256,512]{1,0:T(8,128)} %get-tuple-element.77.block), channel_id=1, source_target_pairs={{0,4},{1,3},{2,6},{3,1},{4,0},{5,7},{6,2},{7,5},{8,12},{9,11},{10,... | collective-permute-start | bytes 1572872 | tf_op jit(solution)/shard_map/ppermute | solution.py:216
  6.3 9.8 %collective-permute-start = (f32[256,256]{1,0:T(8,128)}, f32[256,256]{1,0:T(8,128)S(1)}, u32[]{:S(2)}, u32[]{:S(2)}) collective-permute-start(f32[256,256]{1,0:T(8,128)} %get-tuple-element.69), channel_id=1, source_target_pairs={{0,2},{1,5},{2,0},{3,7},{4,1},{5,6},{6,3},{7,4},{8,10},{9,13},{10,... | collective-permute-start | bytes 786440 | tf_op jit(solution)/shard_map/ppermute | solution.py:216
  7.8 10.6 %collective-permute-start.1 = (f32[256,256]{1,0:T(8,128)}, f32[256,256]{1,0:T(8,128)S(1)}, u32[]{:S(2)}, u32[]{:S(2)}) collective-permute-start(f32[256,256]{1,0:T(8,128)} %get-tuple-element.70), channel_id=1, source_target_pairs={{1,5},{3,7},{4,1},{5,4},{6,3},{7,6},{9,13},{11,15},{12,9},{13,12},... | collective-permute-start | bytes 786440 | tf_op jit(solution)/shard_map/ppermute | solution.py:216
  8.4 9.9 %collective-permute-start.2 = (f32[256,256]{1,0:T(8,128)}, f32[256,256]{1,0:T(8,128)S(1)}, u32[]{:S(2)}, u32[]{:S(2)}) collective-permute-start(f32[256,256]{1,0:T(8,128)} %get-tuple-element.71), channel_id=1, source_target_pairs={{0,1},{1,2},{2,3},{3,0},{4,6},{6,4},{8,9},{9,10},{10,11},{11,8},{1... | collective-permute-start | bytes 786440 | tf_op jit(solution)/shard_map/ppermute | solution.py:216
  11.9 6.5 %collective-permute-start.3 = (f32[256,256]{1,0:T(8,128)}, f32[256,256]{1,0:T(8,128)S(1)}, u32[]{:S(2)}, u32[]{:S(2)}) collective-permute-start(f32[256,256]{1,0:T(8,128)} %get-tuple-element.72), channel_id=1, source_target_pairs={{0,1},{1,0},{2,3},{3,2},{8,9},{9,8},{10,11},{11,10},{16,17},{17,16... | collective-permute-start | bytes 786440 | tf_op jit(solution)/shard_map/ppermute | solution.py:216
  13.9 4.5 %copy-start.1 = (f32[256,512]{1,0:T(8,128)S(1)}, f32[256,512]{1,0:T(8,128)}, u32[]{:S(2)}) copy-start(f32[256,512]{1,0:T(8,128)} %get-tuple-element.68.left.token) | copy-start | bytes 1572868
  13.9 5.0 %copy-start = (f32[1,256,3072]{2,1,0:T(8,128)S(1)}, f32[1,256,3072]{2,1,0:T(8,128)}, u32[]{:S(2)}) copy-start(f32[1,256,3072]{2,1,0:T(8,128)} %param.6) | copy-start | bytes 9437188
  13.9 5.0 %copy-start.3 = (f32[256,512]{1,0:T(8,128)S(1)}, f32[256,512]{1,0:T(8,128)}, u32[]{:S(2)}) copy-start(f32[256,512]{1,0:T(8,128)} %get-tuple-element.77.block) | copy-start | bytes 1572868
  13.9 4.9 %copy-start.6 = (s32[1,12]{1,0:T(1,128)S(1)}, s32[1,12]{1,0:T(1,128)}, u32[]{:S(2)}) copy-start(s32[1,12]{1,0:T(1,128)} %col_blocks.11) | copy-start | bytes 148
  16.0 11.1 %collective-permute-start.4 = (f32[256,512]{1,0:T(8,128)}, f32[256,512]{1,0:T(8,128)S(1)}, u32[]{:S(2)}, u32[]{:S(2)}) collective-permute-start(f32[256,512]{1,0:T(8,128)} %shard_map.57.block), channel_id=1, source_target_pairs={{0,4},{1,3},{2,6},{3,1},{4,0},{5,7},{6,2},{7,5},{8,12},{9,11},{10,... | collective-permute-start | bytes 1572872 | tf_op jit(solution)/shard_map/ppermute | solution.py:216
  18.8 8.3 %copy-start.2 = (f32[256,512]{1,0:T(8,128)S(1)}, f32[256,512]{1,0:T(8,128)}, u32[]{:S(2)}) copy-start(f32[256,512]{1,0:T(8,128)} %shard_map.57.block) | copy-start | bytes 1572868
  20.5 15.6 %collective-permute-start.7 = (f32[256,512]{1,0:T(8,128)S(1)}, f32[256,512]{1,0:T(8,128)S(1)}, u32[]{:S(2)}, u32[]{:S(2)}) collective-permute-start(f32[256,512]{1,0:T(8,128)S(1)} %get-tuple-element.81), channel_id=1, source_target_pairs={{0,2},{1,5},{2,0},{3,7},{4,6},{5,1},{6,4},{7,3},{8,10},{9,13},{10,... | collective-permute-start | bytes 1572872 | tf_op jit(solution)/shard_map/ppermute | solution.py:216
  22.9 15.5 %collective-permute-start.9 = (f32[256,512]{1,0:T(8,128)S(1)}, f32[256,512]{1,0:T(8,128)S(1)}, u32[]{:S(2)}, u32[]{:S(2)}) collective-permute-start(f32[256,512]{1,0:T(8,128)S(1)} %get-tuple-element.84.block), channel_id=1, source_target_pairs={{0,4},{1,3},{2,6},{3,1},{4,0},{5,7},{6,2},{7,5},{8,12},{9,11},{10,... | collective-permute-start | bytes 1572872 | tf_op jit(solution)/shard_map/ppermute | solution.py:216
  28.8 18.5 %collective-permute-start.6 = (f32[256,512]{1,0:T(8,128)S(1)}, f32[256,512]{1,0:T(8,128)S(1)}, u32[]{:S(2)}, u32[]{:S(2)}) collective-permute-start(f32[256,512]{1,0:T(8,128)S(1)} %get-tuple-element.79), channel_id=1, source_target_pairs={{0,2},{1,5},{2,0},{3,7},{4,6},{5,1},{6,4},{7,3},{8,10},{9,13},{10,... | collective-permute-start | bytes 1572872 | tf_op jit(solution)/shard_map/ppermute | solution.py:216
  33.6 16.0 %collective-permute-start.11 = (f32[256,512]{1,0:T(8,128)S(1)}, f32[256,512]{1,0:T(8,128)S(1)}, u32[]{:S(2)}, u32[]{:S(2)}) collective-permute-start(f32[256,512]{1,0:T(8,128)S(1)} %get-tuple-element.89.block), channel_id=1, source_target_pairs={{0,4},{1,3},{2,6},{3,1},{4,0},{5,7},{6,2},{7,5},{8,12},{9,11},{10,... | collective-permute-start | bytes 1572872 | tf_op jit(solution)/shard_map/ppermute | solution.py:216
  36.1 11.2 %collective-permute-start.8 = (f32[256,256]{1,0:T(8,128)S(1)}, f32[256,256]{1,0:T(8,128)S(1)}, u32[]{:S(2)}, u32[]{:S(2)}) collective-permute-start(f32[256,256]{1,0:T(8,128)S(1)} %get-tuple-element.82), channel_id=1, source_target_pairs={{0,8},{8,0},{16,24},{24,16},{1,9},{9,1},{17,25},{25,17},{2,10},{10... | collective-permute-start | bytes 786440 | tf_op jit(solution)/shard_map/ppermute | solution.py:181
  40.0 18.8 %collective-permute-start.13 = (f32[256,512]{1,0:T(8,128)S(1)}, f32[256,512]{1,0:T(8,128)S(1)}, u32[]{:S(2)}, u32[]{:S(2)}) collective-permute-start(f32[256,512]{1,0:T(8,128)S(1)} %get-tuple-element.93), channel_id=1, source_target_pairs={{0,2},{1,5},{2,0},{3,7},{4,6},{5,1},{6,4},{7,3},{8,10},{9,13},{10,... | collective-permute-start | bytes 1572872 | tf_op jit(solution)/shard_map/ppermute | solution.py:216
  44.8 20.9 %collective-permute-start.16 = (f32[256,512]{1,0:T(8,128)S(1)}, f32[256,512]{1,0:T(8,128)}, u32[]{:S(2)}, u32[]{:S(2)}) collective-permute-start(f32[256,512]{1,0:T(8,128)S(1)} %get-tuple-element.97.block), channel_id=1, source_target_pairs={{0,4},{1,3},{2,6},{3,1},{4,0},{5,7},{6,2},{7,5},{8,12},{9,11},{10,... | collective-permute-start | bytes 1572872 | tf_op jit(solution)/shard_map/ppermute | solution.py:216
  47.4 0.7 copy-start.9
  48.0 3.6 %copy-start.4 = (f32[256,128]{1,0:T(8,128)}, f32[256,128]{1,0:T(8,128)S(1)}, u32[]{:S(2)}) copy-start(f32[256,128]{1,0:T(8,128)S(1)} %get-tuple-element.87.refs_1_) | copy-start | bytes 393220
  48.0 10.8 %collective-permute-start.14 = (f32[256,256]{1,0:T(8,128)S(1)}, f32[256,256]{1,0:T(8,128)S(1)}, u32[]{:S(2)}, u32[]{:S(2)}) collective-permute-start(f32[256,256]{1,0:T(8,128)S(1)} %get-tuple-element.94), channel_id=1, source_target_pairs={{0,8},{8,0},{16,24},{24,16},{1,9},{9,1},{17,25},{25,17},{2,10},{10... | collective-permute-start | bytes 786440 | tf_op jit(solution)/shard_map/ppermute | solution.py:181
  51.6 19.4 %collective-permute-start.12 = (f32[256,512]{1,0:T(8,128)}, f32[256,512]{1,0:T(8,128)}, u32[]{:S(2)}, u32[]{:S(2)}) collective-permute-start(f32[256,512]{1,0:T(8,128)} %get-tuple-element.91), channel_id=1, source_target_pairs={{0,2},{1,5},{2,0},{3,7},{4,6},{5,1},{6,4},{7,3},{8,10},{9,13},{10,... | collective-permute-start | bytes 1572872 | tf_op jit(solution)/shard_map/ppermute | solution.py:216
  56.3 16.1 %collective-permute-start.19 = (f32[256,512]{1,0:T(8,128)S(1)}, f32[256,512]{1,0:T(8,128)S(1)}, u32[]{:S(2)}, u32[]{:S(2)}) collective-permute-start(f32[256,512]{1,0:T(8,128)S(1)} %get-tuple-element.104.block), channel_id=1, source_target_pairs={{0,4},{1,3},{2,6},{3,1},{4,0},{5,7},{6,2},{7,5},{8,12},{9,11},{10,... | collective-permute-start | bytes 1572872 | tf_op jit(solution)/shard_map/ppermute | solution.py:216
  59.6 0.7 copy-start.7
  60.3 10.7 %collective-permute-start.15 = (f32[256,256]{1,0:T(8,128)}, f32[256,256]{1,0:T(8,128)}, u32[]{:S(2)}, u32[]{:S(2)}) collective-permute-start(f32[256,256]{1,0:T(8,128)} %get-tuple-element.95), channel_id=1, source_target_pairs={{0,8},{8,0},{16,24},{24,16},{1,9},{9,1},{17,25},{25,17},{2,10},{10... | collective-permute-start | bytes 786440 | tf_op jit(solution)/shard_map/ppermute | solution.py:181
  61.8 9.2 %copy-start.5 = (f32[256,128]{1,0:T(8,128)S(1)}, f32[256,128]{1,0:T(8,128)}, u32[]{:S(2)}) copy-start(f32[256,128]{1,0:T(8,128)} %copy-done.4) | copy-start | bytes 393220
  61.8 8.3 %collective-permute-start.10 = (f32[256,128]{1,0:T(8,128)}, f32[256,128]{1,0:T(8,128)S(1)}, u32[]{:S(2)}, u32[]{:S(2)}) collective-permute-start(f32[256,128]{1,0:T(8,128)} %copy-done.9), channel_id=1, source_target_pairs={{0,16},{8,24},{16,0},{24,8},{1,17},{9,25},{17,1},{25,9},{2,18},{10... | collective-permute-start | bytes 393224 | tf_op jit(solution)/shard_map/ppermute | solution.py:181
  65.7 14.3 %copy-start.8 = (f32[256,128]{1,0:T(8,128)S(1)}, f32[256,128]{1,0:T(8,128)}, u32[]{:S(2)}) copy-start(f32[256,128]{1,0:T(8,128)} %copy-done.7) | copy-start | bytes 393220
  67.8 21.8 %collective-permute-start.18 = (f32[256,512]{1,0:T(8,128)S(1)}, f32[256,512]{1,0:T(8,128)S(1)}, u32[]{:S(2)}, u32[]{:S(2)}) collective-permute-start(f32[256,512]{1,0:T(8,128)S(1)} %get-tuple-element.103), channel_id=1, source_target_pairs={{0,2},{1,5},{2,0},{3,7},{4,6},{5,1},{6,4},{7,3},{8,10},{9,13},{10,... | collective-permute-start | bytes 1572872 | tf_op jit(solution)/shard_map/ppermute | solution.py:216
  74.0 18.4 %collective-permute-start.21 = (f32[256,512]{1,0:T(8,128)S(1)}, f32[256,512]{1,0:T(8,128)S(1)}, u32[]{:S(2)}, u32[]{:S(2)}) collective-permute-start(f32[256,512]{1,0:T(8,128)S(1)} %get-tuple-element.110), channel_id=1, source_target_pairs={{0,2},{1,5},{2,0},{3,7},{4,6},{5,1},{6,4},{7,3},{8,10},{9,13},{10,... | collective-permute-start | bytes 1572872 | tf_op jit(solution)/shard_map/ppermute | solution.py:216
  78.3 13.2 %collective-permute-start.22 = (f32[256,256]{1,0:T(8,128)S(1)}, f32[256,256]{1,0:T(8,128)S(1)}, u32[]{:S(2)}, u32[]{:S(2)}) collective-permute-start(f32[256,256]{1,0:T(8,128)S(1)} %get-tuple-element.111), channel_id=1, source_target_pairs={{0,8},{8,0},{16,24},{24,16},{1,9},{9,1},{17,25},{25,17},{2,10},{10... | collective-permute-start | bytes 786440 | tf_op jit(solution)/shard_map/ppermute | solution.py:181
  80.0 9.6 %collective-permute-start.17 = (f32[256,128]{1,0:T(8,128)S(1)}, f32[256,128]{1,0:T(8,128)S(1)}, u32[]{:S(2)}, u32[]{:S(2)}) collective-permute-start(f32[256,128]{1,0:T(8,128)S(1)} %copy-done.8), channel_id=1, source_target_pairs={{0,16},{8,24},{16,0},{24,8},{1,17},{9,25},{17,1},{25,9},{2,18},{10... | collective-permute-start | bytes 393224 | tf_op jit(solution)/shard_map/ppermute | solution.py:181
  82.6 9.8 %collective-permute-start.20 = (f32[256,128]{1,0:T(8,128)S(1)}, f32[256,128]{1,0:T(8,128)S(1)}, u32[]{:S(2)}, u32[]{:S(2)}) collective-permute-start(f32[256,128]{1,0:T(8,128)S(1)} %get-tuple-element.107), channel_id=1, source_target_pairs={{0,16},{8,24},{16,0},{24,8},{1,17},{9,25},{17,1},{25,9},{2,18},{10... | collective-permute-start | bytes 393224 | tf_op jit(solution)/shard_map/ppermute | solution.py:181
  89.7 11.8 %collective-permute-start.25 = (f32[256,256]{1,0:T(8,128)S(1)}, f32[256,256]{1,0:T(8,128)S(1)}, u32[]{:S(2)}, u32[]{:S(2)}) collective-permute-start(f32[256,256]{1,0:T(8,128)S(1)} %get-tuple-element.119), channel_id=1, source_target_pairs={{0,8},{8,0},{16,24},{24,16},{1,9},{9,1},{17,25},{25,17},{2,10},{10... | collective-permute-start | bytes 786440 | tf_op jit(solution)/shard_map/ppermute | solution.py:181
  92.5 12.6 %collective-permute-start.24 = (f32[256,256]{1,0:T(8,128)S(1)}, f32[256,256]{1,0:T(8,128)S(1)}, u32[]{:S(2)}, u32[]{:S(2)}) collective-permute-start(f32[256,256]{1,0:T(8,128)S(1)} %get-tuple-element.117), channel_id=1, source_target_pairs={{0,8},{8,0},{16,24},{24,16},{1,9},{9,1},{17,25},{25,17},{2,10},{10... | collective-permute-start | bytes 786440 | tf_op jit(solution)/shard_map/ppermute | solution.py:181
  94.3 10.8 %collective-permute-start.23 = (f32[256,128]{1,0:T(8,128)S(1)}, f32[256,128]{1,0:T(8,128)S(1)}, u32[]{:S(2)}, u32[]{:S(2)}) collective-permute-start(f32[256,128]{1,0:T(8,128)S(1)} %get-tuple-element.115), channel_id=1, source_target_pairs={{0,16},{8,24},{16,0},{24,8},{1,17},{9,25},{17,1},{25,9},{2,18},{10... | collective-permute-start | bytes 393224 | tf_op jit(solution)/shard_map/ppermute | solution.py:181
  101.6 9.6 %collective-permute-start.26 = (f32[256,128]{1,0:T(8,128)S(1)}, f32[256,128]{1,0:T(8,128)S(1)}, u32[]{:S(2)}, u32[]{:S(2)}) collective-permute-start(f32[256,128]{1,0:T(8,128)S(1)} %get-tuple-element.123), channel_id=1, source_target_pairs={{0,16},{8,24},{16,0},{24,8},{1,17},{9,25},{17,1},{25,9},{2,18},{10... | collective-permute-start | bytes 393224 | tf_op jit(solution)/shard_map/ppermute | solution.py:181
  105.2 8.8 %collective-permute-start.27 = (f32[256,128]{1,0:T(8,128)S(1)}, f32[256,128]{1,0:T(8,128)S(1)}, u32[]{:S(2)}, u32[]{:S(2)}) collective-permute-start(f32[256,128]{1,0:T(8,128)S(1)} %get-tuple-element.126), channel_id=1, source_target_pairs={{0,16},{8,24},{16,0},{24,8},{1,17},{9,25},{17,1},{25,9},{2,18},{10... | collective-permute-start | bytes 393224 | tf_op jit(solution)/shard_map/ppermute | solution.py:181
  114.2 1.2 collective-permute-start.28
  115.4 3.6 %collective-permute-start.29 = (f32[256]{0:T(256)S(1)}, f32[256]{0:T(256)S(1)}, u32[]{:S(2)}, u32[]{:S(2)}) collective-permute-start(f32[256]{0:T(256)S(1)} %max.9), channel_id=1, source_target_pairs={{0,8},{8,0},{16,24},{24,16},{1,9},{9,1},{17,25},{25,17},{2,10},{10... | collective-permute-start | bytes 3080 | tf_op jit(solution)/shard_map/ppermute | solution.py:181
  119.0 4.5 %collective-permute-start.30 = (f32[256]{0:T(256)S(1)}, f32[256]{0:T(256)S(1)}, u32[]{:S(2)}, u32[]{:S(2)}) collective-permute-start(f32[256]{0:T(256)S(1)} %max.10), channel_id=1, source_target_pairs={{0,16},{8,24},{16,0},{24,8},{1,17},{9,25},{17,1},{25,9},{2,18},{10... | collective-permute-start | bytes 3080 | tf_op jit(solution)/shard_map/ppermute | solution.py:181

commit v3 on v2

--- a/solution.py
+++ b/solution.py
@@ -186,7 +186,8 @@
 
 
 STEPS = (
-    "A0", "A1", "o0", "A2", "o1t0", "A3", "o2t1", "A4", "f0o3t2", "A5", "f1o4", "t3", "f2o5", "t4", "f3t5", "f4", "f5",
+    "A0", "A1", "o0", "o1t0", "A2", "A3", "o2t1", "A4", "f0", "o3t2", "A5", "f1o4", "f2o5", "t3", "t4", "f3t5", "f5",
+    "f4",
 )
 GATHERS = ((0,), (1,), (2,), (3,), (4,), (5,))
 TIES = (None, None, 0, 1, 2, 3)
@@ -255,7 +256,7 @@
     share = lax.dynamic_slice_in_dim(after(ancestor, halves[0]), leaf * share_cols, share_cols, 1)
     x_got, kept, z1, z1_kept, z2, z2_kept, upds = ({} for _ in range(7))
     peak = jnp.zeros((height, LANES), F32)
-    token = lower
+    token = a_token = lower
     for word in STEPS:
         if word[0] == "A":
             t = int(word[1:])
@@ -274,12 +275,13 @@
             members = [chunks[i] for k in later for i in GATHERS[k]]
             res = run(
                 functools.partial(multiply_body, height, (ranges, begin, 4 * wide, members)),
-                [(SMEM, col_blocks)] + [(VMEM, h) for h in halves] + [(VMEM, blocks[g]), (VMEM, gots[g]), (ANY, token)]
+                [(SMEM, col_blocks)] + [(VMEM, h) for h in halves] + [(VMEM, blocks[g]), (VMEM, gots[g]), (ANY, a_token)]
                 + [spec for k in later for spec in tiles_of(GATHERS[k])],
                 [shape(height, 4 * wide)] * 2 + [shape(depth, widths(GATHERS[k])) for k in later],
                 flops=48 * height * depth * wide,
             )
-            kept[t] = token = res[1]
+            kept[t] = a_token = res[1]
+            token = res[1]
             for k in later:
                 blocks[k] = res[2]
                 gots[k] = gather(res[2])
@@ -300,6 +302,7 @@
             outs += new
         res = run(functools.partial(reduce_body, jobs), ins + [(ANY, token)], outs)
         token = res[1]
+        a_token = res[1]
         tops = []
         for k, (step, t) in enumerate(todo):
             a, b = res[2 * k], res[2 * k + 1]

time: 125 us -> 123 us (0.984)
  starting transfers between devices: 65.8 us -> 61.3 us
  waiting for transfers between devices: 35.5 us -> 38.1 us
    ppermute x16, waiting for transfers between devices: 4.36 us -> 19.8 us  [move(): return lax.ppermute(value, ('row', 'col'), pairs)]
    ppermute x15, waiting for transfers between devices: 31.1 us -> 18.2 us  [swap(): return lax.ppermute(value, axis, [(i, i ^ bit) for i in range(size)])]
    ppermute x16, starting transfers between devices: 43.5 us -> 31.5 us  [move(): return lax.ppermute(value, ('row', 'col'), pairs)]
    ppermute x15, starting transfers between devices: 22.3 us -> 29.8 us  [swap(): return lax.ppermute(value, axis, [(i, i ^ bit) for i in range(size)])]
    pallas_call x20 -> x21, Pallas kernels: 18.5 us -> 18.4 us  [run(): pl.pallas_call(body, grid=(1,), in_specs=[whole(a) if s is VMEM else s fo...]
  transfers between devices with their start and end apart: 31 -> 31, of which waited for: 14 -> 15; matrix products, arithmetic and copies ran while one was open for 1% -> 1% of each run, Pallas kernels for 13% -> 13%
where the time goes in v3:
time: 123 us; the launch traced here: 122 us
  starting transfers between devices  61.3 us (50%)
  waiting for transfers between devices  38.1 us (31%)
  Pallas kernels  18.4 us (15%)
  local copies, waits for them, and re-layouts  2.02 us (2%)
    ppermute x16, starting transfers between devices, move(): return lax.ppermute(value, ('row', 'col'), pairs)  31.5 us
    ppermute x15, starting transfers between devices, swap(): return lax.ppermute(value, axis, [(i, i ^ bit) for i in range(size)])  29.8 us
    ppermute x16, waiting for transfers between devices, move(): return lax.ppermute(value, ('row', 'col'), pairs)  19.8 us
    pallas_call x21, Pallas kernels, run(): pl.pallas_call(body, grid=(1,), in_specs=[whole(a) if s is VMEM else s fo...  18.4 us
    ppermute x15, waiting for transfers between devices, swap(): return lax.ppermute(value, axis, [(i, i ^ bit) for i in range(size)])  18.2 us
  transfers between devices with their start and end apart: 31, of which 15 were waited for; matrix products, arithmetic and copies ran while one was open for 1% of the time, Pallas kernels for 13%

profile of v3, /device:TPU:0, one launch (start us, length us, event | category | flops | bytes accessed | tf_op | source)
XLA Modules:
  0.0 122.0 jit_solution(12484493137782009928)
XLA Ops:
  0.7 2.6 %shard_map.55 = (f32[256,256]{1,0:T(8,128)}, f32[256,256]{1,0:T(8,128)}, f32[256,256]{1,0:T(8,128)}, f32[256,256]{1,0:T(8,128)}, f32[256,512]{1,0:T(8,128)}, /*index=5*/f32[256,512]{1,0:T(8,128)}) custom-call(s32[1,1]{1,0:T(1,128)S(6)} %copy.11.row_blocks, f32[256,512]{1,0:T(8,128)} %bitcast.26, f32[256,3072]{1,0:T(8,128)} %bitcast.2, f32[256,3072]{1,0:T(8,128)} %bitcast.3, ...), custom_call_target="tpu_custom_call" | custom-call | bytes 2621440 | tf_op jit(solution)/shard_map/pallas_call | solution.py:50
  3.3 3.0 %collective-permute-start.5 = (f32[256,512]{1,0:T(8,128)}, f32[256,512]{1,0:T(8,128)S(1)}, u32[]{:S(2)}, u32[]{:S(2)}) collective-permute-start(f32[256,512]{1,0:T(8,128)} %get-tuple-element.77.block), channel_id=1, source_target_pairs={{0,4},{1,3},{2,6},{3,1},{4,0},{5,7},{6,2},{7,5},{8,12},{9,11},{10,... | collective-permute-start | bytes 1572872 | tf_op jit(solution)/shard_map/ppermute | solution.py:217
  6.3 1.5 %collective-permute-start = (f32[256,256]{1,0:T(8,128)}, f32[256,256]{1,0:T(8,128)S(1)}, u32[]{:S(2)}, u32[]{:S(2)}) collective-permute-start(f32[256,256]{1,0:T(8,128)} %get-tuple-element.69), channel_id=1, source_target_pairs={{0,2},{1,5},{2,0},{3,7},{4,1},{5,6},{6,3},{7,4},{8,10},{9,13},{10,... | collective-permute-start | bytes 786440 | tf_op jit(solution)/shard_map/ppermute | solution.py:217
  8.4 3.5 %collective-permute-start.2 = (f32[256,256]{1,0:T(8,128)}, f32[256,256]{1,0:T(8,128)S(1)}, u32[]{:S(2)}, u32[]{:S(2)}) collective-permute-start(f32[256,256]{1,0:T(8,128)} %get-tuple-element.71), channel_id=1, source_target_pairs={{0,1},{1,2},{2,3},{3,0},{4,6},{6,4},{8,9},{9,10},{10,11},{11,8},{1... | collective-permute-start | bytes 786440 | tf_op jit(solution)/shard_map/ppermute | solution.py:217
  11.9 1.9 %collective-permute-start.3 = (f32[256,256]{1,0:T(8,128)}, f32[256,256]{1,0:T(8,128)S(1)}, u32[]{:S(2)}, u32[]{:S(2)}) collective-permute-start(f32[256,256]{1,0:T(8,128)} %get-tuple-element.72), channel_id=1, source_target_pairs={{0,1},{1,0},{2,3},{3,2},{8,9},{9,8},{10,11},{11,10},{16,17},{17,16... | collective-permute-start | bytes 786440 | tf_op jit(solution)/shard_map/ppermute | solution.py:217
  13.9 2.1 %shard_map.57.block = f32[256,512]{1,0:T(8,128)} custom-call(f32[256,512]{1,0:T(8,128)} %get-tuple-element.68.left.token, f32[256,3072]{1,0:T(8,128)} %bitcast.6, f32[256,3072]{1,0:T(8,128)} %bitcast.7, f32[256,3072]{1,0:T(8,128)} %bitcast.8, f32[256,3072]{1,0:T(8,128)} %bitcast.9), custom_call_target="tpu_custom_call" | custom-call | bytes 524288 | tf_op jit(solution)/shard_map/pallas_call | solution.py:50
  16.0 2.3 %collective-permute-start.4 = (f32[256,512]{1,0:T(8,128)}, f32[256,512]{1,0:T(8,128)S(1)}, u32[]{:S(2)}, u32[]{:S(2)}) collective-permute-start(f32[256,512]{1,0:T(8,128)} %shard_map.57.block), channel_id=1, source_target_pairs={{0,4},{1,3},{2,6},{3,1},{4,0},{5,7},{6,2},{7,5},{8,12},{9,11},{10,... | collective-permute-start | bytes 1572872 | tf_op jit(solution)/shard_map/ppermute | solution.py:217
  18.8 1.6 %shard_map.58 = (f32[256,512]{1,0:T(8,128)S(1)}, f32[256,512]{1,0:T(8,128)S(1)}, f32[256,512]{1,0:T(8,128)S(1)}) custom-call(s32[1,12]{1,0:T(1,128)S(1)} %copy-done.6, bf16[512,256]{1,0:T(8,128)(2,1)S(1)} %get-tuple-element.73.ah, bf16[512,256]{1,0:T(8,128)(2,1)S(1)} %get-tuple-element.74.al, bf16[512,256]{1,0:T(8,128)(2,1)S(1)} %get-tuple-element.75.bh, ...), custom_call_target="tpu_custom_call" | custom-call | flops 402653184 | bytes 4718592 | tf_op jit(solution)/shard_map/pallas_call | solution.py:50
  20.4 2.4 %collective-permute-start.7 = (f32[256,512]{1,0:T(8,128)S(1)}, f32[256,512]{1,0:T(8,128)S(1)}, u32[]{:S(2)}, u32[]{:S(2)}) collective-permute-start(f32[256,512]{1,0:T(8,128)S(1)} %get-tuple-element.81), channel_id=1, source_target_pairs={{0,2},{1,5},{2,0},{3,7},{4,6},{5,1},{6,4},{7,3},{8,10},{9,13},{10,... | collective-permute-start | bytes 1572872 | tf_op jit(solution)/shard_map/ppermute | solution.py:217
  22.9 4.3 %collective-permute-done.4.got = f32[256,512]{1,0:T(8,128)S(1)} collective-permute-done((f32[256,512]{1,0:T(8,128)}, f32[256,512]{1,0:T(8,128)S(1)}, u32[]{:S(2)}, u32[]{:S(2)}) %collective-permute-start.4) | collective-permute-done | bytes 524320 | tf_op jit(solution)/shard_map/ppermute | solution.py:217
  27.2 1.6 %shard_map.59 = (f32[256,512]{1,0:T(8,128)S(1)}, f32[256,512]{1,0:T(8,128)S(1)}, f32[256,512]{1,0:T(8,128)S(1)}) custom-call(s32[1,12]{1,0:T(1,128)S(1)} %copy-done.6, bf16[512,256]{1,0:T(8,128)(2,1)S(1)} %get-tuple-element.73.ah, bf16[512,256]{1,0:T(8,128)(2,1)S(1)} %get-tuple-element.74.al, bf16[512,256]{1,0:T(8,128)(2,1)S(1)} %get-tuple-element.75.bh, ...), custom_call_target="tpu_custom_call" | custom-call | flops 402653184 | bytes 4718592 | tf_op jit(solution)/shard_map/pallas_call | solution.py:50
  28.8 4.9 %collective-permute-start.6 = (f32[256,512]{1,0:T(8,128)S(1)}, f32[256,512]{1,0:T(8,128)S(1)}, u32[]{:S(2)}, u32[]{:S(2)}) collective-permute-start(f32[256,512]{1,0:T(8,128)S(1)} %get-tuple-element.79), channel_id=1, source_target_pairs={{0,2},{1,5},{2,0},{3,7},{4,6},{5,1},{6,4},{7,3},{8,10},{9,13},{10,... | collective-permute-start | bytes 1572872 | tf_op jit(solution)/shard_map/ppermute | solution.py:217
  33.6 2.4 %collective-permute-start.10 = (f32[256,512]{1,0:T(8,128)S(1)}, f32[256,512]{1,0:T(8,128)S(1)}, u32[]{:S(2)}, u32[]{:S(2)}) collective-permute-start(f32[256,512]{1,0:T(8,128)S(1)} %get-tuple-element.87.block), channel_id=1, source_target_pairs={{0,4},{1,3},{2,6},{3,1},{4,0},{5,7},{6,2},{7,5},{8,12},{9,11},{10,... | collective-permute-start | bytes 1572872 | tf_op jit(solution)/shard_map/ppermute | solution.py:217
  36.1 1.6 %collective-permute-start.8 = (f32[256,256]{1,0:T(8,128)S(1)}, f32[256,256]{1,0:T(8,128)S(1)}, u32[]{:S(2)}, u32[]{:S(2)}) collective-permute-start(f32[256,256]{1,0:T(8,128)S(1)} %get-tuple-element.82), channel_id=1, source_target_pairs={{0,8},{8,0},{16,24},{24,16},{1,9},{9,1},{17,25},{25,17},{2,10},{10... | collective-permute-start | bytes 786440 | tf_op jit(solution)/shard_map/ppermute | solution.py:181
  37.7 8.8 %collective-permute-done.6.refs_0_ = f32[256,512]{1,0:T(8,128)S(1)} collective-permute-done((f32[256,512]{1,0:T(8,128)S(1)}, f32[256,512]{1,0:T(8,128)S(1)}, u32[]{:S(2)}, u32[]{:S(2)}) %collective-permute-start.6) | collective-permute-done | bytes 524320 | tf_op jit(solution)/shard_map/ppermute | solution.py:217
  46.6 1.6 %shard_map.62 = (f32[256,512]{1,0:T(8,128)S(1)}, f32[256,512]{1,0:T(8,128)S(1)}, f32[256,512]{1,0:T(8,128)S(1)}) custom-call(s32[1,12]{1,0:T(1,128)S(1)} %copy-done.6, bf16[512,256]{1,0:T(8,128)(2,1)S(1)} %get-tuple-element.73.ah, bf16[512,256]{1,0:T(8,128)(2,1)S(1)} %get-tuple-element.74.al, bf16[512,256]{1,0:T(8,128)(2,1)S(1)} %get-tuple-element.75.bh, ...), custom_call_target="tpu_custom_call" | custom-call | flops 402653184 | bytes 4718592 | tf_op jit(solution)/shard_map/pallas_call | solution.py:50
  48.3 2.1 %collective-permute-start.12 = (f32[256,512]{1,0:T(8,128)S(1)}, f32[256,512]{1,0:T(8,128)S(1)}, u32[]{:S(2)}, u32[]{:S(2)}) collective-permute-start(f32[256,512]{1,0:T(8,128)S(1)} %get-tuple-element.90), channel_id=1, source_target_pairs={{0,2},{1,5},{2,0},{3,7},{4,6},{5,1},{6,4},{7,3},{8,10},{9,13},{10,... | collective-permute-start | bytes 1572872 | tf_op jit(solution)/shard_map/ppermute | solution.py:217
  50.3 2.2 %collective-permute-start.11 = (f32[256,512]{1,0:T(8,128)S(1)}, f32[256,512]{1,0:T(8,128)}, u32[]{:S(2)}, u32[]{:S(2)}) collective-permute-start(f32[256,512]{1,0:T(8,128)S(1)} %get-tuple-element.89.block), channel_id=1, source_target_pairs={{0,4},{1,3},{2,6},{3,1},{4,0},{5,7},{6,2},{7,5},{8,12},{9,11},{10,... | collective-permute-start | bytes 1572872 | tf_op jit(solution)/shard_map/ppermute | solution.py:217
  52.6 1.7 %collective-permute-start.13 = (f32[256,256]{1,0:T(8,128)S(1)}, f32[256,256]{1,0:T(8,128)S(1)}, u32[]{:S(2)}, u32[]{:S(2)}) collective-permute-start(f32[256,256]{1,0:T(8,128)S(1)} %get-tuple-element.92), channel_id=1, source_target_pairs={{0,8},{8,0},{16,24},{24,16},{1,9},{9,1},{17,25},{25,17},{2,10},{10... | collective-permute-start | bytes 786440 | tf_op jit(solution)/shard_map/ppermute | solution.py:181
  54.3 1.1 collective-permute-done.14.got
  55.4 2.0 %shard_map.63 = (f32[256,512]{1,0:T(8,128)}, f32[256,512]{1,0:T(8,128)S(1)}, f32[256,512]{1,0:T(8,128)S(1)}) custom-call(s32[1,12]{1,0:T(1,128)S(1)} %copy-done.6, bf16[512,256]{1,0:T(8,128)(2,1)S(1)} %get-tuple-element.73.ah, bf16[512,256]{1,0:T(8,128)(2,1)S(1)} %get-tuple-element.74.al, bf16[512,256]{1,0:T(8,128)(2,1)S(1)} %get-tuple-element.75.bh, ...), custom_call_target="tpu_custom_call" | custom-call | flops 402653184 | bytes 4718592 | tf_op jit(solution)/shard_map/pallas_call | solution.py:50
  57.4 2.5 %collective-permute-start.17 = (f32[256,512]{1,0:T(8,128)S(1)}, f32[256,512]{1,0:T(8,128)S(1)}, u32[]{:S(2)}, u32[]{:S(2)}) collective-permute-start(f32[256,512]{1,0:T(8,128)S(1)} %get-tuple-element.102.block), channel_id=1, source_target_pairs={{0,4},{1,3},{2,6},{3,1},{4,0},{5,7},{6,2},{7,5},{8,12},{9,11},{10,... | collective-permute-start | bytes 1572872 | tf_op jit(solution)/shard_map/ppermute | solution.py:217
  59.8 3.3 %collective-permute-done.12.refs_0_ = f32[256,512]{1,0:T(8,128)S(1)} collective-permute-done((f32[256,512]{1,0:T(8,128)S(1)}, f32[256,512]{1,0:T(8,128)S(1)}, u32[]{:S(2)}, u32[]{:S(2)}) %collective-permute-start.12) | collective-permute-done | bytes 524320 | tf_op jit(solution)/shard_map/ppermute | solution.py:217
  64.6 1.6 %collective-permute-start.19 = (f32[256,256]{1,0:T(8,128)}, f32[256,256]{1,0:T(8,128)}, u32[]{:S(2)}, u32[]{:S(2)}) collective-permute-start(f32[256,256]{1,0:T(8,128)} %get-tuple-element.104), channel_id=1, source_target_pairs={{0,8},{8,0},{16,24},{24,16},{1,9},{9,1},{17,25},{25,17},{2,10},{10... | collective-permute-start | bytes 786440 | tf_op jit(solution)/shard_map/ppermute | solution.py:181
  66.2 2.6 %collective-permute-start.9 = (f32[256,128]{1,0:T(8,128)}, f32[256,128]{1,0:T(8,128)S(1)}, u32[]{:S(2)}, u32[]{:S(2)}) collective-permute-start(f32[256,128]{1,0:T(8,128)} %copy-done.9), channel_id=1, source_target_pairs={{0,16},{8,24},{16,0},{24,8},{1,17},{9,25},{17,1},{25,9},{2,18},{10... | collective-permute-start | bytes 393224 | tf_op jit(solution)/shard_map/ppermute | solution.py:181
  68.8 1.3 %constant_dynamic-slice_fusion.5 = (f32[256,128]{1,0:T(8,128)S(1)}, f32[256,128]{1,0:T(8,128)S(1)}, f32[256,128]{1,0:T(8,128)S(1)}, f32[256,128]{1,0:T(8,128)S(1...) fusion(f32[256,3072]{1,0:T(8,128)} %param.9, s32[]{:T(128)S(6)} %add.17, s32[]{:T(128)S(6)} %add.16, s32[]{:T(128)S(6)} %add.15, ...), kind=kLoop, calls=%fused_computation.12 | loop fusion | bytes 1572888 | tf_op jit(solution)/shard_map/slice | solution.py:299
  70.1 2.1 %shard_map.65 = (f32[256,512]{1,0:T(8,128)S(1)}, f32[256,512]{1,0:T(8,128)S(1)}) custom-call(s32[1,12]{1,0:T(1,128)S(1)} %copy-done.6, bf16[512,256]{1,0:T(8,128)(2,1)S(1)} %get-tuple-element.73.ah, bf16[512,256]{1,0:T(8,128)(2,1)S(1)} %get-tuple-element.74.al, bf16[512,256]{1,0:T(8,128)(2,1)S(1)} %get-tuple-element.75.bh, ...), custom_call_target="tpu_custom_call" | custom-call | flops 402653184 | bytes 4194304 | tf_op jit(solution)/shard_map/pallas_call | solution.py:50
  72.2 2.1 %collective-permute-start.16 = (f32[256,512]{1,0:T(8,128)S(1)}, f32[256,512]{1,0:T(8,128)S(1)}, u32[]{:S(2)}, u32[]{:S(2)}) collective-permute-start(f32[256,512]{1,0:T(8,128)S(1)} %get-tuple-element.101), channel_id=1, source_target_pairs={{0,2},{1,5},{2,0},{3,7},{4,6},{5,1},{6,4},{7,3},{8,10},{9,13},{10,... | collective-permute-start | bytes 1572872 | tf_op jit(solution)/shard_map/ppermute | solution.py:217
  74.4 1.2 %shard_map.67 = (f32[256,256]{1,0:T(8,128)S(1)}, f32[256,256]{1,0:T(8,128)S(1)}, f32[256,128]{1,0:T(8,128)S(1)}, f32[256,128]{1,0:T(8,128)S(1)}) custom-call(f32[256,512]{1,0:T(8,128)} %collective-permute-done.18.refs_0_, f32[256,512]{1,0:T(8,128)S(1)} %get-tuple-element.94.refs_4_.refs_1_, f32[256,256]{1,0:T(8,128)} %collective-permute-done.19.refs_2_, ...), custom_call_target="tpu_custom_call" | custom-call | bytes 2359296 | tf_op jit(solution)/shard_map/pallas_call | solution.py:50
  75.6 2.2 %collective-permute-done.17.got = f32[256,512]{1,0:T(8,128)S(1)} collective-permute-done((f32[256,512]{1,0:T(8,128)S(1)}, f32[256,512]{1,0:T(8,128)S(1)}, u32[]{:S(2)}, u32[]{:S(2)}) %collective-permute-start.17) | collective-permute-done | bytes 524320 | tf_op jit(solution)/shard_map/ppermute | solution.py:217
  77.8 1.5 %shard_map.68 = (f32[256,512]{1,0:T(8,128)S(1)}, f32[256,512]{1,0:T(8,128)S(1)}) custom-call(s32[1,12]{1,0:T(1,128)S(1)} %copy-done.6, bf16[512,256]{1,0:T(8,128)(2,1)S(1)} %get-tuple-element.73.ah, bf16[512,256]{1,0:T(8,128)(2,1)S(1)} %get-tuple-element.74.al, bf16[512,256]{1,0:T(8,128)(2,1)S(1)} %get-tuple-element.75.bh, ...), custom_call_target="tpu_custom_call" | custom-call | flops 402653184 | bytes 4194304 | tf_op jit(solution)/shard_map/pallas_call | solution.py:50
  79.5 2.7 %collective-permute-start.15 = (f32[256,128]{1,0:T(8,128)S(1)}, f32[256,128]{1,0:T(8,128)S(1)}, u32[]{:S(2)}, u32[]{:S(2)}) collective-permute-start(f32[256,128]{1,0:T(8,128)S(1)} %copy-done.8), channel_id=1, source_target_pairs={{0,16},{8,24},{16,0},{24,8},{1,17},{9,25},{17,1},{25,9},{2,18},{10... | collective-permute-start | bytes 393224 | tf_op jit(solution)/shard_map/ppermute | solution.py:181
  82.5 1.6 %collective-permute-start.22 = (f32[256,256]{1,0:T(8,128)S(1)}, f32[256,256]{1,0:T(8,128)S(1)}, u32[]{:S(2)}, u32[]{:S(2)}) collective-permute-start(f32[256,256]{1,0:T(8,128)S(1)} %get-tuple-element.113), channel_id=1, source_target_pairs={{0,8},{8,0},{16,24},{24,16},{1,9},{9,1},{17,25},{25,17},{2,10},{10... | collective-permute-start | bytes 786440 | tf_op jit(solution)/shard_map/ppermute | solution.py:181
  84.0 2.9 %collective-permute-done.15.refs_0_ = f32[256,128]{1,0:T(8,128)S(1)} collective-permute-done((f32[256,128]{1,0:T(8,128)S(1)}, f32[256,128]{1,0:T(8,128)S(1)}, u32[]{:S(2)}, u32[]{:S(2)}) %collective-permute-start.15) | collective-permute-done | bytes 131104 | tf_op jit(solution)/shard_map/ppermute | solution.py:181
  87.1 2.4 %collective-permute-start.25 = (f32[256,256]{1,0:T(8,128)S(1)}, f32[256,256]{1,0:T(8,128)S(1)}, u32[]{:S(2)}, u32[]{:S(2)}) collective-permute-start(f32[256,256]{1,0:T(8,128)S(1)} %get-tuple-element.119), channel_id=1, source_target_pairs={{0,8},{8,0},{16,24},{24,16},{1,9},{9,1},{17,25},{25,17},{2,10},{10... | collective-permute-start | bytes 786440 | tf_op jit(solution)/shard_map/ppermute | solution.py:181
  90.5 2.7 %collective-permute-start.24 = (f32[256,256]{1,0:T(8,128)S(1)}, f32[256,256]{1,0:T(8,128)S(1)}, u32[]{:S(2)}, u32[]{:S(2)}) collective-permute-start(f32[256,256]{1,0:T(8,128)S(1)} %get-tuple-element.117), channel_id=1, source_target_pairs={{0,8},{8,0},{16,24},{24,16},{1,9},{9,1},{17,25},{25,17},{2,10},{10... | collective-permute-start | bytes 786440 | tf_op jit(solution)/shard_map/ppermute | solution.py:181
  93.2 2.0 %collective-permute-done.22.refs_0_ = f32[256,256]{1,0:T(8,128)S(1)} collective-permute-done((f32[256,256]{1,0:T(8,128)S(1)}, f32[256,256]{1,0:T(8,128)S(1)}, u32[]{:S(2)}, u32[]{:S(2)}) %collective-permute-start.22) | collective-permute-done | bytes 262176 | tf_op jit(solution)/shard_map/ppermute | solution.py:181
  95.3 2.7 %collective-permute-start.23 = (f32[256,128]{1,0:T(8,128)S(1)}, f32[256,128]{1,0:T(8,128)S(1)}, u32[]{:S(2)}, u32[]{:S(2)}) collective-permute-start(f32[256,128]{1,0:T(8,128)S(1)} %get-tuple-element.115), channel_id=1, source_target_pairs={{0,16},{8,24},{16,0},{24,8},{1,17},{9,25},{17,1},{25,9},{2,18},{10... | collective-permute-start | bytes 393224 | tf_op jit(solution)/shard_map/ppermute | solution.py:181
  98.1 2.7 %collective-permute-start.26 = (f32[256,128]{1,0:T(8,128)S(1)}, f32[256,128]{1,0:T(8,128)S(1)}, u32[]{:S(2)}, u32[]{:S(2)}) collective-permute-start(f32[256,128]{1,0:T(8,128)S(1)} %get-tuple-element.123), channel_id=1, source_target_pairs={{0,16},{8,24},{16,0},{24,8},{1,17},{9,25},{17,1},{25,9},{2,18},{10... | collective-permute-start | bytes 393224 | tf_op jit(solution)/shard_map/ppermute | solution.py:181
  100.8 2.1 %collective-permute-done.23.refs_0_ = f32[256,128]{1,0:T(8,128)S(1)} collective-permute-done((f32[256,128]{1,0:T(8,128)S(1)}, f32[256,128]{1,0:T(8,128)S(1)}, u32[]{:S(2)}, u32[]{:S(2)}) %collective-permute-start.23) | collective-permute-done | bytes 131104 | tf_op jit(solution)/shard_map/ppermute | solution.py:181
  102.9 1.8 %collective-permute-done.24.refs_4_ = f32[256,256]{1,0:T(8,128)S(1)} collective-permute-done((f32[256,256]{1,0:T(8,128)S(1)}, f32[256,256]{1,0:T(8,128)S(1)}, u32[]{:S(2)}, u32[]{:S(2)}) %collective-permute-start.24) | collective-permute-done | bytes 262176 | tf_op jit(solution)/shard_map/ppermute | solution.py:181
  104.9 1.7 %collective-permute-start.27 = (f32[256,128]{1,0:T(8,128)S(1)}, f32[256,128]{1,0:T(8,128)S(1)}, u32[]{:S(2)}, u32[]{:S(2)}) collective-permute-start(f32[256,128]{1,0:T(8,128)S(1)} %get-tuple-element.124), channel_id=1, source_target_pairs={{0,16},{8,24},{16,0},{24,8},{1,17},{9,25},{17,1},{25,9},{2,18},{10... | collective-permute-start | bytes 393224 | tf_op jit(solution)/shard_map/ppermute | solution.py:181
  106.6 4.2 %collective-permute-done.27.refs_0_ = f32[256,128]{1,0:T(8,128)S(1)} collective-permute-done((f32[256,128]{1,0:T(8,128)S(1)}, f32[256,128]{1,0:T(8,128)S(1)}, u32[]{:S(2)}, u32[]{:S(2)}) %collective-permute-start.27) | collective-permute-done | bytes 131104 | tf_op jit(solution)/shard_map/ppermute | solution.py:181
  111.3 1.1 collective-permute-done.28
  112.4 2.6 %collective-permute-start.29 = (f32[256]{0:T(256)S(1)}, f32[256]{0:T(256)S(1)}, u32[]{:S(2)}, u32[]{:S(2)}) collective-permute-start(f32[256]{0:T(256)S(1)} %max.9), channel_id=1, source_target_pairs={{0,8},{8,0},{16,24},{24,16},{1,9},{9,1},{17,25},{25,17},{2,10},{10... | collective-permute-start | bytes 3080 | tf_op jit(solution)/shard_map/ppermute | solution.py:181
  115.0 1.5 %collective-permute-done.29 = f32[256]{0:T(256)S(1)} collective-permute-done((f32[256]{0:T(256)S(1)}, f32[256]{0:T(256)S(1)}, u32[]{:S(2)}, u32[]{:S(2)}) %collective-permute-start.29) | collective-permute-done | bytes 1056 | tf_op jit(solution)/shard_map/ppermute | solution.py:181
  116.5 2.9 %collective-permute-start.30 = (f32[256]{0:T(256)S(1)}, f32[256]{0:T(256)S(1)}, u32[]{:S(2)}, u32[]{:S(2)}) collective-permute-start(f32[256]{0:T(256)S(1)} %max.10), channel_id=1, source_target_pairs={{0,16},{8,24},{16,0},{24,8},{1,17},{9,25},{17,1},{25,9},{2,18},{10... | collective-permute-start | bytes 3080 | tf_op jit(solution)/shard_map/ppermute | solution.py:181
  119.4 1.5 %collective-permute-done.30 = f32[256]{0:T(256)S(1)} collective-permute-done((f32[256]{0:T(256)S(1)}, f32[256]{0:T(256)S(1)}, u32[]{:S(2)}, u32[]{:S(2)}) %collective-permute-start.30) | collective-permute-done | bytes 1056 | tf_op jit(solution)/shard_map/ppermute | solution.py:181
  (68 shorter events, 6.2 us)
Async XLA Ops:
  3.3 15.5 %collective-permute-start.5 = (f32[256,512]{1,0:T(8,128)}, f32[256,512]{1,0:T(8,128)S(1)}, u32[]{:S(2)}, u32[]{:S(2)}) collective-permute-start(f32[256,512]{1,0:T(8,128)} %get-tuple-element.77.block), channel_id=1, source_target_pairs={{0,4},{1,3},{2,6},{3,1},{4,0},{5,7},{6,2},{7,5},{8,12},{9,11},{10,... | collective-permute-start | bytes 1572872 | tf_op jit(solution)/shard_map/ppermute | solution.py:217
  6.3 9.7 %collective-permute-start = (f32[256,256]{1,0:T(8,128)}, f32[256,256]{1,0:T(8,128)S(1)}, u32[]{:S(2)}, u32[]{:S(2)}) collective-permute-start(f32[256,256]{1,0:T(8,128)} %get-tuple-element.69), channel_id=1, source_target_pairs={{0,2},{1,5},{2,0},{3,7},{4,1},{5,6},{6,3},{7,4},{8,10},{9,13},{10,... | collective-permute-start | bytes 786440 | tf_op jit(solution)/shard_map/ppermute | solution.py:217
  7.7 10.6 %collective-permute-start.1 = (f32[256,256]{1,0:T(8,128)}, f32[256,256]{1,0:T(8,128)S(1)}, u32[]{:S(2)}, u32[]{:S(2)}) collective-permute-start(f32[256,256]{1,0:T(8,128)} %get-tuple-element.70), channel_id=1, source_target_pairs={{1,5},{3,7},{4,1},{5,4},{6,3},{7,6},{9,13},{11,15},{12,9},{13,12},... | collective-permute-start | bytes 786440 | tf_op jit(solution)/shard_map/ppermute | solution.py:217
  8.4 9.9 %collective-permute-start.2 = (f32[256,256]{1,0:T(8,128)}, f32[256,256]{1,0:T(8,128)S(1)}, u32[]{:S(2)}, u32[]{:S(2)}) collective-permute-start(f32[256,256]{1,0:T(8,128)} %get-tuple-element.71), channel_id=1, source_target_pairs={{0,1},{1,2},{2,3},{3,0},{4,6},{6,4},{8,9},{9,10},{10,11},{11,8},{1... | collective-permute-start | bytes 786440 | tf_op jit(solution)/shard_map/ppermute | solution.py:217
  11.9 6.5 %collective-permute-start.3 = (f32[256,256]{1,0:T(8,128)}, f32[256,256]{1,0:T(8,128)S(1)}, u32[]{:S(2)}, u32[]{:S(2)}) collective-permute-start(f32[256,256]{1,0:T(8,128)} %get-tuple-element.72), channel_id=1, source_target_pairs={{0,1},{1,0},{2,3},{3,2},{8,9},{9,8},{10,11},{11,10},{16,17},{17,16... | collective-permute-start | bytes 786440 | tf_op jit(solution)/shard_map/ppermute | solution.py:217
  13.8 4.5 %copy-start.1 = (f32[256,512]{1,0:T(8,128)S(1)}, f32[256,512]{1,0:T(8,128)}, u32[]{:S(2)}) copy-start(f32[256,512]{1,0:T(8,128)} %get-tuple-element.68.left.token) | copy-start | bytes 1572868
  13.8 5.0 %copy-start = (f32[1,256,3072]{2,1,0:T(8,128)S(1)}, f32[1,256,3072]{2,1,0:T(8,128)}, u32[]{:S(2)}) copy-start(f32[1,256,3072]{2,1,0:T(8,128)} %param.6) | copy-start | bytes 9437188
  13.9 5.0 %copy-start.3 = (f32[256,512]{1,0:T(8,128)S(1)}, f32[256,512]{1,0:T(8,128)}, u32[]{:S(2)}) copy-start(f32[256,512]{1,0:T(8,128)} %get-tuple-element.77.block) | copy-start | bytes 1572868
  13.9 4.9 %copy-start.6 = (s32[1,12]{1,0:T(1,128)S(1)}, s32[1,12]{1,0:T(1,128)}, u32[]{:S(2)}) copy-start(s32[1,12]{1,0:T(1,128)} %col_blocks.11) | copy-start | bytes 148
  16.0 11.1 %collective-permute-start.4 = (f32[256,512]{1,0:T(8,128)}, f32[256,512]{1,0:T(8,128)S(1)}, u32[]{:S(2)}, u32[]{:S(2)}) collective-permute-start(f32[256,512]{1,0:T(8,128)} %shard_map.57.block), channel_id=1, source_target_pairs={{0,4},{1,3},{2,6},{3,1},{4,0},{5,7},{6,2},{7,5},{8,12},{9,11},{10,... | collective-permute-start | bytes 1572872 | tf_op jit(solution)/shard_map/ppermute | solution.py:217
  18.8 8.3 %copy-start.2 = (f32[256,512]{1,0:T(8,128)S(1)}, f32[256,512]{1,0:T(8,128)}, u32[]{:S(2)}) copy-start(f32[256,512]{1,0:T(8,128)} %shard_map.57.block) | copy-start | bytes 1572868
  20.4 15.6 %collective-permute-start.7 = (f32[256,512]{1,0:T(8,128)S(1)}, f32[256,512]{1,0:T(8,128)S(1)}, u32[]{:S(2)}, u32[]{:S(2)}) collective-permute-start(f32[256,512]{1,0:T(8,128)S(1)} %get-tuple-element.81), channel_id=1, source_target_pairs={{0,2},{1,5},{2,0},{3,7},{4,6},{5,1},{6,4},{7,3},{8,10},{9,13},{10,... | collective-permute-start | bytes 1572872 | tf_op jit(solution)/shard_map/ppermute | solution.py:217
  28.8 17.7 %collective-permute-start.6 = (f32[256,512]{1,0:T(8,128)S(1)}, f32[256,512]{1,0:T(8,128)S(1)}, u32[]{:S(2)}, u32[]{:S(2)}) collective-permute-start(f32[256,512]{1,0:T(8,128)S(1)} %get-tuple-element.79), channel_id=1, source_target_pairs={{0,2},{1,5},{2,0},{3,7},{4,6},{5,1},{6,4},{7,3},{8,10},{9,13},{10,... | collective-permute-start | bytes 1572872 | tf_op jit(solution)/shard_map/ppermute | solution.py:217
  33.6 13.0 %collective-permute-start.10 = (f32[256,512]{1,0:T(8,128)S(1)}, f32[256,512]{1,0:T(8,128)S(1)}, u32[]{:S(2)}, u32[]{:S(2)}) collective-permute-start(f32[256,512]{1,0:T(8,128)S(1)} %get-tuple-element.87.block), channel_id=1, source_target_pairs={{0,4},{1,3},{2,6},{3,1},{4,0},{5,7},{6,2},{7,5},{8,12},{9,11},{10,... | collective-permute-start | bytes 1572872 | tf_op jit(solution)/shard_map/ppermute | solution.py:217
  36.1 10.4 %collective-permute-start.8 = (f32[256,256]{1,0:T(8,128)S(1)}, f32[256,256]{1,0:T(8,128)S(1)}, u32[]{:S(2)}, u32[]{:S(2)}) collective-permute-start(f32[256,256]{1,0:T(8,128)S(1)} %get-tuple-element.82), channel_id=1, source_target_pairs={{0,8},{8,0},{16,24},{24,16},{1,9},{9,1},{17,25},{25,17},{2,10},{10... | collective-permute-start | bytes 786440 | tf_op jit(solution)/shard_map/ppermute | solution.py:181
  37.7 17.6 %collective-permute-start.14 = (f32[256,512]{1,0:T(8,128)S(1)}, f32[256,512]{1,0:T(8,128)S(1)}, u32[]{:S(2)}, u32[]{:S(2)}) collective-permute-start(f32[256,512]{1,0:T(8,128)S(1)} %get-tuple-element.93.block), channel_id=1, source_target_pairs={{0,4},{1,3},{2,6},{3,1},{4,0},{5,7},{6,2},{7,5},{8,12},{9,11},{10,... | collective-permute-start | bytes 1572872 | tf_op jit(solution)/shard_map/ppermute | solution.py:217
  46.6 1.6 %copy-start.4 = (f32[256,128]{1,0:T(8,128)}, f32[256,128]{1,0:T(8,128)S(1)}, u32[]{:S(2)}) copy-start(f32[256,128]{1,0:T(8,128)S(1)} %get-tuple-element.85.refs_1_) | copy-start | bytes 393220
  46.6 1.6 %copy-start.9 = (f32[256,128]{1,0:T(8,128)}, f32[256,128]{1,0:T(8,128)S(1)}, u32[]{:S(2)}) copy-start(f32[256,128]{1,0:T(8,128)S(1)} %get-tuple-element.84) | copy-start | bytes 393220
  48.3 14.9 %collective-permute-start.12 = (f32[256,512]{1,0:T(8,128)S(1)}, f32[256,512]{1,0:T(8,128)S(1)}, u32[]{:S(2)}, u32[]{:S(2)}) collective-permute-start(f32[256,512]{1,0:T(8,128)S(1)} %get-tuple-element.90), channel_id=1, source_target_pairs={{0,2},{1,5},{2,0},{3,7},{4,6},{5,1},{6,4},{7,3},{8,10},{9,13},{10,... | collective-permute-start | bytes 1572872 | tf_op jit(solution)/shard_map/ppermute | solution.py:217
  50.3 19.7 %collective-permute-start.11 = (f32[256,512]{1,0:T(8,128)S(1)}, f32[256,512]{1,0:T(8,128)}, u32[]{:S(2)}, u32[]{:S(2)}) collective-permute-start(f32[256,512]{1,0:T(8,128)S(1)} %get-tuple-element.89.block), channel_id=1, source_target_pairs={{0,4},{1,3},{2,6},{3,1},{4,0},{5,7},{6,2},{7,5},{8,12},{9,11},{10,... | collective-permute-start | bytes 1572872 | tf_op jit(solution)/shard_map/ppermute | solution.py:217
  52.6 7.3 %collective-permute-start.13 = (f32[256,256]{1,0:T(8,128)S(1)}, f32[256,256]{1,0:T(8,128)S(1)}, u32[]{:S(2)}, u32[]{:S(2)}) collective-permute-start(f32[256,256]{1,0:T(8,128)S(1)} %get-tuple-element.92), channel_id=1, source_target_pairs={{0,8},{8,0},{16,24},{24,16},{1,9},{9,1},{17,25},{25,17},{2,10},{10... | collective-permute-start | bytes 786440 | tf_op jit(solution)/shard_map/ppermute | solution.py:181
  57.4 17.0 %collective-permute-start.18 = (f32[256,512]{1,0:T(8,128)}, f32[256,512]{1,0:T(8,128)}, u32[]{:S(2)}, u32[]{:S(2)}) collective-permute-start(f32[256,512]{1,0:T(8,128)} %get-tuple-element.103), channel_id=1, source_target_pairs={{0,2},{1,5},{2,0},{3,7},{4,6},{5,1},{6,4},{7,3},{8,10},{9,13},{10,... | collective-permute-start | bytes 1572872 | tf_op jit(solution)/shard_map/ppermute | solution.py:217
  57.4 20.5 %collective-permute-start.17 = (f32[256,512]{1,0:T(8,128)S(1)}, f32[256,512]{1,0:T(8,128)S(1)}, u32[]{:S(2)}, u32[]{:S(2)}) collective-permute-start(f32[256,512]{1,0:T(8,128)S(1)} %get-tuple-element.102.block), channel_id=1, source_target_pairs={{0,4},{1,3},{2,6},{3,1},{4,0},{5,7},{6,2},{7,5},{8,12},{9,11},{10,... | collective-permute-start | bytes 1572872 | tf_op jit(solution)/shard_map/ppermute | solution.py:217
  64.0 0.6 copy-start.7
  64.6 9.8 %collective-permute-start.19 = (f32[256,256]{1,0:T(8,128)}, f32[256,256]{1,0:T(8,128)}, u32[]{:S(2)}, u32[]{:S(2)}) collective-permute-start(f32[256,256]{1,0:T(8,128)} %get-tuple-element.104), channel_id=1, source_target_pairs={{0,8},{8,0},{16,24},{24,16},{1,9},{9,1},{17,25},{25,17},{2,10},{10... | collective-permute-start | bytes 786440 | tf_op jit(solution)/shard_map/ppermute | solution.py:181
  66.2 8.1 %copy-start.5 = (f32[256,128]{1,0:T(8,128)S(1)}, f32[256,128]{1,0:T(8,128)}, u32[]{:S(2)}) copy-start(f32[256,128]{1,0:T(8,128)} %copy-done.4) | copy-start | bytes 393220
  66.2 8.0 %collective-permute-start.9 = (f32[256,128]{1,0:T(8,128)}, f32[256,128]{1,0:T(8,128)S(1)}, u32[]{:S(2)}, u32[]{:S(2)}) collective-permute-start(f32[256,128]{1,0:T(8,128)} %copy-done.9), channel_id=1, source_target_pairs={{0,16},{8,24},{16,0},{24,8},{1,17},{9,25},{17,1},{25,9},{2,18},{10... | collective-permute-start | bytes 393224 | tf_op jit(solution)/shard_map/ppermute | solution.py:181
  72.1 7.3 %copy-start.8 = (f32[256,128]{1,0:T(8,128)S(1)}, f32[256,128]{1,0:T(8,128)}, u32[]{:S(2)}) copy-start(f32[256,128]{1,0:T(8,128)} %copy-done.7) | copy-start | bytes 393220
  72.2 14.8 %collective-permute-start.16 = (f32[256,512]{1,0:T(8,128)S(1)}, f32[256,512]{1,0:T(8,128)S(1)}, u32[]{:S(2)}, u32[]{:S(2)}) collective-permute-start(f32[256,512]{1,0:T(8,128)S(1)} %get-tuple-element.101), channel_id=1, source_target_pairs={{0,2},{1,5},{2,0},{3,7},{4,6},{5,1},{6,4},{7,3},{8,10},{9,13},{10,... | collective-permute-start | bytes 1572872 | tf_op jit(solution)/shard_map/ppermute | solution.py:217
  79.4 11.0 %collective-permute-start.21 = (f32[256,512]{1,0:T(8,128)S(1)}, f32[256,512]{1,0:T(8,128)S(1)}, u32[]{:S(2)}, u32[]{:S(2)}) collective-permute-start(f32[256,512]{1,0:T(8,128)S(1)} %get-tuple-element.111), channel_id=1, source_target_pairs={{0,2},{1,5},{2,0},{3,7},{4,6},{5,1},{6,4},{7,3},{8,10},{9,13},{10,... | collective-permute-start | bytes 1572872 | tf_op jit(solution)/shard_map/ppermute | solution.py:217
  79.5 7.4 %collective-permute-start.15 = (f32[256,128]{1,0:T(8,128)S(1)}, f32[256,128]{1,0:T(8,128)S(1)}, u32[]{:S(2)}, u32[]{:S(2)}) collective-permute-start(f32[256,128]{1,0:T(8,128)S(1)} %copy-done.8), channel_id=1, source_target_pairs={{0,16},{8,24},{16,0},{24,8},{1,17},{9,25},{17,1},{25,9},{2,18},{10... | collective-permute-start | bytes 393224 | tf_op jit(solution)/shard_map/ppermute | solution.py:181
  82.1 8.3 %collective-permute-start.20 = (f32[256,128]{1,0:T(8,128)S(1)}, f32[256,128]{1,0:T(8,128)S(1)}, u32[]{:S(2)}, u32[]{:S(2)}) collective-permute-start(f32[256,128]{1,0:T(8,128)S(1)} %get-tuple-element.108), channel_id=1, source_target_pairs={{0,16},{8,24},{16,0},{24,8},{1,17},{9,25},{17,1},{25,9},{2,18},{10... | collective-permute-start | bytes 393224 | tf_op jit(solution)/shard_map/ppermute | solution.py:181
  82.5 12.8 %collective-permute-start.22 = (f32[256,256]{1,0:T(8,128)S(1)}, f32[256,256]{1,0:T(8,128)S(1)}, u32[]{:S(2)}, u32[]{:S(2)}) collective-permute-start(f32[256,256]{1,0:T(8,128)S(1)} %get-tuple-element.113), channel_id=1, source_target_pairs={{0,8},{8,0},{16,24},{24,16},{1,9},{9,1},{17,25},{25,17},{2,10},{10... | collective-permute-start | bytes 786440 | tf_op jit(solution)/shard_map/ppermute | solution.py:181
  87.1 11.0 %collective-permute-start.25 = (f32[256,256]{1,0:T(8,128)S(1)}, f32[256,256]{1,0:T(8,128)S(1)}, u32[]{:S(2)}, u32[]{:S(2)}) collective-permute-start(f32[256,256]{1,0:T(8,128)S(1)} %get-tuple-element.119), channel_id=1, source_target_pairs={{0,8},{8,0},{16,24},{24,16},{1,9},{9,1},{17,25},{25,17},{2,10},{10... | collective-permute-start | bytes 786440 | tf_op jit(solution)/shard_map/ppermute | solution.py:181
  90.5 14.2 %collective-permute-start.24 = (f32[256,256]{1,0:T(8,128)S(1)}, f32[256,256]{1,0:T(8,128)S(1)}, u32[]{:S(2)}, u32[]{:S(2)}) collective-permute-start(f32[256,256]{1,0:T(8,128)S(1)} %get-tuple-element.117), channel_id=1, source_target_pairs={{0,8},{8,0},{16,24},{24,16},{1,9},{9,1},{17,25},{25,17},{2,10},{10... | collective-permute-start | bytes 786440 | tf_op jit(solution)/shard_map/ppermute | solution.py:181
  95.3 7.6 %collective-permute-start.23 = (f32[256,128]{1,0:T(8,128)S(1)}, f32[256,128]{1,0:T(8,128)S(1)}, u32[]{:S(2)}, u32[]{:S(2)}) collective-permute-start(f32[256,128]{1,0:T(8,128)S(1)} %get-tuple-element.115), channel_id=1, source_target_pairs={{0,16},{8,24},{16,0},{24,8},{1,17},{9,25},{17,1},{25,9},{2,18},{10... | collective-permute-start | bytes 393224 | tf_op jit(solution)/shard_map/ppermute | solution.py:181
  98.1 12.8 %collective-permute-start.26 = (f32[256,128]{1,0:T(8,128)S(1)}, f32[256,128]{1,0:T(8,128)S(1)}, u32[]{:S(2)}, u32[]{:S(2)}) collective-permute-start(f32[256,128]{1,0:T(8,128)S(1)} %get-tuple-element.123), channel_id=1, source_target_pairs={{0,16},{8,24},{16,0},{24,8},{1,17},{9,25},{17,1},{25,9},{2,18},{10... | collective-permute-start | bytes 393224 | tf_op jit(solution)/shard_map/ppermute | solution.py:181
  104.9 5.9 %collective-permute-start.27 = (f32[256,128]{1,0:T(8,128)S(1)}, f32[256,128]{1,0:T(8,128)S(1)}, u32[]{:S(2)}, u32[]{:S(2)}) collective-permute-start(f32[256,128]{1,0:T(8,128)S(1)} %get-tuple-element.124), channel_id=1, source_target_pairs={{0,16},{8,24},{16,0},{24,8},{1,17},{9,25},{17,1},{25,9},{2,18},{10... | collective-permute-start | bytes 393224 | tf_op jit(solution)/shard_map/ppermute | solution.py:181
  111.2 1.2 collective-permute-start.28
  112.4 4.1 %collective-permute-start.29 = (f32[256]{0:T(256)S(1)}, f32[256]{0:T(256)S(1)}, u32[]{:S(2)}, u32[]{:S(2)}) collective-permute-start(f32[256]{0:T(256)S(1)} %max.9), channel_id=1, source_target_pairs={{0,8},{8,0},{16,24},{24,16},{1,9},{9,1},{17,25},{25,17},{2,10},{10... | collective-permute-start | bytes 3080 | tf_op jit(solution)/shard_map/ppermute | solution.py:181
  116.5 4.5 %collective-permute-start.30 = (f32[256]{0:T(256)S(1)}, f32[256]{0:T(256)S(1)}, u32[]{:S(2)}, u32[]{:S(2)}) collective-permute-start(f32[256]{0:T(256)S(1)} %max.10), channel_id=1, source_target_pairs={{0,16},{8,24},{16,0},{24,8},{1,17},{9,25},{17,1},{25,9},{2,18},{10... | collective-permute-start | bytes 3080 | tf_op jit(solution)/shard_map/ppermute | solution.py:181

commit v4 on v3

--- a/solution.py
+++ b/solution.py
@@ -163,17 +163,26 @@
         mine, ins = ins[:count], ins[count:]
         send, keep, outs = outs[0], outs[1], outs[2:]
         if step == "f":
-            got, kept, share, peak = mine
-            value = share[...] - (kept[...] + got[...])
-            send[...] = value
-            top = jnp.max(jnp.abs(value), axis=1, keepdims=True)
+            got, *kept, share, peak = mine
+            at, top = 0, None
+            for piece in kept:
+                lanes = pl.ds(at, piece.shape[1])
+                value = share[:, lanes] - (piece[...] + got[:, lanes])
+                send[:, lanes] = value
+                high = jnp.max(jnp.abs(value), axis=1, keepdims=True)
+                top = high if top is None else jnp.maximum(top, high)
+                at += piece.shape[1]
             keep[...] = jnp.maximum(peak[...], jnp.broadcast_to(top, keep.shape))
             continue
         bit = (leaf % 2 if step == "o" else leaf // 2) == 1
         half = 2 * wide if step == "o" else wide
         total = mine[0][...] + mine[1][...]
         a, b = total[:, :half], total[:, half:]
-        send[...] = jnp.where(bit, a, b)
+        at = 0
+        for earlier in mine[2:]:
+            send[:, pl.ds(at, earlier.shape[1])] = earlier[...]
+            at += earlier.shape[1]
+        send[:, pl.ds(at, half)] = jnp.where(bit, a, b)
         keep[...] = jnp.where(bit, b, a)
 
 
@@ -186,12 +195,12 @@
 
 
 STEPS = (
-    "A0", "A1", "o0", "o1t0", "A2", "A3", "o2t1", "A4", "f0", "o3t2", "A5", "f1o4", "f2o5", "t3", "t4", "f3t5", "f5",
-    "f4",
+    "A0", "A1", "o0", "A2", "o1t0", "A3", "o2t1", "A4", "o3t2", "f1", "A5", "o4t3", "o5t4", "f3", "t5", "f4", "f5",
 )
 GATHERS = ((0,), (1,), (2,), (3,), (4,), (5,))
 TIES = (None, None, 0, 1, 2, 3)
 FIRST = 56
+GROUPS = ((0, 1), (2, 3), (4,), (5,))
 
 
 def chunked(left, upper, row_blocks, col_blocks, ancestor):
@@ -254,6 +263,7 @@
     halves = run(panel_body, [(VMEM, lower)] + [(VMEM, v) for v in landed], [shape(2 * height, depth, dtype=BF16)] * 4)
 
     share = lax.dynamic_slice_in_dim(after(ancestor, halves[0]), leaf * share_cols, share_cols, 1)
+    waiting = {}
     x_got, kept, z1, z1_kept, z2, z2_kept, upds = ({} for _ in range(7))
     peak = jnp.zeros((height, LANES), F32)
     token = a_token = lower
@@ -294,9 +304,15 @@
             if step == "o":
                 mine, new = [x_got[t], kept[t]], [shape(height, 2 * wide)] * 2
             elif step == "t":
-                mine, new = [z1[t], z1_kept[t]], [shape(height, wide)] * 2
+                group = [g for g in GROUPS if t in g][0]
+                before = [waiting[i] for i in group[:-1]] if t == group[-1] else []
+                mine = [z1[t], z1_kept[t]] + before
+                new = [shape(height, wide + sum(b.shape[1] for b in before)), shape(height, wide)]
             else:
-                mine, new = [z2[t], z2_kept[t], share[:, at:at + wide], peak], [shape(height, wide), shape(height, LANES)]
+                group = [g for g in GROUPS if t in g][0]
+                at, wide = chunks[group[0]][0], sum(chunks[i][1] for i in group)
+                mine = [z2[t]] + [z2_kept[i] for i in group] + [share[:, at:at + wide], peak]
+                new = [shape(height, wide), shape(height, LANES)]
             jobs.append((step, len(mine), wide))
             ins += [(VMEM, v) for v in mine]
             outs += new
@@ -309,14 +325,16 @@
             if step == "o":
                 z1[t], z1_kept[t] = swap(a, "leaf", leaf_count, 1), b
             elif step == "t":
-                z2[t], z2_kept[t] = swap(a, "leaf", leaf_count, 2), b
+                waiting[t], z2_kept[t] = a, b
+                if t in [g[-1] for g in GROUPS]:
+                    z2[t] = swap(a, "leaf", leaf_count, 2)
             else:
                 upds[t] = a
                 tops.append(b)
         if tops:
             peak = functools.reduce(jnp.maximum, tops)
 
-    updated = jnp.concatenate([upds[g] for g in range(n)], 1)
+    updated = jnp.concatenate([upds[g[-1]] for g in GROUPS], 1)
     top = jnp.max(peak, axis=1)
     top = jnp.maximum(top, swap(top, "col", cols, 1))
     for bit in (1, 2):

time: 123 us -> 121 us (0.984)
  starting transfers between devices: 61.3 us -> 57.2 us
  Pallas kernels: 18.4 us -> 20.3 us
    ppermute x15 -> x13, waiting for transfers between devices: 18.2 us -> 33.2 us  [swap(): return lax.ppermute(value, axis, [(i, i ^ bit) for i in range(size)])]
    ppermute x16, waiting for transfers between devices: 19.8 us -> 4.98 us  [move(): return lax.ppermute(value, ('row', 'col'), pairs)]
    ppermute x15 -> x13, starting transfers between devices: 29.8 us -> 16.3 us  [swap(): return lax.ppermute(value, axis, [(i, i ^ bit) for i in range(size)])]
    ppermute x16, starting transfers between devices: 31.5 us -> 40.9 us  [move(): return lax.ppermute(value, ('row', 'col'), pairs)]
    pallas_call x21 -> x20, Pallas kernels: 18.4 us -> 20.3 us  [run(): pl.pallas_call(body, grid=(1,), in_specs=[whole(a) if s is VMEM else s fo...]
  transfers between devices with their start and end apart: 31 -> 29, of which waited for: 15 -> 13; matrix products, arithmetic and copies ran while one was open for 1% -> 2% of each run, Pallas kernels for 13% -> 15%
where the time goes in v4:
time: 121 us; the launch traced here: 120 us
  starting transfers between devices  57.2 us (47%)
  waiting for transfers between devices  38.2 us (32%)
  Pallas kernels  20.3 us (17%)
  local copies, waits for them, and re-layouts  2.13 us (2%)
    ppermute x16, starting transfers between devices, move(): return lax.ppermute(value, ('row', 'col'), pairs)  40.9 us
    ppermute x13, waiting for transfers between devices, swap(): return lax.ppermute(value, axis, [(i, i ^ bit) for i in range(size)])  33.2 us
    pallas_call x20, Pallas kernels, run(): pl.pallas_call(body, grid=(1,), in_specs=[whole(a) if s is VMEM else s fo...  20.3 us
    ppermute x13, starting transfers between devices, swap(): return lax.ppermute(value, axis, [(i, i ^ bit) for i in range(size)])  16.3 us
    ppermute x16, waiting for transfers between devices, move(): return lax.ppermute(value, ('row', 'col'), pairs)  4.98 us
  transfers between devices with their start and end apart: 29, of which 13 were waited for; matrix products, arithmetic and copies ran while one was open for 2% of the time, Pallas kernels for 15%

profile of v4, /device:TPU:0, one launch (start us, length us, event | category | flops | bytes accessed | tf_op | source)
XLA Modules:
  0.0 119.9 jit_solution(11409212434049988572)
XLA Ops:
  0.7 2.7 %shard_map.55 = (f32[256,256]{1,0:T(8,128)}, f32[256,256]{1,0:T(8,128)}, f32[256,256]{1,0:T(8,128)}, f32[256,256]{1,0:T(8,128)}, f32[256,512]{1,0:T(8,128)}, /*index=5*/f32[256,512]{1,0:T(8,128)}) custom-call(s32[1,1]{1,0:T(1,128)S(6)} %copy.6.row_blocks, f32[256,512]{1,0:T(8,128)} %bitcast.26, f32[256,3072]{1,0:T(8,128)} %bitcast.2, f32[256,3072]{1,0:T(8,128)} %bitcast.3, ...), custom_call_target="tpu_custom_call" | custom-call | bytes 2621440 | tf_op jit(solution)/shard_map/pallas_call | solution.py:50
  3.3 3.0 %collective-permute-start.4 = (f32[256,512]{1,0:T(8,128)}, f32[256,512]{1,0:T(8,128)S(1)}, u32[]{:S(2)}, u32[]{:S(2)}) collective-permute-start(f32[256,512]{1,0:T(8,128)} %get-tuple-element.73.block), channel_id=1, source_target_pairs={{0,4},{1,3},{2,6},{3,1},{4,0},{5,7},{6,2},{7,5},{8,12},{9,11},{10,... | collective-permute-start | bytes 1572872 | tf_op jit(solution)/shard_map/ppermute | solution.py:226
  6.3 1.5 %collective-permute-start = (f32[256,256]{1,0:T(8,128)}, f32[256,256]{1,0:T(8,128)S(1)}, u32[]{:S(2)}, u32[]{:S(2)}) collective-permute-start(f32[256,256]{1,0:T(8,128)} %get-tuple-element.65), channel_id=1, source_target_pairs={{0,2},{1,5},{2,0},{3,7},{4,1},{5,6},{6,3},{7,4},{8,10},{9,13},{10,... | collective-permute-start | bytes 786440 | tf_op jit(solution)/shard_map/ppermute | solution.py:226
  8.4 3.5 %collective-permute-start.2 = (f32[256,256]{1,0:T(8,128)}, f32[256,256]{1,0:T(8,128)S(1)}, u32[]{:S(2)}, u32[]{:S(2)}) collective-permute-start(f32[256,256]{1,0:T(8,128)} %get-tuple-element.67), channel_id=1, source_target_pairs={{0,1},{1,2},{2,3},{3,0},{4,6},{6,4},{8,9},{9,10},{10,11},{11,8},{1... | collective-permute-start | bytes 786440 | tf_op jit(solution)/shard_map/ppermute | solution.py:226
  11.9 1.9 %collective-permute-start.3 = (f32[256,256]{1,0:T(8,128)}, f32[256,256]{1,0:T(8,128)S(1)}, u32[]{:S(2)}, u32[]{:S(2)}) collective-permute-start(f32[256,256]{1,0:T(8,128)} %get-tuple-element.68), channel_id=1, source_target_pairs={{0,1},{1,0},{2,3},{3,2},{8,9},{9,8},{10,11},{11,10},{16,17},{17,16... | collective-permute-start | bytes 786440 | tf_op jit(solution)/shard_map/ppermute | solution.py:226
  13.9 2.1 %shard_map.58.block = f32[256,512]{1,0:T(8,128)} custom-call(f32[256,512]{1,0:T(8,128)} %get-tuple-element.64.left.token, f32[256,3072]{1,0:T(8,128)} %bitcast.6, f32[256,3072]{1,0:T(8,128)} %bitcast.7, f32[256,3072]{1,0:T(8,128)} %bitcast.8, f32[256,3072]{1,0:T(8,128)} %bitcast.9), custom_call_target="tpu_custom_call" | custom-call | bytes 524288 | tf_op jit(solution)/shard_map/pallas_call | solution.py:50
  16.0 2.4 %collective-permute-start.7 = (f32[256,512]{1,0:T(8,128)}, f32[256,512]{1,0:T(8,128)S(1)}, u32[]{:S(2)}, u32[]{:S(2)}) collective-permute-start(f32[256,512]{1,0:T(8,128)} %shard_map.58.block), channel_id=1, source_target_pairs={{0,4},{1,3},{2,6},{3,1},{4,0},{5,7},{6,2},{7,5},{8,12},{9,11},{10,... | collective-permute-start | bytes 1572872 | tf_op jit(solution)/shard_map/ppermute | solution.py:226
  18.8 1.6 %shard_map.57 = (f32[256,512]{1,0:T(8,128)S(1)}, f32[256,512]{1,0:T(8,128)S(1)}, f32[256,512]{1,0:T(8,128)S(1)}) custom-call(s32[1,12]{1,0:T(1,128)S(1)} %copy-done.6, bf16[512,256]{1,0:T(8,128)(2,1)S(1)} %get-tuple-element.69.ah, bf16[512,256]{1,0:T(8,128)(2,1)S(1)} %get-tuple-element.70.al, bf16[512,256]{1,0:T(8,128)(2,1)S(1)} %get-tuple-element.71.bh, ...), custom_call_target="tpu_custom_call" | custom-call | flops 402653184 | bytes 4718592 | tf_op jit(solution)/shard_map/pallas_call | solution.py:50
  20.4 2.4 %collective-permute-start.6 = (f32[256,512]{1,0:T(8,128)S(1)}, f32[256,512]{1,0:T(8,128)S(1)}, u32[]{:S(2)}, u32[]{:S(2)}) collective-permute-start(f32[256,512]{1,0:T(8,128)S(1)} %get-tuple-element.75), channel_id=1, source_target_pairs={{0,2},{1,5},{2,0},{3,7},{4,6},{5,1},{6,4},{7,3},{8,10},{9,13},{10,... | collective-permute-start | bytes 1572872 | tf_op jit(solution)/shard_map/ppermute | solution.py:226
  22.9 0.8 collective-permute-start.5
  23.7 3.5 %collective-permute-done.7.got = f32[256,512]{1,0:T(8,128)S(1)} collective-permute-done((f32[256,512]{1,0:T(8,128)}, f32[256,512]{1,0:T(8,128)S(1)}, u32[]{:S(2)}, u32[]{:S(2)}) %collective-permute-start.7) | collective-permute-done | bytes 524320 | tf_op jit(solution)/shard_map/ppermute | solution.py:226
  27.2 1.6 %shard_map.59 = (f32[256,512]{1,0:T(8,128)S(1)}, f32[256,512]{1,0:T(8,128)S(1)}, f32[256,512]{1,0:T(8,128)S(1)}) custom-call(s32[1,12]{1,0:T(1,128)S(1)} %copy-done.6, bf16[512,256]{1,0:T(8,128)(2,1)S(1)} %get-tuple-element.69.ah, bf16[512,256]{1,0:T(8,128)(2,1)S(1)} %get-tuple-element.70.al, bf16[512,256]{1,0:T(8,128)(2,1)S(1)} %get-tuple-element.71.bh, ...), custom_call_target="tpu_custom_call" | custom-call | flops 402653184 | bytes 4718592 | tf_op jit(solution)/shard_map/pallas_call | solution.py:50
  28.8 4.9 %collective-permute-start.9 = (f32[256,512]{1,0:T(8,128)S(1)}, f32[256,512]{1,0:T(8,128)S(1)}, u32[]{:S(2)}, u32[]{:S(2)}) collective-permute-start(f32[256,512]{1,0:T(8,128)S(1)} %get-tuple-element.81), channel_id=1, source_target_pairs={{0,2},{1,5},{2,0},{3,7},{4,6},{5,1},{6,4},{7,3},{8,10},{9,13},{10,... | collective-permute-start | bytes 1572872 | tf_op jit(solution)/shard_map/ppermute | solution.py:226
  33.7 2.4 %collective-permute-start.12 = (f32[256,512]{1,0:T(8,128)S(1)}, f32[256,512]{1,0:T(8,128)S(1)}, u32[]{:S(2)}, u32[]{:S(2)}) collective-permute-start(f32[256,512]{1,0:T(8,128)S(1)} %get-tuple-element.86.block), channel_id=1, source_target_pairs={{0,4},{1,3},{2,6},{3,1},{4,0},{5,7},{6,2},{7,5},{8,12},{9,11},{10,... | collective-permute-start | bytes 1572872 | tf_op jit(solution)/shard_map/ppermute | solution.py:226
  36.1 1.6 %collective-permute-start.10 = (f32[256,256]{1,0:T(8,128)S(1)}, f32[256,256]{1,0:T(8,128)S(1)}, u32[]{:S(2)}, u32[]{:S(2)}) collective-permute-start(f32[256,256]{1,0:T(8,128)S(1)} %get-tuple-element.82), channel_id=1, source_target_pairs={{0,8},{8,0},{16,24},{24,16},{1,9},{9,1},{17,25},{25,17},{2,10},{10... | collective-permute-start | bytes 786440 | tf_op jit(solution)/shard_map/ppermute | solution.py:190
  38.4 1.6 %shard_map.61 = (f32[256,512]{1,0:T(8,128)S(1)}, f32[256,512]{1,0:T(8,128)S(1)}, f32[256,512]{1,0:T(8,128)S(1)}) custom-call(s32[1,12]{1,0:T(1,128)S(1)} %copy-done.6, bf16[512,256]{1,0:T(8,128)(2,1)S(1)} %get-tuple-element.69.ah, bf16[512,256]{1,0:T(8,128)(2,1)S(1)} %get-tuple-element.70.al, bf16[512,256]{1,0:T(8,128)(2,1)S(1)} %get-tuple-element.71.bh, ...), custom_call_target="tpu_custom_call" | custom-call | flops 402653184 | bytes 4718592 | tf_op jit(solution)/shard_map/pallas_call | solution.py:50
  40.0 4.8 %collective-permute-start.8 = (f32[256,512]{1,0:T(8,128)S(1)}, f32[256,512]{1,0:T(8,128)S(1)}, u32[]{:S(2)}, u32[]{:S(2)}) collective-permute-start(f32[256,512]{1,0:T(8,128)S(1)} %get-tuple-element.79), channel_id=1, source_target_pairs={{0,2},{1,5},{2,0},{3,7},{4,6},{5,1},{6,4},{7,3},{8,10},{9,13},{10,... | collective-permute-start | bytes 1572872 | tf_op jit(solution)/shard_map/ppermute | solution.py:226
  44.8 2.5 %collective-permute-start.16 = (f32[256,512]{1,0:T(8,128)S(1)}, f32[256,512]{1,0:T(8,128)S(1)}, u32[]{:S(2)}, u32[]{:S(2)}) collective-permute-start(f32[256,512]{1,0:T(8,128)S(1)} %get-tuple-element.95.block), channel_id=1, source_target_pairs={{0,4},{1,3},{2,6},{3,1},{4,0},{5,7},{6,2},{7,5},{8,12},{9,11},{10,... | collective-permute-start | bytes 1572872 | tf_op jit(solution)/shard_map/ppermute | solution.py:226
  47.4 1.6 %collective-permute-start.11 = (f32[256,256]{1,0:T(8,128)S(1)}, f32[256,256]{1,0:T(8,128)S(1)}, u32[]{:S(2)}, u32[]{:S(2)}) collective-permute-start(f32[256,256]{1,0:T(8,128)S(1)} %get-tuple-element.83), channel_id=1, source_target_pairs={{0,8},{8,0},{16,24},{24,16},{1,9},{9,1},{17,25},{25,17},{2,10},{10... | collective-permute-start | bytes 786440 | tf_op jit(solution)/shard_map/ppermute | solution.py:190
  49.7 2.0 %shard_map.63 = (f32[256,512]{1,0:T(8,128)}, f32[256,512]{1,0:T(8,128)S(1)}, f32[256,512]{1,0:T(8,128)S(1)}) custom-call(s32[1,12]{1,0:T(1,128)S(1)} %copy-done.6, bf16[512,256]{1,0:T(8,128)(2,1)S(1)} %get-tuple-element.69.ah, bf16[512,256]{1,0:T(8,128)(2,1)S(1)} %get-tuple-element.70.al, bf16[512,256]{1,0:T(8,128)(2,1)S(1)} %get-tuple-element.71.bh, ...), custom_call_target="tpu_custom_call" | custom-call | flops 402653184 | bytes 4718592 | tf_op jit(solution)/shard_map/pallas_call | solution.py:50
  51.6 4.7 %collective-permute-start.14 = (f32[256,512]{1,0:T(8,128)}, f32[256,512]{1,0:T(8,128)}, u32[]{:S(2)}, u32[]{:S(2)}) collective-permute-start(f32[256,512]{1,0:T(8,128)} %get-tuple-element.92), channel_id=1, source_target_pairs={{0,2},{1,5},{2,0},{3,7},{4,6},{5,1},{6,4},{7,3},{8,10},{9,13},{10,... | collective-permute-start | bytes 1572872 | tf_op jit(solution)/shard_map/ppermute | solution.py:226
  56.3 2.5 %collective-permute-start.19 = (f32[256,512]{1,0:T(8,128)S(1)}, f32[256,512]{1,0:T(8,128)S(1)}, u32[]{:S(2)}, u32[]{:S(2)}) collective-permute-start(f32[256,512]{1,0:T(8,128)S(1)} %get-tuple-element.102.block), channel_id=1, source_target_pairs={{0,4},{1,3},{2,6},{3,1},{4,0},{5,7},{6,2},{7,5},{8,12},{9,11},{10,... | collective-permute-start | bytes 1572872 | tf_op jit(solution)/shard_map/ppermute | solution.py:226
  58.8 0.9 shard_map.64
  59.8 1.6 %collective-permute-start.15 = (f32[256,256]{1,0:T(8,128)}, f32[256,256]{1,0:T(8,128)}, u32[]{:S(2)}, u32[]{:S(2)}) collective-permute-start(f32[256,256]{1,0:T(8,128)} %get-tuple-element.93), channel_id=1, source_target_pairs={{0,8},{8,0},{16,24},{24,16},{1,9},{9,1},{17,25},{25,17},{2,10},{10... | collective-permute-start | bytes 786440 | tf_op jit(solution)/shard_map/ppermute | solution.py:190
  61.3 2.6 %collective-permute-start.13 = (f32[256,256]{1,0:T(8,128)}, f32[256,256]{1,0:T(8,128)}, u32[]{:S(2)}, u32[]{:S(2)}) collective-permute-start(f32[256,256]{1,0:T(8,128)} %get-tuple-element.88), channel_id=1, source_target_pairs={{0,16},{8,24},{16,0},{24,8},{1,17},{9,25},{17,1},{25,9},{2,18},{10... | collective-permute-start | bytes 786440 | tf_op jit(solution)/shard_map/ppermute | solution.py:190
  63.9 1.9 %shard_map.65 = (f32[256,512]{1,0:T(8,128)}, f32[256,512]{1,0:T(8,128)S(1)}) custom-call(s32[1,12]{1,0:T(1,128)S(1)} %copy-done.6, bf16[512,256]{1,0:T(8,128)(2,1)S(1)} %get-tuple-element.69.ah, bf16[512,256]{1,0:T(8,128)(2,1)S(1)} %get-tuple-element.70.al, bf16[512,256]{1,0:T(8,128)(2,1)S(1)} %get-tuple-element.71.bh, ...), custom_call_target="tpu_custom_call" | custom-call | flops 402653184 | bytes 4194304 | tf_op jit(solution)/shard_map/pallas_call | solution.py:50
  65.9 1.7 %collective-permute-start.17 = (f32[256,512]{1,0:T(8,128)}, f32[256,512]{1,0:T(8,128)}, u32[]{:S(2)}, u32[]{:S(2)}) collective-permute-start(f32[256,512]{1,0:T(8,128)} %get-tuple-element.99), channel_id=1, source_target_pairs={{0,2},{1,5},{2,0},{3,7},{4,6},{5,1},{6,4},{7,3},{8,10},{9,13},{10,... | collective-permute-start | bytes 1572872 | tf_op jit(solution)/shard_map/ppermute | solution.py:226
  67.5 1.1 constant_dynamic-slice_fusion.1
  68.6 4.4 %collective-permute-done.15.refs_2_ = f32[256,256]{1,0:T(8,128)} collective-permute-done((f32[256,256]{1,0:T(8,128)}, f32[256,256]{1,0:T(8,128)}, u32[]{:S(2)}, u32[]{:S(2)}) %collective-permute-start.15) | collective-permute-done | bytes 262176 | tf_op jit(solution)/shard_map/ppermute | solution.py:190
  73.1 1.2 shard_map.66
  74.3 1.2 collective-permute-done.13.refs_0_
  75.6 1.1 shard_map.67
  76.7 1.5 %shard_map.68 = (f32[256,512]{1,0:T(8,128)S(1)}, f32[256,512]{1,0:T(8,128)S(1)}) custom-call(s32[1,12]{1,0:T(1,128)S(1)} %copy-done.6, bf16[512,256]{1,0:T(8,128)(2,1)S(1)} %get-tuple-element.69.ah, bf16[512,256]{1,0:T(8,128)(2,1)S(1)} %get-tuple-element.70.al, bf16[512,256]{1,0:T(8,128)(2,1)S(1)} %get-tuple-element.71.bh, ...), custom_call_target="tpu_custom_call" | custom-call | flops 402653184 | bytes 4194304 | tf_op jit(solution)/shard_map/pallas_call | solution.py:50
  78.2 1.5 %collective-permute-start.21 = (f32[256,512]{1,0:T(8,128)S(1)}, f32[256,512]{1,0:T(8,128)S(1)}, u32[]{:S(2)}, u32[]{:S(2)}) collective-permute-start(f32[256,512]{1,0:T(8,128)S(1)} %get-tuple-element.108), channel_id=1, source_target_pairs={{0,2},{1,5},{2,0},{3,7},{4,6},{5,1},{6,4},{7,3},{8,10},{9,13},{10,... | collective-permute-start | bytes 1572872 | tf_op jit(solution)/shard_map/ppermute | solution.py:226
  79.7 1.1 collective-permute-done.18.refs_2_
  80.8 1.1 shard_map.69
  82.1 3.6 %collective-permute-start.20 = (f32[256,256]{1,0:T(8,128)S(1)}, f32[256,256]{1,0:T(8,128)S(1)}, u32[]{:S(2)}, u32[]{:S(2)}) collective-permute-start(f32[256,256]{1,0:T(8,128)S(1)} %get-tuple-element.105), channel_id=1, source_target_pairs={{0,16},{8,24},{16,0},{24,8},{1,17},{9,25},{17,1},{25,9},{2,18},{10... | collective-permute-start | bytes 786440 | tf_op jit(solution)/shard_map/ppermute | solution.py:190
  85.7 8.4 %collective-permute-done.22.refs_2_ = f32[256,256]{1,0:T(8,128)S(1)} collective-permute-done((f32[256,256]{1,0:T(8,128)S(1)}, f32[256,256]{1,0:T(8,128)S(1)}, u32[]{:S(2)}, u32[]{:S(2)}) %collective-permute-start.22) | collective-permute-done | bytes 262176 | tf_op jit(solution)/shard_map/ppermute | solution.py:190
  94.2 2.6 %collective-permute-start.23 = (f32[256,128]{1,0:T(8,128)S(1)}, f32[256,128]{1,0:T(8,128)S(1)}, u32[]{:S(2)}, u32[]{:S(2)}) collective-permute-start(f32[256,128]{1,0:T(8,128)S(1)} %get-tuple-element.113), channel_id=1, source_target_pairs={{0,16},{8,24},{16,0},{24,8},{1,17},{9,25},{17,1},{25,9},{2,18},{10... | collective-permute-start | bytes 393224 | tf_op jit(solution)/shard_map/ppermute | solution.py:190
  97.0 5.0 %collective-permute-done.24.refs_0_ = f32[256,256]{1,0:T(8,128)S(1)} collective-permute-done((f32[256,256]{1,0:T(8,128)S(1)}, f32[256,256]{1,0:T(8,128)S(1)}, u32[]{:S(2)}, u32[]{:S(2)}) %collective-permute-start.24) | collective-permute-done | bytes 262176 | tf_op jit(solution)/shard_map/ppermute | solution.py:190
  102.0 1.5 %collective-permute-start.25 = (f32[256,128]{1,0:T(8,128)S(1)}, f32[256,128]{1,0:T(8,128)S(1)}, u32[]{:S(2)}, u32[]{:S(2)}) collective-permute-start(f32[256,128]{1,0:T(8,128)S(1)} %get-tuple-element.119), channel_id=1, source_target_pairs={{0,16},{8,24},{16,0},{24,8},{1,17},{9,25},{17,1},{25,9},{2,18},{10... | collective-permute-start | bytes 393224 | tf_op jit(solution)/shard_map/ppermute | solution.py:190
  103.5 1.0 constant_dynamic-slice_fusion
  104.6 4.7 %collective-permute-done.25.refs_0_ = f32[256,128]{1,0:T(8,128)S(1)} collective-permute-done((f32[256,128]{1,0:T(8,128)S(1)}, f32[256,128]{1,0:T(8,128)S(1)}, u32[]{:S(2)}, u32[]{:S(2)}) %collective-permute-start.25) | collective-permute-done | bytes 131104 | tf_op jit(solution)/shard_map/ppermute | solution.py:190
  109.7 1.1 collective-permute-done.26
  110.8 3.6 %collective-permute-done.27 = f32[256]{0:T(256)S(1)} collective-permute-done((f32[256]{0:T(256)S(1)}, f32[256]{0:T(256)S(1)}, u32[]{:S(2)}, u32[]{:S(2)}) %collective-permute-start.27) | collective-permute-done | bytes 1056 | tf_op jit(solution)/shard_map/ppermute | solution.py:190
  114.4 0.8 collective-permute-start.28
  115.2 3.6 %collective-permute-done.28 = f32[256]{0:T(256)S(1)} collective-permute-done((f32[256]{0:T(256)S(1)}, f32[256]{0:T(256)S(1)}, u32[]{:S(2)}, u32[]{:S(2)}) %collective-permute-start.28) | collective-permute-done | bytes 1056 | tf_op jit(solution)/shard_map/ppermute | solution.py:190
  118.9 1.0 maximum_divide_fusion
  (52 shorter events, 3.7 us)
Async XLA Ops:
  3.3 15.5 %collective-permute-start.4 = (f32[256,512]{1,0:T(8,128)}, f32[256,512]{1,0:T(8,128)S(1)}, u32[]{:S(2)}, u32[]{:S(2)}) collective-permute-start(f32[256,512]{1,0:T(8,128)} %get-tuple-element.73.block), channel_id=1, source_target_pairs={{0,4},{1,3},{2,6},{3,1},{4,0},{5,7},{6,2},{7,5},{8,12},{9,11},{10,... | collective-permute-start | bytes 1572872 | tf_op jit(solution)/shard_map/ppermute | solution.py:226
  6.3 9.7 %collective-permute-start = (f32[256,256]{1,0:T(8,128)}, f32[256,256]{1,0:T(8,128)S(1)}, u32[]{:S(2)}, u32[]{:S(2)}) collective-permute-start(f32[256,256]{1,0:T(8,128)} %get-tuple-element.65), channel_id=1, source_target_pairs={{0,2},{1,5},{2,0},{3,7},{4,1},{5,6},{6,3},{7,4},{8,10},{9,13},{10,... | collective-permute-start | bytes 786440 | tf_op jit(solution)/shard_map/ppermute | solution.py:226
  7.8 10.6 %collective-permute-start.1 = (f32[256,256]{1,0:T(8,128)}, f32[256,256]{1,0:T(8,128)S(1)}, u32[]{:S(2)}, u32[]{:S(2)}) collective-permute-start(f32[256,256]{1,0:T(8,128)} %get-tuple-element.66), channel_id=1, source_target_pairs={{1,5},{3,7},{4,1},{5,4},{6,3},{7,6},{9,13},{11,15},{12,9},{13,12},... | collective-permute-start | bytes 786440 | tf_op jit(solution)/shard_map/ppermute | solution.py:226
  8.4 9.9 %collective-permute-start.2 = (f32[256,256]{1,0:T(8,128)}, f32[256,256]{1,0:T(8,128)S(1)}, u32[]{:S(2)}, u32[]{:S(2)}) collective-permute-start(f32[256,256]{1,0:T(8,128)} %get-tuple-element.67), channel_id=1, source_target_pairs={{0,1},{1,2},{2,3},{3,0},{4,6},{6,4},{8,9},{9,10},{10,11},{11,8},{1... | collective-permute-start | bytes 786440 | tf_op jit(solution)/shard_map/ppermute | solution.py:226
  11.9 6.5 %collective-permute-start.3 = (f32[256,256]{1,0:T(8,128)}, f32[256,256]{1,0:T(8,128)S(1)}, u32[]{:S(2)}, u32[]{:S(2)}) collective-permute-start(f32[256,256]{1,0:T(8,128)} %get-tuple-element.68), channel_id=1, source_target_pairs={{0,1},{1,0},{2,3},{3,2},{8,9},{9,8},{10,11},{11,10},{16,17},{17,16... | collective-permute-start | bytes 786440 | tf_op jit(solution)/shard_map/ppermute | solution.py:226
  13.9 4.5 %copy-start.1 = (f32[256,512]{1,0:T(8,128)S(1)}, f32[256,512]{1,0:T(8,128)}, u32[]{:S(2)}) copy-start(f32[256,512]{1,0:T(8,128)} %get-tuple-element.64.left.token) | copy-start | bytes 1572868
  13.9 5.0 %copy-start = (f32[1,256,3072]{2,1,0:T(8,128)S(1)}, f32[1,256,3072]{2,1,0:T(8,128)}, u32[]{:S(2)}) copy-start(f32[1,256,3072]{2,1,0:T(8,128)} %param.6) | copy-start | bytes 9437188
  13.9 5.0 %copy-start.3 = (f32[256,512]{1,0:T(8,128)S(1)}, f32[256,512]{1,0:T(8,128)}, u32[]{:S(2)}) copy-start(f32[256,512]{1,0:T(8,128)} %get-tuple-element.73.block) | copy-start | bytes 1572868
  13.9 4.9 %copy-start.6 = (s32[1,12]{1,0:T(1,128)S(1)}, s32[1,12]{1,0:T(1,128)}, u32[]{:S(2)}) copy-start(s32[1,12]{1,0:T(1,128)} %col_blocks.11) | copy-start | bytes 148
  16.0 11.2 %collective-permute-start.7 = (f32[256,512]{1,0:T(8,128)}, f32[256,512]{1,0:T(8,128)S(1)}, u32[]{:S(2)}, u32[]{:S(2)}) collective-permute-start(f32[256,512]{1,0:T(8,128)} %shard_map.58.block), channel_id=1, source_target_pairs={{0,4},{1,3},{2,6},{3,1},{4,0},{5,7},{6,2},{7,5},{8,12},{9,11},{10,... | collective-permute-start | bytes 1572872 | tf_op jit(solution)/shard_map/ppermute | solution.py:226
  18.8 8.4 %copy-start.2 = (f32[256,512]{1,0:T(8,128)S(1)}, f32[256,512]{1,0:T(8,128)}, u32[]{:S(2)}) copy-start(f32[256,512]{1,0:T(8,128)} %shard_map.58.block) | copy-start | bytes 1572868
  20.4 15.6 %collective-permute-start.6 = (f32[256,512]{1,0:T(8,128)S(1)}, f32[256,512]{1,0:T(8,128)S(1)}, u32[]{:S(2)}, u32[]{:S(2)}) collective-permute-start(f32[256,512]{1,0:T(8,128)S(1)} %get-tuple-element.75), channel_id=1, source_target_pairs={{0,2},{1,5},{2,0},{3,7},{4,6},{5,1},{6,4},{7,3},{8,10},{9,13},{10,... | collective-permute-start | bytes 1572872 | tf_op jit(solution)/shard_map/ppermute | solution.py:226
  22.9 15.6 %collective-permute-start.5 = (f32[256,512]{1,0:T(8,128)S(1)}, f32[256,512]{1,0:T(8,128)S(1)}, u32[]{:S(2)}, u32[]{:S(2)}) collective-permute-start(f32[256,512]{1,0:T(8,128)S(1)} %get-tuple-element.74.block), channel_id=1, source_target_pairs={{0,4},{1,3},{2,6},{3,1},{4,0},{5,7},{6,2},{7,5},{8,12},{9,11},{10,... | collective-permute-start | bytes 1572872 | tf_op jit(solution)/shard_map/ppermute | solution.py:226
  28.8 18.5 %collective-permute-start.9 = (f32[256,512]{1,0:T(8,128)S(1)}, f32[256,512]{1,0:T(8,128)S(1)}, u32[]{:S(2)}, u32[]{:S(2)}) collective-permute-start(f32[256,512]{1,0:T(8,128)S(1)} %get-tuple-element.81), channel_id=1, source_target_pairs={{0,2},{1,5},{2,0},{3,7},{4,6},{5,1},{6,4},{7,3},{8,10},{9,13},{10,... | collective-permute-start | bytes 1572872 | tf_op jit(solution)/shard_map/ppermute | solution.py:226
  33.7 16.0 %collective-permute-start.12 = (f32[256,512]{1,0:T(8,128)S(1)}, f32[256,512]{1,0:T(8,128)S(1)}, u32[]{:S(2)}, u32[]{:S(2)}) collective-permute-start(f32[256,512]{1,0:T(8,128)S(1)} %get-tuple-element.86.block), channel_id=1, source_target_pairs={{0,4},{1,3},{2,6},{3,1},{4,0},{5,7},{6,2},{7,5},{8,12},{9,11},{10,... | collective-permute-start | bytes 1572872 | tf_op jit(solution)/shard_map/ppermute | solution.py:226
  36.1 11.1 %collective-permute-start.10 = (f32[256,256]{1,0:T(8,128)S(1)}, f32[256,256]{1,0:T(8,128)S(1)}, u32[]{:S(2)}, u32[]{:S(2)}) collective-permute-start(f32[256,256]{1,0:T(8,128)S(1)} %get-tuple-element.82), channel_id=1, source_target_pairs={{0,8},{8,0},{16,24},{24,16},{1,9},{9,1},{17,25},{25,17},{2,10},{10... | collective-permute-start | bytes 786440 | tf_op jit(solution)/shard_map/ppermute | solution.py:190
  40.0 18.8 %collective-permute-start.8 = (f32[256,512]{1,0:T(8,128)S(1)}, f32[256,512]{1,0:T(8,128)S(1)}, u32[]{:S(2)}, u32[]{:S(2)}) collective-permute-start(f32[256,512]{1,0:T(8,128)S(1)} %get-tuple-element.79), channel_id=1, source_target_pairs={{0,2},{1,5},{2,0},{3,7},{4,6},{5,1},{6,4},{7,3},{8,10},{9,13},{10,... | collective-permute-start | bytes 1572872 | tf_op jit(solution)/shard_map/ppermute | solution.py:226
  44.8 19.1 %collective-permute-start.16 = (f32[256,512]{1,0:T(8,128)S(1)}, f32[256,512]{1,0:T(8,128)S(1)}, u32[]{:S(2)}, u32[]{:S(2)}) collective-permute-start(f32[256,512]{1,0:T(8,128)S(1)} %get-tuple-element.95.block), channel_id=1, source_target_pairs={{0,4},{1,3},{2,6},{3,1},{4,0},{5,7},{6,2},{7,5},{8,12},{9,11},{10,... | collective-permute-start | bytes 1572872 | tf_op jit(solution)/shard_map/ppermute | solution.py:226
  47.4 11.4 %collective-permute-start.11 = (f32[256,256]{1,0:T(8,128)S(1)}, f32[256,256]{1,0:T(8,128)S(1)}, u32[]{:S(2)}, u32[]{:S(2)}) collective-permute-start(f32[256,256]{1,0:T(8,128)S(1)} %get-tuple-element.83), channel_id=1, source_target_pairs={{0,8},{8,0},{16,24},{24,16},{1,9},{9,1},{17,25},{25,17},{2,10},{10... | collective-permute-start | bytes 786440 | tf_op jit(solution)/shard_map/ppermute | solution.py:190
  51.6 21.4 %collective-permute-start.14 = (f32[256,512]{1,0:T(8,128)}, f32[256,512]{1,0:T(8,128)}, u32[]{:S(2)}, u32[]{:S(2)}) collective-permute-start(f32[256,512]{1,0:T(8,128)} %get-tuple-element.92), channel_id=1, source_target_pairs={{0,2},{1,5},{2,0},{3,7},{4,6},{5,1},{6,4},{7,3},{8,10},{9,13},{10,... | collective-permute-start | bytes 1572872 | tf_op jit(solution)/shard_map/ppermute | solution.py:226
  56.3 20.3 %collective-permute-start.19 = (f32[256,512]{1,0:T(8,128)S(1)}, f32[256,512]{1,0:T(8,128)S(1)}, u32[]{:S(2)}, u32[]{:S(2)}) collective-permute-start(f32[256,512]{1,0:T(8,128)S(1)} %get-tuple-element.102.block), channel_id=1, source_target_pairs={{0,4},{1,3},{2,6},{3,1},{4,0},{5,7},{6,2},{7,5},{8,12},{9,11},{10,... | collective-permute-start | bytes 1572872 | tf_op jit(solution)/shard_map/ppermute | solution.py:226
  59.8 6.1 %copy-start.4 = (f32[256,128]{1,0:T(8,128)}, f32[256,128]{1,0:T(8,128)S(1)}, u32[]{:S(2)}) copy-start(f32[256,128]{1,0:T(8,128)S(1)} %get-tuple-element.90.refs_2_) | copy-start | bytes 393220
  59.8 13.3 %collective-permute-start.15 = (f32[256,256]{1,0:T(8,128)}, f32[256,256]{1,0:T(8,128)}, u32[]{:S(2)}, u32[]{:S(2)}) collective-permute-start(f32[256,256]{1,0:T(8,128)} %get-tuple-element.93), channel_id=1, source_target_pairs={{0,8},{8,0},{16,24},{24,16},{1,9},{9,1},{17,25},{25,17},{2,10},{10... | collective-permute-start | bytes 786440 | tf_op jit(solution)/shard_map/ppermute | solution.py:190
  61.3 14.2 %collective-permute-start.13 = (f32[256,256]{1,0:T(8,128)}, f32[256,256]{1,0:T(8,128)}, u32[]{:S(2)}, u32[]{:S(2)}) collective-permute-start(f32[256,256]{1,0:T(8,128)} %get-tuple-element.88), channel_id=1, source_target_pairs={{0,16},{8,24},{16,0},{24,8},{1,17},{9,25},{17,1},{25,9},{2,18},{10... | collective-permute-start | bytes 786440 | tf_op jit(solution)/shard_map/ppermute | solution.py:190
  65.9 14.9 %collective-permute-start.17 = (f32[256,512]{1,0:T(8,128)}, f32[256,512]{1,0:T(8,128)}, u32[]{:S(2)}, u32[]{:S(2)}) collective-permute-start(f32[256,512]{1,0:T(8,128)} %get-tuple-element.99), channel_id=1, source_target_pairs={{0,2},{1,5},{2,0},{3,7},{4,6},{5,1},{6,4},{7,3},{8,10},{9,13},{10,... | collective-permute-start | bytes 1572872 | tf_op jit(solution)/shard_map/ppermute | solution.py:226
  67.5 8.0 %copy-start.5 = (f32[256,128]{1,0:T(8,128)S(1)}, f32[256,128]{1,0:T(8,128)}, u32[]{:S(2)}) copy-start(f32[256,128]{1,0:T(8,128)} %copy-done.4) | copy-start | bytes 393220
  74.3 6.5 %collective-permute-start.18 = (f32[256,256]{1,0:T(8,128)S(1)}, f32[256,256]{1,0:T(8,128)S(1)}, u32[]{:S(2)}, u32[]{:S(2)}) collective-permute-start(f32[256,256]{1,0:T(8,128)S(1)} %get-tuple-element.100), channel_id=1, source_target_pairs={{0,8},{8,0},{16,24},{24,16},{1,9},{9,1},{17,25},{25,17},{2,10},{10... | collective-permute-start | bytes 786440 | tf_op jit(solution)/shard_map/ppermute | solution.py:190
  78.2 15.9 %collective-permute-start.21 = (f32[256,512]{1,0:T(8,128)S(1)}, f32[256,512]{1,0:T(8,128)S(1)}, u32[]{:S(2)}, u32[]{:S(2)}) collective-permute-start(f32[256,512]{1,0:T(8,128)S(1)} %get-tuple-element.108), channel_id=1, source_target_pairs={{0,2},{1,5},{2,0},{3,7},{4,6},{5,1},{6,4},{7,3},{8,10},{9,13},{10,... | collective-permute-start | bytes 1572872 | tf_op jit(solution)/shard_map/ppermute | solution.py:226
  81.9 12.2 %collective-permute-start.22 = (f32[256,256]{1,0:T(8,128)S(1)}, f32[256,256]{1,0:T(8,128)S(1)}, u32[]{:S(2)}, u32[]{:S(2)}) collective-permute-start(f32[256,256]{1,0:T(8,128)S(1)} %get-tuple-element.109), channel_id=1, source_target_pairs={{0,8},{8,0},{16,24},{24,16},{1,9},{9,1},{17,25},{25,17},{2,10},{10... | collective-permute-start | bytes 786440 | tf_op jit(solution)/shard_map/ppermute | solution.py:190
  82.1 14.7 %collective-permute-start.20 = (f32[256,256]{1,0:T(8,128)S(1)}, f32[256,256]{1,0:T(8,128)S(1)}, u32[]{:S(2)}, u32[]{:S(2)}) collective-permute-start(f32[256,256]{1,0:T(8,128)S(1)} %get-tuple-element.105), channel_id=1, source_target_pairs={{0,16},{8,24},{16,0},{24,8},{1,17},{9,25},{17,1},{25,9},{2,18},{10... | collective-permute-start | bytes 786440 | tf_op jit(solution)/shard_map/ppermute | solution.py:190
  94.2 7.8 %collective-permute-start.24 = (f32[256,256]{1,0:T(8,128)S(1)}, f32[256,256]{1,0:T(8,128)S(1)}, u32[]{:S(2)}, u32[]{:S(2)}) collective-permute-start(f32[256,256]{1,0:T(8,128)S(1)} %get-tuple-element.116), channel_id=1, source_target_pairs={{0,8},{8,0},{16,24},{24,16},{1,9},{9,1},{17,25},{25,17},{2,10},{10... | collective-permute-start | bytes 786440 | tf_op jit(solution)/shard_map/ppermute | solution.py:190
  94.2 10.3 %collective-permute-start.23 = (f32[256,128]{1,0:T(8,128)S(1)}, f32[256,128]{1,0:T(8,128)S(1)}, u32[]{:S(2)}, u32[]{:S(2)}) collective-permute-start(f32[256,128]{1,0:T(8,128)S(1)} %get-tuple-element.113), channel_id=1, source_target_pairs={{0,16},{8,24},{16,0},{24,8},{1,17},{9,25},{17,1},{25,9},{2,18},{10... | collective-permute-start | bytes 393224 | tf_op jit(solution)/shard_map/ppermute | solution.py:190
  102.0 7.3 %collective-permute-start.25 = (f32[256,128]{1,0:T(8,128)S(1)}, f32[256,128]{1,0:T(8,128)S(1)}, u32[]{:S(2)}, u32[]{:S(2)}) collective-permute-start(f32[256,128]{1,0:T(8,128)S(1)} %get-tuple-element.119), channel_id=1, source_target_pairs={{0,16},{8,24},{16,0},{24,8},{1,17},{9,25},{17,1},{25,9},{2,18},{10... | collective-permute-start | bytes 393224 | tf_op jit(solution)/shard_map/ppermute | solution.py:190
  109.6 1.2 %collective-permute-start.26 = (f32[256]{0:T(256)S(1)}, f32[256]{0:T(256)S(1)}, u32[]{:S(2)}, u32[]{:S(2)}) collective-permute-start(f32[256]{0:T(256)S(1)} %reduce_max.9), channel_id=1, source_target_pairs={{0,1},{1,0},{2,3},{3,2},{4,5},{5,4},{6,7},{7,6},{8,9},{9,8},{10,11... | collective-permute-start | bytes 3080 | tf_op jit(solution)/shard_map/ppermute | solution.py:190
  110.8 3.6 %collective-permute-start.27 = (f32[256]{0:T(256)S(1)}, f32[256]{0:T(256)S(1)}, u32[]{:S(2)}, u32[]{:S(2)}) collective-permute-start(f32[256]{0:T(256)S(1)} %max.9), channel_id=1, source_target_pairs={{0,8},{8,0},{16,24},{24,16},{1,9},{9,1},{17,25},{25,17},{2,10},{10... | collective-permute-start | bytes 3080 | tf_op jit(solution)/shard_map/ppermute | solution.py:190
  114.4 4.5 %collective-permute-start.28 = (f32[256]{0:T(256)S(1)}, f32[256]{0:T(256)S(1)}, u32[]{:S(2)}, u32[]{:S(2)}) collective-permute-start(f32[256]{0:T(256)S(1)} %max.10), channel_id=1, source_target_pairs={{0,16},{8,24},{16,0},{24,8},{1,17},{9,25},{17,1},{25,9},{2,18},{10... | collective-permute-start | bytes 3080 | tf_op jit(solution)/shard_map/ppermute | solution.py:190

commit v5 on v4

--- a/solution.py
+++ b/solution.py
@@ -116,9 +116,7 @@
     tiles, outs = refs[:count], refs[count:]
     for out, (index, _) in zip(outs, PANEL_ROUNDS):
         out[...] = pick(y, c, *(named[k] for k in index))
-    outs[4][:, :depth] = l0
-    outs[4][:, depth:] = l1
-    copy_message(tiles, outs[5], chunks)
+    copy_message(tiles, outs[4], chunks)
 
 
 def spanned(chunk):
@@ -126,11 +124,12 @@
     return (at + wide - 1) // LANES - at // LANES + 1
 
 
-def panel_body(left, *refs):
+def panel_body(row_blocks, left, *refs):
     x, y, c = coordinates()
     height, depth = left.shape[0], left.shape[1] // 2
     r1, r2, r3, r4 = (r[...] for r in refs[:4])
-    l0, l1 = left[:, :depth], left[:, depth:]
+    mask = jnp.where(row_blocks[0, 0] > 0, 1.0, 0.0).astype(F32)
+    l0, l1 = left[:, :depth] * mask, left[:, depth:] * mask
     lx = jnp.where(x, l1, l0)
     partner = pick(y, c, r1, r1, r3, r1), pick(y, c, r3, r2, r1, r2)
     own = pick(y, c, lx, r3, lx, l0), pick(y, c, r4, r4, r2, l1)
@@ -247,12 +246,12 @@
     first = run(
         functools.partial(first_body, [chunks[i] for i in GATHERS[0]]),
         [(SMEM, row_blocks), (VMEM, left)] + tiles_of(GATHERS[0]),
-        [shape(height, depth)] * 4 + [shape(height, 2 * depth), shape(depth, widths(GATHERS[0]))],
+        [shape(height, depth)] * 4 + [shape(depth, widths(GATHERS[0]))],
         limit=FIRST,
     )
-    blocks, gots = {0: first[5]}, {0: gather(first[5])}
+    blocks, gots = {0: first[4]}, {0: gather(first[4])}
     landed = [move(v, lambda r, c, hops=hops: hops[(r // 2) * 2 + c]) for v, (_, hops) in zip(first[:4], PANEL_ROUNDS)]
-    lower = first[4]
+    lower = first[0]
     for g, tie in enumerate(TIES):
         if g and tie is None:
             blocks[g], = run(
@@ -260,7 +259,7 @@
                 [(ANY, lower)] + tiles_of(GATHERS[g]), [shape(depth, widths(GATHERS[g]))], limit=FIRST,
             )
             gots[g] = gather(blocks[g])
-    halves = run(panel_body, [(VMEM, lower)] + [(VMEM, v) for v in landed], [shape(2 * height, depth, dtype=BF16)] * 4)
+    halves = run(panel_body, [(SMEM, row_blocks), (VMEM, left)] + [(VMEM, v) for v in landed], [shape(2 * height, depth, dtype=BF16)] * 4)
 
     share = lax.dynamic_slice_in_dim(after(ancestor, halves[0]), leaf * share_cols, share_cols, 1)
     waiting = {}

time: 121 us -> 122 us (level)
  transfers between devices with their start and end apart: 29 -> 29, of which waited for: 13 -> 13; matrix products, arithmetic and copies ran while one was open for 2% -> 2% of each run, Pallas kernels for 15% -> 14%
where the time goes in v5:
time: 122 us; the launch traced here: 121 us
  starting transfers between devices  57.1 us (47%)
  waiting for transfers between devices  39.1 us (32%)
  Pallas kernels  20.1 us (16%)
  local copies, waits for them, and re-layouts  2.78 us (2%)
    ppermute x16, starting transfers between devices, move(): return lax.ppermute(value, ('row', 'col'), pairs)  40.6 us
    ppermute x13, waiting for transfers between devices, swap(): return lax.ppermute(value, axis, [(i, i ^ bit) for i in range(size)])  34.1 us
    pallas_call x20, Pallas kernels, run(): pl.pallas_call(body, grid=(1,), in_specs=[whole(a) if s is VMEM else s fo...  20.1 us
    ppermute x13, starting transfers between devices, swap(): return lax.ppermute(value, axis, [(i, i ^ bit) for i in range(size)])  16.5 us
    ppermute x16, waiting for transfers between devices, move(): return lax.ppermute(value, ('row', 'col'), pairs)  4.95 us
  transfers between devices with their start and end apart: 29, of which 13 were waited for; matrix products, arithmetic and copies ran while one was open for 2% of the time, Pallas kernels for 14%

profile of v5, /device:TPU:0, one launch (start us, length us, event | category | flops | bytes accessed | tf_op | source)
XLA Modules:
  0.0 121.1 jit_solution(5314772094739558080)
XLA Ops:
  0.7 2.5 %shard_map.55 = (f32[256,256]{1,0:T(8,128)}, f32[256,256]{1,0:T(8,128)}, f32[256,256]{1,0:T(8,128)}, f32[256,256]{1,0:T(8,128)}, f32[256,512]{1,0:T(8,128)}) custom-call(s32[1,1]{1,0:T(1,128)S(6)} %copy.6.row_blocks, f32[256,512]{1,0:T(8,128)} %bitcast.26, f32[256,3072]{1,0:T(8,128)} %bitcast.2, f32[256,3072]{1,0:T(8,128)} %bitcast.3, f32[256,3072]{1,0:T(8,128)} %bitcast.4, ...), custom_call_target="tpu_custom_call" | custom-call | bytes 2097152 | tf_op jit(solution)/shard_map/pallas_call | solution.py:50
  3.1 3.0 %collective-permute-start.4 = (f32[256,512]{1,0:T(8,128)}, f32[256,512]{1,0:T(8,128)S(1)}, u32[]{:S(2)}, u32[]{:S(2)}) collective-permute-start(f32[256,512]{1,0:T(8,128)} %get-tuple-element.71.block), channel_id=1, source_target_pairs={{0,4},{1,3},{2,6},{3,1},{4,0},{5,7},{6,2},{7,5},{8,12},{9,11},{10,... | collective-permute-start | bytes 1572872 | tf_op jit(solution)/shard_map/ppermute | solution.py:225
  6.1 1.5 %collective-permute-start = (f32[256,256]{1,0:T(8,128)}, f32[256,256]{1,0:T(8,128)S(1)}, u32[]{:S(2)}, u32[]{:S(2)}) collective-permute-start(f32[256,256]{1,0:T(8,128)} %get-tuple-element.63.token), channel_id=1, source_target_pairs={{0,2},{1,5},{2,0},{3,7},{4,1},{5,6},{6,3},{7,4},{8,10},{9,13},{10,... | collective-permute-start | bytes 786440 | tf_op jit(solution)/shard_map/ppermute | solution.py:225
  8.2 3.5 %collective-permute-start.2 = (f32[256,256]{1,0:T(8,128)}, f32[256,256]{1,0:T(8,128)S(1)}, u32[]{:S(2)}, u32[]{:S(2)}) collective-permute-start(f32[256,256]{1,0:T(8,128)} %get-tuple-element.65), channel_id=1, source_target_pairs={{0,1},{1,2},{2,3},{3,0},{4,6},{6,4},{8,9},{9,10},{10,11},{11,8},{1... | collective-permute-start | bytes 786440 | tf_op jit(solution)/shard_map/ppermute | solution.py:225
  11.8 2.1 %collective-permute-start.3 = (f32[256,256]{1,0:T(8,128)}, f32[256,256]{1,0:T(8,128)S(1)}, u32[]{:S(2)}, u32[]{:S(2)}) collective-permute-start(f32[256,256]{1,0:T(8,128)} %get-tuple-element.66), channel_id=1, source_target_pairs={{0,1},{1,0},{2,3},{3,2},{8,9},{9,8},{10,11},{11,10},{16,17},{17,16... | collective-permute-start | bytes 786440 | tf_op jit(solution)/shard_map/ppermute | solution.py:225
  13.8 2.1 %shard_map.58.block = f32[256,512]{1,0:T(8,128)} custom-call(f32[256,256]{1,0:T(8,128)} %get-tuple-element.63.token, f32[256,3072]{1,0:T(8,128)} %bitcast.6, f32[256,3072]{1,0:T(8,128)} %bitcast.7, f32[256,3072]{1,0:T(8,128)} %bitcast.8, f32[256,3072]{1,0:T(8,128)} %bitcast.9), custom_call_target="tpu_custom_call" | custom-call | bytes 524288 | tf_op jit(solution)/shard_map/pallas_call | solution.py:50
  16.0 2.2 %collective-permute-start.7 = (f32[256,512]{1,0:T(8,128)}, f32[256,512]{1,0:T(8,128)S(1)}, u32[]{:S(2)}, u32[]{:S(2)}) collective-permute-start(f32[256,512]{1,0:T(8,128)} %shard_map.58.block), channel_id=1, source_target_pairs={{0,4},{1,3},{2,6},{3,1},{4,0},{5,7},{6,2},{7,5},{8,12},{9,11},{10,... | collective-permute-start | bytes 1572872 | tf_op jit(solution)/shard_map/ppermute | solution.py:225
  18.7 1.6 %shard_map.57 = (f32[256,512]{1,0:T(8,128)S(1)}, f32[256,512]{1,0:T(8,128)S(1)}, f32[256,512]{1,0:T(8,128)S(1)}) custom-call(s32[1,12]{1,0:T(1,128)S(1)} %copy-done.7, bf16[512,256]{1,0:T(8,128)(2,1)S(1)} %get-tuple-element.67.ah, bf16[512,256]{1,0:T(8,128)(2,1)S(1)} %get-tuple-element.68.al, bf16[512,256]{1,0:T(8,128)(2,1)S(1)} %get-tuple-element.69.bh, ...), custom_call_target="tpu_custom_call" | custom-call | flops 402653184 | bytes 4718592 | tf_op jit(solution)/shard_map/pallas_call | solution.py:50
  20.3 2.4 %collective-permute-start.6 = (f32[256,512]{1,0:T(8,128)S(1)}, f32[256,512]{1,0:T(8,128)S(1)}, u32[]{:S(2)}, u32[]{:S(2)}) collective-permute-start(f32[256,512]{1,0:T(8,128)S(1)} %get-tuple-element.73), channel_id=1, source_target_pairs={{0,2},{1,5},{2,0},{3,7},{4,6},{5,1},{6,4},{7,3},{8,10},{9,13},{10,... | collective-permute-start | bytes 1572872 | tf_op jit(solution)/shard_map/ppermute | solution.py:225
  22.7 0.8 collective-permute-start.5
  23.5 3.5 %collective-permute-done.7.got = f32[256,512]{1,0:T(8,128)S(1)} collective-permute-done((f32[256,512]{1,0:T(8,128)}, f32[256,512]{1,0:T(8,128)S(1)}, u32[]{:S(2)}, u32[]{:S(2)}) %collective-permute-start.7) | collective-permute-done | bytes 524320 | tf_op jit(solution)/shard_map/ppermute | solution.py:225
  27.0 1.6 %shard_map.59 = (f32[256,512]{1,0:T(8,128)S(1)}, f32[256,512]{1,0:T(8,128)S(1)}, f32[256,512]{1,0:T(8,128)S(1)}) custom-call(s32[1,12]{1,0:T(1,128)S(1)} %copy-done.7, bf16[512,256]{1,0:T(8,128)(2,1)S(1)} %get-tuple-element.67.ah, bf16[512,256]{1,0:T(8,128)(2,1)S(1)} %get-tuple-element.68.al, bf16[512,256]{1,0:T(8,128)(2,1)S(1)} %get-tuple-element.69.bh, ...), custom_call_target="tpu_custom_call" | custom-call | flops 402653184 | bytes 4718592 | tf_op jit(solution)/shard_map/pallas_call | solution.py:50
  28.6 4.9 %collective-permute-start.9 = (f32[256,512]{1,0:T(8,128)S(1)}, f32[256,512]{1,0:T(8,128)S(1)}, u32[]{:S(2)}, u32[]{:S(2)}) collective-permute-start(f32[256,512]{1,0:T(8,128)S(1)} %get-tuple-element.79), channel_id=1, source_target_pairs={{0,2},{1,5},{2,0},{3,7},{4,6},{5,1},{6,4},{7,3},{8,10},{9,13},{10,... | collective-permute-start | bytes 1572872 | tf_op jit(solution)/shard_map/ppermute | solution.py:225
  33.4 2.4 %collective-permute-start.12 = (f32[256,512]{1,0:T(8,128)S(1)}, f32[256,512]{1,0:T(8,128)S(1)}, u32[]{:S(2)}, u32[]{:S(2)}) collective-permute-start(f32[256,512]{1,0:T(8,128)S(1)} %get-tuple-element.84.block), channel_id=1, source_target_pairs={{0,4},{1,3},{2,6},{3,1},{4,0},{5,7},{6,2},{7,5},{8,12},{9,11},{10,... | collective-permute-start | bytes 1572872 | tf_op jit(solution)/shard_map/ppermute | solution.py:225
  35.9 1.6 %collective-permute-start.10 = (f32[256,256]{1,0:T(8,128)S(1)}, f32[256,256]{1,0:T(8,128)S(1)}, u32[]{:S(2)}, u32[]{:S(2)}) collective-permute-start(f32[256,256]{1,0:T(8,128)S(1)} %get-tuple-element.80), channel_id=1, source_target_pairs={{0,8},{8,0},{16,24},{24,16},{1,9},{9,1},{17,25},{25,17},{2,10},{10... | collective-permute-start | bytes 786440 | tf_op jit(solution)/shard_map/ppermute | solution.py:189
  38.2 1.6 %shard_map.61 = (f32[256,512]{1,0:T(8,128)S(1)}, f32[256,512]{1,0:T(8,128)S(1)}, f32[256,512]{1,0:T(8,128)S(1)}) custom-call(s32[1,12]{1,0:T(1,128)S(1)} %copy-done.7, bf16[512,256]{1,0:T(8,128)(2,1)S(1)} %get-tuple-element.67.ah, bf16[512,256]{1,0:T(8,128)(2,1)S(1)} %get-tuple-element.68.al, bf16[512,256]{1,0:T(8,128)(2,1)S(1)} %get-tuple-element.69.bh, ...), custom_call_target="tpu_custom_call" | custom-call | flops 402653184 | bytes 4718592 | tf_op jit(solution)/shard_map/pallas_call | solution.py:50
  39.8 4.8 %collective-permute-start.8 = (f32[256,512]{1,0:T(8,128)S(1)}, f32[256,512]{1,0:T(8,128)S(1)}, u32[]{:S(2)}, u32[]{:S(2)}) collective-permute-start(f32[256,512]{1,0:T(8,128)S(1)} %get-tuple-element.77), channel_id=1, source_target_pairs={{0,2},{1,5},{2,0},{3,7},{4,6},{5,1},{6,4},{7,3},{8,10},{9,13},{10,... | collective-permute-start | bytes 1572872 | tf_op jit(solution)/shard_map/ppermute | solution.py:225
  44.5 2.5 %collective-permute-start.16 = (f32[256,512]{1,0:T(8,128)S(1)}, f32[256,512]{1,0:T(8,128)S(1)}, u32[]{:S(2)}, u32[]{:S(2)}) collective-permute-start(f32[256,512]{1,0:T(8,128)S(1)} %get-tuple-element.93.block), channel_id=1, source_target_pairs={{0,4},{1,3},{2,6},{3,1},{4,0},{5,7},{6,2},{7,5},{8,12},{9,11},{10,... | collective-permute-start | bytes 1572872 | tf_op jit(solution)/shard_map/ppermute | solution.py:225
  47.2 1.6 %collective-permute-start.11 = (f32[256,256]{1,0:T(8,128)S(1)}, f32[256,256]{1,0:T(8,128)S(1)}, u32[]{:S(2)}, u32[]{:S(2)}) collective-permute-start(f32[256,256]{1,0:T(8,128)S(1)} %get-tuple-element.81), channel_id=1, source_target_pairs={{0,8},{8,0},{16,24},{24,16},{1,9},{9,1},{17,25},{25,17},{2,10},{10... | collective-permute-start | bytes 786440 | tf_op jit(solution)/shard_map/ppermute | solution.py:189
  49.4 2.0 %shard_map.63 = (f32[256,512]{1,0:T(8,128)}, f32[256,512]{1,0:T(8,128)S(1)}, f32[256,512]{1,0:T(8,128)S(1)}) custom-call(s32[1,12]{1,0:T(1,128)S(1)} %copy-done.7, bf16[512,256]{1,0:T(8,128)(2,1)S(1)} %get-tuple-element.67.ah, bf16[512,256]{1,0:T(8,128)(2,1)S(1)} %get-tuple-element.68.al, bf16[512,256]{1,0:T(8,128)(2,1)S(1)} %get-tuple-element.69.bh, ...), custom_call_target="tpu_custom_call" | custom-call | flops 402653184 | bytes 4718592 | tf_op jit(solution)/shard_map/pallas_call | solution.py:50
  51.4 4.7 %collective-permute-start.14 = (f32[256,512]{1,0:T(8,128)}, f32[256,512]{1,0:T(8,128)}, u32[]{:S(2)}, u32[]{:S(2)}) collective-permute-start(f32[256,512]{1,0:T(8,128)} %get-tuple-element.90), channel_id=1, source_target_pairs={{0,2},{1,5},{2,0},{3,7},{4,6},{5,1},{6,4},{7,3},{8,10},{9,13},{10,... | collective-permute-start | bytes 1572872 | tf_op jit(solution)/shard_map/ppermute | solution.py:225
  56.1 2.5 %collective-permute-start.19 = (f32[256,512]{1,0:T(8,128)S(1)}, f32[256,512]{1,0:T(8,128)S(1)}, u32[]{:S(2)}, u32[]{:S(2)}) collective-permute-start(f32[256,512]{1,0:T(8,128)S(1)} %get-tuple-element.100.block), channel_id=1, source_target_pairs={{0,4},{1,3},{2,6},{3,1},{4,0},{5,7},{6,2},{7,5},{8,12},{9,11},{10,... | collective-permute-start | bytes 1572872 | tf_op jit(solution)/shard_map/ppermute | solution.py:225
  58.6 0.9 shard_map.64
  60.2 1.6 %collective-permute-start.15 = (f32[256,256]{1,0:T(8,128)}, f32[256,256]{1,0:T(8,128)}, u32[]{:S(2)}, u32[]{:S(2)}) collective-permute-start(f32[256,256]{1,0:T(8,128)} %get-tuple-element.91), channel_id=1, source_target_pairs={{0,8},{8,0},{16,24},{24,16},{1,9},{9,1},{17,25},{25,17},{2,10},{10... | collective-permute-start | bytes 786440 | tf_op jit(solution)/shard_map/ppermute | solution.py:189
  61.7 2.6 %collective-permute-start.13 = (f32[256,256]{1,0:T(8,128)}, f32[256,256]{1,0:T(8,128)}, u32[]{:S(2)}, u32[]{:S(2)}) collective-permute-start(f32[256,256]{1,0:T(8,128)} %get-tuple-element.86), channel_id=1, source_target_pairs={{0,16},{8,24},{16,0},{24,8},{1,17},{9,25},{17,1},{25,9},{2,18},{10... | collective-permute-start | bytes 786440 | tf_op jit(solution)/shard_map/ppermute | solution.py:189
  64.3 1.9 %shard_map.65 = (f32[256,512]{1,0:T(8,128)}, f32[256,512]{1,0:T(8,128)S(1)}) custom-call(s32[1,12]{1,0:T(1,128)S(1)} %copy-done.7, bf16[512,256]{1,0:T(8,128)(2,1)S(1)} %get-tuple-element.67.ah, bf16[512,256]{1,0:T(8,128)(2,1)S(1)} %get-tuple-element.68.al, bf16[512,256]{1,0:T(8,128)(2,1)S(1)} %get-tuple-element.69.bh, ...), custom_call_target="tpu_custom_call" | custom-call | flops 402653184 | bytes 4194304 | tf_op jit(solution)/shard_map/pallas_call | solution.py:50
  66.3 1.4 %collective-permute-start.17 = (f32[256,512]{1,0:T(8,128)}, f32[256,512]{1,0:T(8,128)}, u32[]{:S(2)}, u32[]{:S(2)}) collective-permute-start(f32[256,512]{1,0:T(8,128)} %get-tuple-element.97), channel_id=1, source_target_pairs={{0,2},{1,5},{2,0},{3,7},{4,6},{5,1},{6,4},{7,3},{8,10},{9,13},{10,... | collective-permute-start | bytes 1572872 | tf_op jit(solution)/shard_map/ppermute | solution.py:225
  67.7 1.1 constant_dynamic-slice_fusion.1
  68.8 4.7 %collective-permute-done.15.refs_2_ = f32[256,256]{1,0:T(8,128)} collective-permute-done((f32[256,256]{1,0:T(8,128)}, f32[256,256]{1,0:T(8,128)}, u32[]{:S(2)}, u32[]{:S(2)}) %collective-permute-start.15) | collective-permute-done | bytes 262176 | tf_op jit(solution)/shard_map/ppermute | solution.py:189
  73.5 1.2 shard_map.66
  74.8 1.2 collective-permute-done.13.refs_0_
  76.0 1.1 shard_map.67
  77.1 1.5 %shard_map.68 = (f32[256,512]{1,0:T(8,128)S(1)}, f32[256,512]{1,0:T(8,128)S(1)}) custom-call(s32[1,12]{1,0:T(1,128)S(1)} %copy-done.7, bf16[512,256]{1,0:T(8,128)(2,1)S(1)} %get-tuple-element.67.ah, bf16[512,256]{1,0:T(8,128)(2,1)S(1)} %get-tuple-element.68.al, bf16[512,256]{1,0:T(8,128)(2,1)S(1)} %get-tuple-element.69.bh, ...), custom_call_target="tpu_custom_call" | custom-call | flops 402653184 | bytes 4194304 | tf_op jit(solution)/shard_map/pallas_call | solution.py:50
  78.7 1.4 %collective-permute-start.21 = (f32[256,512]{1,0:T(8,128)S(1)}, f32[256,512]{1,0:T(8,128)S(1)}, u32[]{:S(2)}, u32[]{:S(2)}) collective-permute-start(f32[256,512]{1,0:T(8,128)S(1)} %get-tuple-element.106), channel_id=1, source_target_pairs={{0,2},{1,5},{2,0},{3,7},{4,6},{5,1},{6,4},{7,3},{8,10},{9,13},{10,... | collective-permute-start | bytes 1572872 | tf_op jit(solution)/shard_map/ppermute | solution.py:225
  80.1 1.3 %collective-permute-done.18.refs_2_ = f32[256,256]{1,0:T(8,128)S(1)} collective-permute-done((f32[256,256]{1,0:T(8,128)S(1)}, f32[256,256]{1,0:T(8,128)S(1)}, u32[]{:S(2)}, u32[]{:S(2)}) %collective-permute-start.18) | collective-permute-done | bytes 262176 | tf_op jit(solution)/shard_map/ppermute | solution.py:189
  81.4 1.1 shard_map.69
  82.8 3.4 %collective-permute-start.20 = (f32[256,256]{1,0:T(8,128)S(1)}, f32[256,256]{1,0:T(8,128)S(1)}, u32[]{:S(2)}, u32[]{:S(2)}) collective-permute-start(f32[256,256]{1,0:T(8,128)S(1)} %get-tuple-element.103), channel_id=1, source_target_pairs={{0,16},{8,24},{16,0},{24,8},{1,17},{9,25},{17,1},{25,9},{2,18},{10... | collective-permute-start | bytes 786440 | tf_op jit(solution)/shard_map/ppermute | solution.py:189
  86.1 8.4 %collective-permute-done.22.refs_2_ = f32[256,256]{1,0:T(8,128)S(1)} collective-permute-done((f32[256,256]{1,0:T(8,128)S(1)}, f32[256,256]{1,0:T(8,128)S(1)}, u32[]{:S(2)}, u32[]{:S(2)}) %collective-permute-start.22) | collective-permute-done | bytes 262176 | tf_op jit(solution)/shard_map/ppermute | solution.py:189
  94.7 1.6 %collective-permute-start.23 = (f32[256,128]{1,0:T(8,128)S(1)}, f32[256,128]{1,0:T(8,128)S(1)}, u32[]{:S(2)}, u32[]{:S(2)}) collective-permute-start(f32[256,128]{1,0:T(8,128)S(1)} %get-tuple-element.111), channel_id=1, source_target_pairs={{0,16},{8,24},{16,0},{24,8},{1,17},{9,25},{17,1},{25,9},{2,18},{10... | collective-permute-start | bytes 393224 | tf_op jit(solution)/shard_map/ppermute | solution.py:189
  96.5 6.0 %collective-permute-done.24.refs_0_ = f32[256,256]{1,0:T(8,128)S(1)} collective-permute-done((f32[256,256]{1,0:T(8,128)S(1)}, f32[256,256]{1,0:T(8,128)S(1)}, u32[]{:S(2)}, u32[]{:S(2)}) %collective-permute-start.24) | collective-permute-done | bytes 262176 | tf_op jit(solution)/shard_map/ppermute | solution.py:189
  102.5 1.9 %collective-permute-start.25 = (f32[256,128]{1,0:T(8,128)S(1)}, f32[256,128]{1,0:T(8,128)S(1)}, u32[]{:S(2)}, u32[]{:S(2)}) collective-permute-start(f32[256,128]{1,0:T(8,128)S(1)} %get-tuple-element.117), channel_id=1, source_target_pairs={{0,16},{8,24},{16,0},{24,8},{1,17},{9,25},{17,1},{25,9},{2,18},{10... | collective-permute-start | bytes 393224 | tf_op jit(solution)/shard_map/ppermute | solution.py:189
  104.4 1.0 constant_dynamic-slice_fusion
  105.6 5.1 %collective-permute-done.25.refs_0_ = f32[256,128]{1,0:T(8,128)S(1)} collective-permute-done((f32[256,128]{1,0:T(8,128)S(1)}, f32[256,128]{1,0:T(8,128)S(1)}, u32[]{:S(2)}, u32[]{:S(2)}) %collective-permute-start.25) | collective-permute-done | bytes 131104 | tf_op jit(solution)/shard_map/ppermute | solution.py:189
  111.0 1.1 collective-permute-done.26
  112.3 3.4 %collective-permute-done.27 = f32[256]{0:T(256)S(1)} collective-permute-done((f32[256]{0:T(256)S(1)}, f32[256]{0:T(256)S(1)}, u32[]{:S(2)}, u32[]{:S(2)}) %collective-permute-start.27) | collective-permute-done | bytes 1056 | tf_op jit(solution)/shard_map/ppermute | solution.py:189
  115.7 1.6 %collective-permute-start.28 = (f32[256]{0:T(256)S(1)}, f32[256]{0:T(256)S(1)}, u32[]{:S(2)}, u32[]{:S(2)}) collective-permute-start(f32[256]{0:T(256)S(1)} %max.10), channel_id=1, source_target_pairs={{0,16},{8,24},{16,0},{24,8},{1,17},{9,25},{17,1},{25,9},{2,18},{10... | collective-permute-start | bytes 3080 | tf_op jit(solution)/shard_map/ppermute | solution.py:189
  117.2 2.9 %collective-permute-done.28 = f32[256]{0:T(256)S(1)} collective-permute-done((f32[256]{0:T(256)S(1)}, f32[256]{0:T(256)S(1)}, u32[]{:S(2)}, u32[]{:S(2)}) %collective-permute-start.28) | collective-permute-done | bytes 1056 | tf_op jit(solution)/shard_map/ppermute | solution.py:189
  120.1 1.0 maximum_divide_fusion
  (54 shorter events, 4.6 us)
Async XLA Ops:
  3.1 15.5 %collective-permute-start.4 = (f32[256,512]{1,0:T(8,128)}, f32[256,512]{1,0:T(8,128)S(1)}, u32[]{:S(2)}, u32[]{:S(2)}) collective-permute-start(f32[256,512]{1,0:T(8,128)} %get-tuple-element.71.block), channel_id=1, source_target_pairs={{0,4},{1,3},{2,6},{3,1},{4,0},{5,7},{6,2},{7,5},{8,12},{9,11},{10,... | collective-permute-start | bytes 1572872 | tf_op jit(solution)/shard_map/ppermute | solution.py:225
  6.1 9.9 %collective-permute-start = (f32[256,256]{1,0:T(8,128)}, f32[256,256]{1,0:T(8,128)S(1)}, u32[]{:S(2)}, u32[]{:S(2)}) collective-permute-start(f32[256,256]{1,0:T(8,128)} %get-tuple-element.63.token), channel_id=1, source_target_pairs={{0,2},{1,5},{2,0},{3,7},{4,1},{5,6},{6,3},{7,4},{8,10},{9,13},{10,... | collective-permute-start | bytes 786440 | tf_op jit(solution)/shard_map/ppermute | solution.py:225
  7.6 10.6 %collective-permute-start.1 = (f32[256,256]{1,0:T(8,128)}, f32[256,256]{1,0:T(8,128)S(1)}, u32[]{:S(2)}, u32[]{:S(2)}) collective-permute-start(f32[256,256]{1,0:T(8,128)} %get-tuple-element.64), channel_id=1, source_target_pairs={{1,5},{3,7},{4,1},{5,4},{6,3},{7,6},{9,13},{11,15},{12,9},{13,12},... | collective-permute-start | bytes 786440 | tf_op jit(solution)/shard_map/ppermute | solution.py:225
  8.2 9.9 %collective-permute-start.2 = (f32[256,256]{1,0:T(8,128)}, f32[256,256]{1,0:T(8,128)S(1)}, u32[]{:S(2)}, u32[]{:S(2)}) collective-permute-start(f32[256,256]{1,0:T(8,128)} %get-tuple-element.65), channel_id=1, source_target_pairs={{0,1},{1,2},{2,3},{3,0},{4,6},{6,4},{8,9},{9,10},{10,11},{11,8},{1... | collective-permute-start | bytes 786440 | tf_op jit(solution)/shard_map/ppermute | solution.py:225
  11.7 6.5 %copy-start.2 = (f32[1,256,512]{2,1,0:T(8,128)S(1)}, f32[1,256,512]{2,1,0:T(8,128)}, u32[]{:S(2)}) copy-start(f32[1,256,512]{2,1,0:T(8,128)} %param.5) | copy-start | bytes 1572868
  11.7 6.9 %copy-start.3 = (f32[256,256]{1,0:T(8,128)S(1)}, f32[256,256]{1,0:T(8,128)}, u32[]{:S(2)}) copy-start(f32[256,256]{1,0:T(8,128)} %get-tuple-element.63.token) | copy-start | bytes 786436
  11.7 6.9 %copy-start.4 = (f32[256,512]{1,0:T(8,128)S(1)}, f32[256,512]{1,0:T(8,128)}, u32[]{:S(2)}) copy-start(f32[256,512]{1,0:T(8,128)} %get-tuple-element.71.block) | copy-start | bytes 1572868
  11.8 6.9 %copy-start.7 = (s32[1,12]{1,0:T(1,128)S(1)}, s32[1,12]{1,0:T(1,128)}, u32[]{:S(2)}) copy-start(s32[1,12]{1,0:T(1,128)} %col_blocks.11) | copy-start | bytes 148
  11.8 6.4 %collective-permute-start.3 = (f32[256,256]{1,0:T(8,128)}, f32[256,256]{1,0:T(8,128)S(1)}, u32[]{:S(2)}, u32[]{:S(2)}) collective-permute-start(f32[256,256]{1,0:T(8,128)} %get-tuple-element.66), channel_id=1, source_target_pairs={{0,1},{1,0},{2,3},{3,2},{8,9},{9,8},{10,11},{11,10},{16,17},{17,16... | collective-permute-start | bytes 786440 | tf_op jit(solution)/shard_map/ppermute | solution.py:225
  13.8 4.8 %copy-start = (f32[1,256,3072]{2,1,0:T(8,128)S(1)}, f32[1,256,3072]{2,1,0:T(8,128)}, u32[]{:S(2)}) copy-start(f32[1,256,3072]{2,1,0:T(8,128)} %param.6) | copy-start | bytes 9437188
  16.0 11.0 %collective-permute-start.7 = (f32[256,512]{1,0:T(8,128)}, f32[256,512]{1,0:T(8,128)S(1)}, u32[]{:S(2)}, u32[]{:S(2)}) collective-permute-start(f32[256,512]{1,0:T(8,128)} %shard_map.58.block), channel_id=1, source_target_pairs={{0,4},{1,3},{2,6},{3,1},{4,0},{5,7},{6,2},{7,5},{8,12},{9,11},{10,... | collective-permute-start | bytes 1572872 | tf_op jit(solution)/shard_map/ppermute | solution.py:225
  18.6 8.3 %copy-start.1 = (f32[256,512]{1,0:T(8,128)S(1)}, f32[256,512]{1,0:T(8,128)}, u32[]{:S(2)}) copy-start(f32[256,512]{1,0:T(8,128)} %shard_map.58.block) | copy-start | bytes 1572868
  20.3 15.5 %collective-permute-start.6 = (f32[256,512]{1,0:T(8,128)S(1)}, f32[256,512]{1,0:T(8,128)S(1)}, u32[]{:S(2)}, u32[]{:S(2)}) collective-permute-start(f32[256,512]{1,0:T(8,128)S(1)} %get-tuple-element.73), channel_id=1, source_target_pairs={{0,2},{1,5},{2,0},{3,7},{4,6},{5,1},{6,4},{7,3},{8,10},{9,13},{10,... | collective-permute-start | bytes 1572872 | tf_op jit(solution)/shard_map/ppermute | solution.py:225
  22.7 15.5 %collective-permute-start.5 = (f32[256,512]{1,0:T(8,128)S(1)}, f32[256,512]{1,0:T(8,128)S(1)}, u32[]{:S(2)}, u32[]{:S(2)}) collective-permute-start(f32[256,512]{1,0:T(8,128)S(1)} %get-tuple-element.72.block), channel_id=1, source_target_pairs={{0,4},{1,3},{2,6},{3,1},{4,0},{5,7},{6,2},{7,5},{8,12},{9,11},{10,... | collective-permute-start | bytes 1572872 | tf_op jit(solution)/shard_map/ppermute | solution.py:225
  28.6 18.5 %collective-permute-start.9 = (f32[256,512]{1,0:T(8,128)S(1)}, f32[256,512]{1,0:T(8,128)S(1)}, u32[]{:S(2)}, u32[]{:S(2)}) collective-permute-start(f32[256,512]{1,0:T(8,128)S(1)} %get-tuple-element.79), channel_id=1, source_target_pairs={{0,2},{1,5},{2,0},{3,7},{4,6},{5,1},{6,4},{7,3},{8,10},{9,13},{10,... | collective-permute-start | bytes 1572872 | tf_op jit(solution)/shard_map/ppermute | solution.py:225
  33.4 16.0 %collective-permute-start.12 = (f32[256,512]{1,0:T(8,128)S(1)}, f32[256,512]{1,0:T(8,128)S(1)}, u32[]{:S(2)}, u32[]{:S(2)}) collective-permute-start(f32[256,512]{1,0:T(8,128)S(1)} %get-tuple-element.84.block), channel_id=1, source_target_pairs={{0,4},{1,3},{2,6},{3,1},{4,0},{5,7},{6,2},{7,5},{8,12},{9,11},{10,... | collective-permute-start | bytes 1572872 | tf_op jit(solution)/shard_map/ppermute | solution.py:225
  35.9 11.2 %collective-permute-start.10 = (f32[256,256]{1,0:T(8,128)S(1)}, f32[256,256]{1,0:T(8,128)S(1)}, u32[]{:S(2)}, u32[]{:S(2)}) collective-permute-start(f32[256,256]{1,0:T(8,128)S(1)} %get-tuple-element.80), channel_id=1, source_target_pairs={{0,8},{8,0},{16,24},{24,16},{1,9},{9,1},{17,25},{25,17},{2,10},{10... | collective-permute-start | bytes 786440 | tf_op jit(solution)/shard_map/ppermute | solution.py:189
  39.8 18.8 %collective-permute-start.8 = (f32[256,512]{1,0:T(8,128)S(1)}, f32[256,512]{1,0:T(8,128)S(1)}, u32[]{:S(2)}, u32[]{:S(2)}) collective-permute-start(f32[256,512]{1,0:T(8,128)S(1)} %get-tuple-element.77), channel_id=1, source_target_pairs={{0,2},{1,5},{2,0},{3,7},{4,6},{5,1},{6,4},{7,3},{8,10},{9,13},{10,... | collective-permute-start | bytes 1572872 | tf_op jit(solution)/shard_map/ppermute | solution.py:225
  44.5 19.8 %collective-permute-start.16 = (f32[256,512]{1,0:T(8,128)S(1)}, f32[256,512]{1,0:T(8,128)S(1)}, u32[]{:S(2)}, u32[]{:S(2)}) collective-permute-start(f32[256,512]{1,0:T(8,128)S(1)} %get-tuple-element.93.block), channel_id=1, source_target_pairs={{0,4},{1,3},{2,6},{3,1},{4,0},{5,7},{6,2},{7,5},{8,12},{9,11},{10,... | collective-permute-start | bytes 1572872 | tf_op jit(solution)/shard_map/ppermute | solution.py:225
  47.2 11.4 %collective-permute-start.11 = (f32[256,256]{1,0:T(8,128)S(1)}, f32[256,256]{1,0:T(8,128)S(1)}, u32[]{:S(2)}, u32[]{:S(2)}) collective-permute-start(f32[256,256]{1,0:T(8,128)S(1)} %get-tuple-element.81), channel_id=1, source_target_pairs={{0,8},{8,0},{16,24},{24,16},{1,9},{9,1},{17,25},{25,17},{2,10},{10... | collective-permute-start | bytes 786440 | tf_op jit(solution)/shard_map/ppermute | solution.py:189
  51.4 22.1 %collective-permute-start.14 = (f32[256,512]{1,0:T(8,128)}, f32[256,512]{1,0:T(8,128)}, u32[]{:S(2)}, u32[]{:S(2)}) collective-permute-start(f32[256,512]{1,0:T(8,128)} %get-tuple-element.90), channel_id=1, source_target_pairs={{0,2},{1,5},{2,0},{3,7},{4,6},{5,1},{6,4},{7,3},{8,10},{9,13},{10,... | collective-permute-start | bytes 1572872 | tf_op jit(solution)/shard_map/ppermute | solution.py:225
  56.1 21.0 %collective-permute-start.19 = (f32[256,512]{1,0:T(8,128)S(1)}, f32[256,512]{1,0:T(8,128)S(1)}, u32[]{:S(2)}, u32[]{:S(2)}) collective-permute-start(f32[256,512]{1,0:T(8,128)S(1)} %get-tuple-element.100.block), channel_id=1, source_target_pairs={{0,4},{1,3},{2,6},{3,1},{4,0},{5,7},{6,2},{7,5},{8,12},{9,11},{10,... | collective-permute-start | bytes 1572872 | tf_op jit(solution)/shard_map/ppermute | solution.py:225
  59.5 0.6 copy-start.5
  60.2 13.4 %collective-permute-start.15 = (f32[256,256]{1,0:T(8,128)}, f32[256,256]{1,0:T(8,128)}, u32[]{:S(2)}, u32[]{:S(2)}) collective-permute-start(f32[256,256]{1,0:T(8,128)} %get-tuple-element.91), channel_id=1, source_target_pairs={{0,8},{8,0},{16,24},{24,16},{1,9},{9,1},{17,25},{25,17},{2,10},{10... | collective-permute-start | bytes 786440 | tf_op jit(solution)/shard_map/ppermute | solution.py:189
  61.7 14.3 %collective-permute-start.13 = (f32[256,256]{1,0:T(8,128)}, f32[256,256]{1,0:T(8,128)}, u32[]{:S(2)}, u32[]{:S(2)}) collective-permute-start(f32[256,256]{1,0:T(8,128)} %get-tuple-element.86), channel_id=1, source_target_pairs={{0,16},{8,24},{16,0},{24,8},{1,17},{9,25},{17,1},{25,9},{2,18},{10... | collective-permute-start | bytes 786440 | tf_op jit(solution)/shard_map/ppermute | solution.py:189
  66.3 15.1 %collective-permute-start.17 = (f32[256,512]{1,0:T(8,128)}, f32[256,512]{1,0:T(8,128)}, u32[]{:S(2)}, u32[]{:S(2)}) collective-permute-start(f32[256,512]{1,0:T(8,128)} %get-tuple-element.97), channel_id=1, source_target_pairs={{0,2},{1,5},{2,0},{3,7},{4,6},{5,1},{6,4},{7,3},{8,10},{9,13},{10,... | collective-permute-start | bytes 1572872 | tf_op jit(solution)/shard_map/ppermute | solution.py:225
  67.7 8.3 %copy-start.6 = (f32[256,128]{1,0:T(8,128)S(1)}, f32[256,128]{1,0:T(8,128)}, u32[]{:S(2)}) copy-start(f32[256,128]{1,0:T(8,128)} %copy-done.5) | copy-start | bytes 393220
  74.7 6.7 %collective-permute-start.18 = (f32[256,256]{1,0:T(8,128)S(1)}, f32[256,256]{1,0:T(8,128)S(1)}, u32[]{:S(2)}, u32[]{:S(2)}) collective-permute-start(f32[256,256]{1,0:T(8,128)S(1)} %get-tuple-element.98), channel_id=1, source_target_pairs={{0,8},{8,0},{16,24},{24,16},{1,9},{9,1},{17,25},{25,17},{2,10},{10... | collective-permute-start | bytes 786440 | tf_op jit(solution)/shard_map/ppermute | solution.py:189
  78.7 15.9 %collective-permute-start.21 = (f32[256,512]{1,0:T(8,128)S(1)}, f32[256,512]{1,0:T(8,128)S(1)}, u32[]{:S(2)}, u32[]{:S(2)}) collective-permute-start(f32[256,512]{1,0:T(8,128)S(1)} %get-tuple-element.106), channel_id=1, source_target_pairs={{0,2},{1,5},{2,0},{3,7},{4,6},{5,1},{6,4},{7,3},{8,10},{9,13},{10,... | collective-permute-start | bytes 1572872 | tf_op jit(solution)/shard_map/ppermute | solution.py:225
  82.5 12.0 %collective-permute-start.22 = (f32[256,256]{1,0:T(8,128)S(1)}, f32[256,256]{1,0:T(8,128)S(1)}, u32[]{:S(2)}, u32[]{:S(2)}) collective-permute-start(f32[256,256]{1,0:T(8,128)S(1)} %get-tuple-element.107), channel_id=1, source_target_pairs={{0,8},{8,0},{16,24},{24,16},{1,9},{9,1},{17,25},{25,17},{2,10},{10... | collective-permute-start | bytes 786440 | tf_op jit(solution)/shard_map/ppermute | solution.py:189
  82.8 13.5 %collective-permute-start.20 = (f32[256,256]{1,0:T(8,128)S(1)}, f32[256,256]{1,0:T(8,128)S(1)}, u32[]{:S(2)}, u32[]{:S(2)}) collective-permute-start(f32[256,256]{1,0:T(8,128)S(1)} %get-tuple-element.103), channel_id=1, source_target_pairs={{0,16},{8,24},{16,0},{24,8},{1,17},{9,25},{17,1},{25,9},{2,18},{10... | collective-permute-start | bytes 786440 | tf_op jit(solution)/shard_map/ppermute | solution.py:189
  94.7 7.8 %collective-permute-start.24 = (f32[256,256]{1,0:T(8,128)S(1)}, f32[256,256]{1,0:T(8,128)S(1)}, u32[]{:S(2)}, u32[]{:S(2)}) collective-permute-start(f32[256,256]{1,0:T(8,128)S(1)} %get-tuple-element.114), channel_id=1, source_target_pairs={{0,8},{8,0},{16,24},{24,16},{1,9},{9,1},{17,25},{25,17},{2,10},{10... | collective-permute-start | bytes 786440 | tf_op jit(solution)/shard_map/ppermute | solution.py:189
  94.7 10.7 %collective-permute-start.23 = (f32[256,128]{1,0:T(8,128)S(1)}, f32[256,128]{1,0:T(8,128)S(1)}, u32[]{:S(2)}, u32[]{:S(2)}) collective-permute-start(f32[256,128]{1,0:T(8,128)S(1)} %get-tuple-element.111), channel_id=1, source_target_pairs={{0,16},{8,24},{16,0},{24,8},{1,17},{9,25},{17,1},{25,9},{2,18},{10... | collective-permute-start | bytes 393224 | tf_op jit(solution)/shard_map/ppermute | solution.py:189
  102.5 8.1 %collective-permute-start.25 = (f32[256,128]{1,0:T(8,128)S(1)}, f32[256,128]{1,0:T(8,128)S(1)}, u32[]{:S(2)}, u32[]{:S(2)}) collective-permute-start(f32[256,128]{1,0:T(8,128)S(1)} %get-tuple-element.117), channel_id=1, source_target_pairs={{0,16},{8,24},{16,0},{24,8},{1,17},{9,25},{17,1},{25,9},{2,18},{10... | collective-permute-start | bytes 393224 | tf_op jit(solution)/shard_map/ppermute | solution.py:189
  110.9 1.2 collective-permute-start.26
  112.1 3.6 %collective-permute-start.27 = (f32[256]{0:T(256)S(1)}, f32[256]{0:T(256)S(1)}, u32[]{:S(2)}, u32[]{:S(2)}) collective-permute-start(f32[256]{0:T(256)S(1)} %max.9), channel_id=1, source_target_pairs={{0,8},{8,0},{16,24},{24,16},{1,9},{9,1},{17,25},{25,17},{2,10},{10... | collective-permute-start | bytes 3080 | tf_op jit(solution)/shard_map/ppermute | solution.py:189
  115.7 4.5 %collective-permute-start.28 = (f32[256]{0:T(256)S(1)}, f32[256]{0:T(256)S(1)}, u32[]{:S(2)}, u32[]{:S(2)}) collective-permute-start(f32[256]{0:T(256)S(1)} %max.10), channel_id=1, source_target_pairs={{0,16},{8,24},{16,0},{24,8},{1,17},{9,25},{17,1},{25,9},{2,18},{10... | collective-permute-start | bytes 3080 | tf_op jit(solution)/shard_map/ppermute | solution.py:189
